TPU v7x, 32 devices: a whole 2x2x4 slice. The times are simulated.
32 devices in a mesh: batch: 8 (over z, core), mem: 4 (over y, x).
Axes of the slice: x: 2, y: 2, z: 4, core: 2. Of those that a mesh axis runs over, the one named last changes fastest.
Arguments:
- queries: bfloat16 [4096, 256], P(('mem', 'batch')), may hold values from -10 to 10
- positives: bfloat16 [4096, 256], P(('mem', 'batch')), may hold values from -0.25 to 0.25, as said below
- pos_ids: int32 [4096], replicated, may hold values from 0 to 31
- pos_logq: int32 [4096], replicated, may hold values from -10240 to -4097
- mem_items: bfloat16 [1024, 256], P(('batch', 'mem')), may hold values from -0.375 to 0.375
- mem_ids: int32 [1024], replicated, may hold values from 0 to 31
- mem_logq: int32 [1024], replicated, may hold values from -12288 to -6145
- mem_age: int32 [1024], replicated, may hold values from 0 to 23
- counts: int32 [512], replicated, may hold values from 1 to 64, 4096 in all
Outputs:
- row_loss: float32 [4096], P(('mem', 'batch'))
- query_grad: float32 [4096, 256], P(('mem', 'batch'))
- positive_grad: float32 [4096, 256], P(('mem', 'batch'))
Inputs may be any that keep to these rules, and one draw needn't show every extreme that they name: `positives`: item embeddings. The counts sum to 4096; the largest is 64.
All inputs are finite; a program needn't handle non-finite values.
Results may differ from a plain program's by a relative error of at most 0.0033.
Values may be sent and summed in bfloat16 or wider, within the bound.
No kernel may reach another device: no remote copies, remote signals or barrier semaphores. Data moves between devices by JAX's collectives and lax.ppermute only.
A program may use at most 64 MiB of HBM per device.

v0:
```python
import jax
import jax.numpy as jnp
from jax import lax
from jax.sharding import PartitionSpec as P

AGE_LIMIT = 16


inv_temp = 8.0
logq_unit = 1.0 / 1024.0
very_low = -1e30


def request_of(counts, positions):
    req_ends = jnp.cumsum(counts)
    return jnp.searchsorted(req_ends, positions, side="right")


def scores(left_mat, right_mat):
    return lax.dot_general(
        left_mat, right_mat, (((1,), (1,)), ((), ())), preferred_element_type=jnp.float32
    )


def transposed(left_mat, right_mat):
    return lax.dot_general(
        left_mat, right_mat, (((0,), (0,)), ((), ())), preferred_element_type=jnp.float32
    )


def masked_exp(tile_logits, level):
    return jnp.where(tile_logits > very_low, jnp.exp(tile_logits - level[:, None]), 0.0)


def body(queries, positives, pos_ids, pos_logq, mem_items, mem_ids, mem_logq, mem_age, counts):
    own_count = queries.shape[0]
    batch_count = lax.axis_size("batch")
    group_rows = own_count * batch_count
    bank_rows = mem_items.shape[0] * lax.axis_size("mem")
    batch_index = lax.axis_index("batch")
    group_first = lax.axis_index("mem") * group_rows
    own_first = group_first + batch_index * own_count
    bank_first = batch_index * bank_rows
    own_rows = own_first + jnp.arange(own_count, dtype=jnp.int32)
    own_req = request_of(counts, own_rows)
    weight = 1.0 / jnp.take(counts, own_req).astype(jnp.float32)
    own_ids = lax.dynamic_slice_in_dim(pos_ids, own_first, own_count, 0)
    own_shift = (
        -lax.dynamic_slice_in_dim(pos_logq, own_first, own_count, 0).astype(jnp.float32) * logq_unit
    )
    cand_rows = group_first + jnp.arange(group_rows, dtype=jnp.int32)
    cand_req = request_of(counts, cand_rows)
    cand_ids = lax.dynamic_slice_in_dim(pos_ids, group_first, group_rows, 0)
    cand_shift = (
        -lax.dynamic_slice_in_dim(pos_logq, group_first, group_rows, 0).astype(jnp.float32)
        * logq_unit
    )
    bank_ids = lax.dynamic_slice_in_dim(mem_ids, bank_first, bank_rows, 0)
    bank_shift = (
        -lax.dynamic_slice_in_dim(mem_logq, bank_first, bank_rows, 0).astype(jnp.float32)
        * logq_unit
    )
    bank_live = lax.dynamic_slice_in_dim(mem_age, bank_first, bank_rows, 0) < AGE_LIMIT
    bank_items = lax.all_gather(mem_items, "mem", axis=0, tiled=True)
    mem_mask = bank_live[None, :] & (bank_ids[None, :] != own_ids[:, None])
    mem_logits = jnp.where(
        mem_mask, inv_temp * scores(queries, bank_items) + bank_shift[None, :], very_low
    )
    mem_max = jnp.max(mem_logits, axis=1)
    group_items = lax.all_gather(positives, "batch", axis=0, tiled=True)
    piece_rows = group_items.shape[0]
    col_rows = group_first + jnp.arange(piece_rows, dtype=jnp.int32)
    kept_mask = (col_rows[None, :] == own_rows[:, None]) | (
        cand_ids[None, :] != own_ids[:, None]
    ) & (cand_req[None, :] != own_req[:, None])
    group_logits = jnp.where(
        kept_mask, inv_temp * scores(queries, group_items) + cand_shift[None, :], very_low
    )
    row_max = jnp.maximum(jnp.max(group_logits, axis=1), mem_max)
    pos_total = jnp.sum(masked_exp(group_logits, row_max), axis=1)
    mem_total = jnp.sum(masked_exp(mem_logits, row_max), axis=1)
    row_lse = row_max + jnp.log(pos_total + mem_total)
    pos_coef = (weight[:, None] * masked_exp(group_logits, row_lse)).astype(jnp.bfloat16)
    mem_coef = (weight[:, None] * masked_exp(mem_logits, row_lse)).astype(jnp.bfloat16)
    own_term = inv_temp * weight[:, None]
    query_grad = inv_temp * (
        jnp.dot(pos_coef, group_items, preferred_element_type=jnp.float32)
        + jnp.dot(mem_coef, bank_items, preferred_element_type=jnp.float32)
    ) - own_term * positives.astype(jnp.float32)
    column_share = lax.psum_scatter(
        inv_temp * transposed(pos_coef, queries), "batch", scatter_dimension=0, tiled=True
    )
    positive_grad = column_share - own_term * queries.astype(jnp.float32)
    own_logit = (
        inv_temp * jnp.sum(queries.astype(jnp.float32) * positives.astype(jnp.float32), axis=1)
        + own_shift
    )
    return (row_lse - own_logit, query_grad, positive_grad)


def solution(mesh):
    in_specs = (
        P(("mem", "batch"), None),
        P(("mem", "batch"), None),
        P(),
        P(),
        P(("batch", "mem"), None),
        P(),
        P(),
        P(),
        P(),
    )
    out_specs = (P(("mem", "batch")), P(("mem", "batch"), None), P(("mem", "batch"), None))
    return jax.shard_map(body, mesh=mesh, in_specs=in_specs, out_specs=out_specs, check_vma=False)
```

profile of v0, /device:TPU:0, one launch (start us, length us, event | category | flops | bytes accessed | tf_op | source)
XLA Modules:
  0.0 165.9 jit_solution(11975383600506005967)
XLA Ops:
  8.5 13.4 %while.49 = (s32[]{:T(128)}, u32[128]{0:T(128)S(1)}, u32[128]{0:T(128)S(1)}, s32[512]{0:T(512)S(1)}, s32[]{:T(128)}, /*index=5*/s32[]{:T(128)}, s32[]{:T(128)}, s32[]{}) while((s32[]{:T(128)}, u32[128]{0:T(128)S(1)}, u32[128]{0:T(128)S(1)}, s32[512]{0:T(512)S(1)}, s32[]{:T(128)}, /*index=5*/s32[]{:T(128)}, s32[]{:T(128)}, s32[]{}) %tuple.69), condition=%wide.region_5.6_spmd.clone, body=%wide.region_4.5_spmd.clone.sunk | while | flops 2820 | bytes 10352 | solution.py:16
  8.5 1.3 gather_fusion.1
  9.9 1.3 gather_fusion.1
  11.2 1.3 gather_fusion.1
  12.6 1.3 gather_fusion.1
  13.9 1.3 gather_fusion.1
  15.2 1.3 gather_fusion.1
  16.6 1.3 gather_fusion.1
  17.9 1.3 gather_fusion.1
  19.3 1.3 gather_fusion.1
  20.6 1.3 gather_fusion.1
  21.9 0.8 dynamic_slice.25
  23.5 0.8 dynamic-slice_compare_fusion
  24.2 16.7 %all_gather.6 = bf16[1024,256]{1,0:T(8,128)(2,1)S(1)} all-gather(bf16[128,256]{1,0:T(8,128)(2,1)S(1)} %copy-done.2), channel_id=1, replica_groups=mesh['batch'=8,'mem'=4] {'batch'}, dimensions={0}, use_global_device_ids=true | all-gather | bytes 589824 | tf_op jit(solution)/shard_map/all_gather | solution.py:70
  41.1 1.3 gather_fusion.2
  43.1 69.4 %while.48 = (s32[]{:T(128)}, u32[1024]{0:T(1024)S(1)}, u32[1024]{0:T(1024)S(1)}, s32[512]{0:T(512)S(1)}, s32[]{:T(128)}, /*index=5*/s32[]{:T(128)}, s32[]{:T(128)}, s32[]{}) while((s32[]{:T(128)}, u32[1024]{0:T(1024)S(1)}, u32[1024]{0:T(1024)S(1)}, s32[512]{0:T(512)S(1)}, s32[]{:T(128)}, /*index=5*/s32[]{:T(128)}, s32[]{:T(128)}, ...), condition=%wide.region_3.4_spmd.clone, body=%wide.region_2.3_spmd.clone.sunk | while | flops 20484 | bytes 63601 | solution.py:16
  43.2 6.9 %gather_fusion = s32[1024]{0:T(1024)S(1)} fusion(s32[512]{0:T(512)S(1)} %get-tuple-element.322, u32[1024]{0:T(1024)S(1)} %broadcast_clamp_fusion.2), kind=kCustom, calls=%fused_computation.clone.clone.1 | custom fusion | bytes 12288 | tf_op jit(solution)/shard_map/jit(searchsorted)/jit(_searchsorted_scan_impl)/vmap(jit(_searchsorted_scan_impl))/while/body/eval_jaxpr/gather | solution.py:16
  50.1 6.9 %gather_fusion = s32[1024]{0:T(1024)S(1)} fusion(s32[512]{0:T(512)S(1)} %get-tuple-element.322, u32[1024]{0:T(1024)S(1)} %broadcast_clamp_fusion.2), kind=kCustom, calls=%fused_computation.clone.clone.1 | custom fusion | bytes 12288 | tf_op jit(solution)/shard_map/jit(searchsorted)/jit(_searchsorted_scan_impl)/vmap(jit(_searchsorted_scan_impl))/while/body/eval_jaxpr/gather | solution.py:16
  57.0 6.9 %gather_fusion = s32[1024]{0:T(1024)S(1)} fusion(s32[512]{0:T(512)S(1)} %get-tuple-element.322, u32[1024]{0:T(1024)S(1)} %broadcast_clamp_fusion.2), kind=kCustom, calls=%fused_computation.clone.clone.1 | custom fusion | bytes 12288 | tf_op jit(solution)/shard_map/jit(searchsorted)/jit(_searchsorted_scan_impl)/vmap(jit(_searchsorted_scan_impl))/while/body/eval_jaxpr/gather | solution.py:16
  64.0 6.9 %gather_fusion = s32[1024]{0:T(1024)S(1)} fusion(s32[512]{0:T(512)S(1)} %get-tuple-element.322, u32[1024]{0:T(1024)S(1)} %broadcast_clamp_fusion.2), kind=kCustom, calls=%fused_computation.clone.clone.1 | custom fusion | bytes 12288 | tf_op jit(solution)/shard_map/jit(searchsorted)/jit(_searchsorted_scan_impl)/vmap(jit(_searchsorted_scan_impl))/while/body/eval_jaxpr/gather | solution.py:16
  70.9 6.9 %gather_fusion = s32[1024]{0:T(1024)S(1)} fusion(s32[512]{0:T(512)S(1)} %get-tuple-element.322, u32[1024]{0:T(1024)S(1)} %broadcast_clamp_fusion.2), kind=kCustom, calls=%fused_computation.clone.clone.1 | custom fusion | bytes 12288 | tf_op jit(solution)/shard_map/jit(searchsorted)/jit(_searchsorted_scan_impl)/vmap(jit(_searchsorted_scan_impl))/while/body/eval_jaxpr/gather | solution.py:16
  77.9 6.9 %gather_fusion = s32[1024]{0:T(1024)S(1)} fusion(s32[512]{0:T(512)S(1)} %get-tuple-element.322, u32[1024]{0:T(1024)S(1)} %broadcast_clamp_fusion.2), kind=kCustom, calls=%fused_computation.clone.clone.1 | custom fusion | bytes 12288 | tf_op jit(solution)/shard_map/jit(searchsorted)/jit(_searchsorted_scan_impl)/vmap(jit(_searchsorted_scan_impl))/while/body/eval_jaxpr/gather | solution.py:16
  84.8 6.9 %gather_fusion = s32[1024]{0:T(1024)S(1)} fusion(s32[512]{0:T(512)S(1)} %get-tuple-element.322, u32[1024]{0:T(1024)S(1)} %broadcast_clamp_fusion.2), kind=kCustom, calls=%fused_computation.clone.clone.1 | custom fusion | bytes 12288 | tf_op jit(solution)/shard_map/jit(searchsorted)/jit(_searchsorted_scan_impl)/vmap(jit(_searchsorted_scan_impl))/while/body/eval_jaxpr/gather | solution.py:16
  91.7 6.9 %gather_fusion = s32[1024]{0:T(1024)S(1)} fusion(s32[512]{0:T(512)S(1)} %get-tuple-element.322, u32[1024]{0:T(1024)S(1)} %broadcast_clamp_fusion.2), kind=kCustom, calls=%fused_computation.clone.clone.1 | custom fusion | bytes 12288 | tf_op jit(solution)/shard_map/jit(searchsorted)/jit(_searchsorted_scan_impl)/vmap(jit(_searchsorted_scan_impl))/while/body/eval_jaxpr/gather | solution.py:16
  98.7 6.9 %gather_fusion = s32[1024]{0:T(1024)S(1)} fusion(s32[512]{0:T(512)S(1)} %get-tuple-element.322, u32[1024]{0:T(1024)S(1)} %broadcast_clamp_fusion.2), kind=kCustom, calls=%fused_computation.clone.clone.1 | custom fusion | bytes 12288 | tf_op jit(solution)/shard_map/jit(searchsorted)/jit(_searchsorted_scan_impl)/vmap(jit(_searchsorted_scan_impl))/while/body/eval_jaxpr/gather | solution.py:16
  105.6 6.9 %gather_fusion = s32[1024]{0:T(1024)S(1)} fusion(s32[512]{0:T(512)S(1)} %get-tuple-element.322, u32[1024]{0:T(1024)S(1)} %broadcast_clamp_fusion.2), kind=kCustom, calls=%fused_computation.clone.clone.1 | custom fusion | bytes 12288 | tf_op jit(solution)/shard_map/jit(searchsorted)/jit(_searchsorted_scan_impl)/vmap(jit(_searchsorted_scan_impl))/while/body/eval_jaxpr/gather | solution.py:16
  112.6 8.2 %all_gather.7 = bf16[128,256]{1,0:T(8,128)(2,1)S(1)} all-gather(bf16[32,256]{1,0:T(8,128)(2,1)S(1)} %copy-done.3), channel_id=1, replica_groups=mesh['batch'=8,'mem'=4] {'mem'}, dimensions={0}, use_global_device_ids=true | all-gather | bytes 81920 | tf_op jit(solution)/shard_map/all_gather | solution.py:64
  122.2 1.3 add_subtract_fusion
  123.5 1.4 convolution_multiply_fusion
  125.2 1.0 fusion.9
  126.2 31.2 %reduce-scatter.2.cloned.1.call-done = f32[128,256]{1,0:T(8,128)} async-done(((f32[1024,256]{1,0:T(8,128)}), f32[128,256]{1,0:T(8,128)}) %reduce-scatter.2.cloned.1.call-update) | async-done | bytes 131088 | tf_op jit(solution)/shard_map/reduce_scatter | solution.py:90
  157.4 1.6 fusion.12
  (110 shorter events, 5.3 us)
Async XLA Ops:
  7.2 150.2 %reduce-scatter.2.cloned.1.call-start = ((), (), s32[]{:S(2)}) async-start(), calls=%async_computation.1 | async-start | bytes 1179648 | tf_op jit(solution)/shard_map/reduce_scatter | solution.py:90
  7.2 0.7 copy-start
  8.5 15.7 %copy-start.2 = (bf16[128,256]{1,0:T(8,128)(2,1)S(1)}, bf16[128,256]{1,0:T(8,128)(2,1)}, u32[]{:S(2)}) copy-start(bf16[128,256]{1,0:T(8,128)(2,1)} %param.14) | copy-start | bytes 196612
  24.2 16.7 %copy-start.1 = (bf16[128,256]{1,0:T(8,128)(2,1)S(1)}, bf16[128,256]{1,0:T(8,128)(2,1)}, u32[]{:S(2)}) copy-start(bf16[128,256]{1,0:T(8,128)(2,1)} %param.13) | copy-start | bytes 196612
  41.1 1.3 copy-start.4
  43.1 69.4 %copy-start.3 = (bf16[32,256]{1,0:T(8,128)(2,1)S(1)}, bf16[32,256]{1,0:T(8,128)(2,1)}, u32[]{:S(2)}) copy-start(bf16[32,256]{1,0:T(8,128)(2,1)} %param.17) | copy-start | bytes 49156
  120.8 0.7 dynamic-slice-start
Sparse Core Ops, SparseCore 0:
  125.1 32.2 reduce-scatter.1
where the time goes:
time: 166 us
  local copies, waits for them, and re-layouts  84.8 us (51%)
  waiting for transfers between devices  31.3 us (19%)
  blocking collectives  24.9 us (15%)
  between operations  14.2 us (9%)
  other arithmetic  6.58 us (4%)
  matrix products  3.24 us (2%)
    gather x20, local copies, waits for them, and re-layouts, request_of(): return jnp.searchsorted(req_ends, positions, side='right')  81.3 us
    reduce_scatter x1, waiting for transfers between devices, body(): lax.psum_scatter(inv_temp * transposed(pos_coef, queries), 'batch', scatt...  31.2 us
    all_gather x1, blocking collectives, body(): group_items = lax.all_gather(positives, 'batch', axis=0, tiled=True)  16.7 us
    all_gather x1, blocking collectives, body(): bank_items = lax.all_gather(mem_items, 'mem', axis=0, tiled=True)  8.25 us
  transfers between devices with their start and end apart: 1, of which 1 were waited for; matrix products, arithmetic and copies ran while one was open for 1% of the time, Pallas kernels for 0%

commit v1 on v0

v1 whole, which is shorter than its diff:
```python
import jax
import jax.numpy as jnp
from jax import lax
from jax.experimental import pallas as pl
from jax.experimental.pallas import tpu as pltpu
from jax.sharding import PartitionSpec as P

AGE_LIMIT = 16
inv_temp = 8.0
logq_unit = 1.0 / 1024.0
very_low = -1e30
LANES = 128
VMEM_LIMIT = 32 * 1024 * 1024


def nt_dot(left_mat, right_mat):
    return lax.dot_general(
        left_mat, right_mat, (((1,), (1,)), ((), ())), preferred_element_type=jnp.float32
    )


def tn_dot(left_mat, right_mat):
    return lax.dot_general(
        left_mat, right_mat, (((0,), (0,)), ((), ())), preferred_element_type=jnp.float32
    )


def as_column(row):
    return jnp.broadcast_to(row, (LANES, LANES)).T


def prep_kernel(n_batch, ids_ref, logq_ref, counts_ref, bias_ref, weight_ref, wcol_ref):
    own = lax.axis_index("batch")
    first_block = lax.axis_index("mem") * n_batch
    reqs = counts_ref.shape[0] * LANES
    sub = lax.broadcasted_iota(jnp.int32, (reqs, LANES), 0)
    lane = lax.broadcasted_iota(jnp.int32, (reqs, LANES), 1)
    ones = jnp.ones((LANES, LANES), jnp.bfloat16)
    ends = jnp.zeros((reqs, LANES), jnp.float32)
    for c in range(counts_ref.shape[0]):
        part = counts_ref[c : c + 1, :].astype(jnp.float32)
        tri = jnp.where(lane + c * LANES <= sub, part, 0.0).astype(jnp.bfloat16)
        ends = ends + jnp.dot(tri, ones, preferred_element_type=jnp.float32)
    ends = ends.astype(jnp.int32)
    sub = sub[:LANES]
    lane = lane[:LANES]
    rows = []
    for k in range(n_batch):
        block = first_block + jnp.bitwise_xor(own, k)
        pos = block * LANES + lane[:1]
        done = ends <= pos
        start = jnp.max(jnp.where(done, ends, 0), axis=0, keepdims=True)
        end = jnp.min(jnp.where(done, jnp.int32(2**30), ends), axis=0, keepdims=True)
        weight = 1.0 / (end - start).astype(jnp.float32)
        weight_ref[k : k + 1, :] = weight
        if k == 0:
            wcol_ref[...] = as_column(weight)
        rows.append((ids_ref[pl.ds(block, 1), :], start, end))
    for n in range(n_batch):
        block = first_block + jnp.bitwise_xor(own, n)
        id_col = as_column(ids_ref[pl.ds(block, 1), :])
        shift_col = as_column(-logq_ref[pl.ds(block, 1), :].astype(jnp.float32) * logq_unit)
        pos_col = block * LANES + sub
        for k in range(n_batch):
            id_row, start, end = rows[k]
            keep = (id_col != id_row) & ((pos_col < start) | (pos_col >= end))
            if n == k:
                keep = keep | (sub == lane)
            bias_ref[n * LANES : (n + 1) * LANES, k * LANES : (k + 1) * LANES] = jnp.where(
                keep, shift_col, very_low
            )


def bank_kernel(
    n_batch, pack_ref, s0, s1, s2, s3, ids_ref, mem_ids_ref, mem_logq_ref, mem_age_ref,
    bank_ref, logit_ref, lse_ref,
):
    own = lax.axis_index("batch")
    group = lax.axis_index("mem")
    slots = s0.shape[0]
    for k, shard in enumerate((s0, s1, s2, s3)):
        at = pl.multiple_of(jnp.bitwise_xor(group, k) * slots, slots)
        bank_ref[pl.ds(at, slots), :] = shard[...]
    id_row = ids_ref[pl.ds(group * n_batch + own, 1), :]
    id_col = as_column(mem_ids_ref[pl.ds(own, 1), :])
    shift_col = as_column(-mem_logq_ref[pl.ds(own, 1), :].astype(jnp.float32) * logq_unit)
    age_col = as_column(mem_age_ref[pl.ds(own, 1), :])
    keep = (age_col < AGE_LIMIT) & (id_col != id_row)
    logit = nt_dot(bank_ref[...], pack_ref[:LANES, :])
    logit = jnp.where(keep, logit + shift_col, very_low)
    top = jnp.max(logit, axis=0, keepdims=True)
    total = jnp.sum(jnp.exp(logit - top), axis=0, keepdims=True)
    logit_ref[...] = logit
    lse_ref[...] = top + jnp.log(total)


def main_kernel(n_batch, *refs):
    packs = refs[:n_batch]
    lses = refs[n_batch : 2 * n_batch]
    bias_ref, weight_ref, wcol_ref, bank_ref, mem_logit_ref = refs[2 * n_batch : 2 * n_batch + 5]
    loss_ref, qgrad_ref, pgrad_ref = refs[2 * n_batch + 5 : 2 * n_batch + 8]
    items, queries = refs[2 * n_batch + 8 :]
    for k in range(n_batch):
        queries[k * LANES : (k + 1) * LANES, :] = packs[k][:LANES, :]
        items[k * LANES : (k + 1) * LANES, :] = packs[k][LANES:, :]
    width = 2 * LANES
    pgrad = -wcol_ref[:, :1] * queries[:LANES, :].astype(jnp.float32)
    for c in range(n_batch // 2):
        at = slice(c * width, (c + 1) * width)
        q_part = queries[at, :]
        logit = nt_dot(items[...], q_part) + bias_ref[:, at]
        top = jnp.max(logit, axis=0, keepdims=True)
        total = jnp.sum(jnp.exp(logit - top), axis=0, keepdims=True)
        mem_lse = jnp.concatenate([lses[2 * c][...], lses[2 * c + 1][...]], axis=1)
        weight = jnp.concatenate(
            [weight_ref[2 * c : 2 * c + 1, :], weight_ref[2 * c + 1 : 2 * c + 2, :]], axis=1
        )
        high = jnp.maximum(top, mem_lse)
        lse = high + jnp.log(total * jnp.exp(top - high) + jnp.exp(mem_lse - high))
        coef = (weight * jnp.exp(logit[:LANES] - lse)).astype(jnp.bfloat16)
        pgrad = pgrad + jnp.dot(coef, q_part, preferred_element_type=jnp.float32)
        if c == 0:
            own_lse = lse[:, :LANES]
            own_weight = weight[:, :LANES]
            own = logit[:, :LANES]
            diag = lax.broadcasted_iota(jnp.int32, (LANES, LANES), 0) == (
                lax.broadcasted_iota(jnp.int32, (LANES, LANES), 1)
            )
            own_logit = jnp.sum(jnp.where(diag, own[:LANES], 0.0), axis=0, keepdims=True)
            loss_ref[...] = own_lse - own_logit
            row_coef = (own_weight * jnp.exp(own - own_lse)).astype(jnp.bfloat16)
            mem_coef = (own_weight * jnp.exp(mem_logit_ref[...] - own_lse)).astype(jnp.bfloat16)
            qgrad = tn_dot(row_coef, items[...]) + tn_dot(mem_coef, bank_ref[...])
            qgrad_ref[...] = inv_temp * (
                qgrad - wcol_ref[:, :1] * items[:LANES, :].astype(jnp.float32)
            )
    pgrad_ref[...] = pgrad


def in_vmem(count):
    return [pl.BlockSpec(memory_space=pltpu.VMEM)] * count


def call(kernel, outs, args, scratch=()):
    return pl.pallas_call(
        kernel,
        out_shape=outs,
        in_specs=in_vmem(len(args)),
        out_specs=in_vmem(len(outs)),
        scratch_shapes=list(scratch),
        compiler_params=pltpu.CompilerParams(vmem_limit_bytes=VMEM_LIMIT),
    )(*args)


def f32(*shape):
    return jax.ShapeDtypeStruct(shape, jnp.float32)


def swap(array, axis, mask):
    size = lax.axis_size(axis)
    return lax.ppermute(array, axis, [(s, s ^ mask) for s in range(size)])


def small_body(
    queries, positives, pos_ids, pos_logq, mem_items, mem_ids, mem_logq, mem_age, counts
):
    own_count, depth = queries.shape
    n_batch = lax.axis_size("batch")
    group_rows = own_count * n_batch
    ids = pos_ids.reshape(-1, LANES)
    logq = pos_logq.reshape(-1, LANES)
    banks = [a.reshape(-1, LANES) for a in (mem_ids, mem_logq, mem_age)]

    pack = jnp.concatenate([queries * jnp.bfloat16(inv_temp), positives], 0)
    far = swap(pack, "batch", 4)
    near = swap(pack, "batch", 2)
    shards = [mem_items] + [swap(mem_items, "mem", k) for k in (1, 2, 3)]
    bias, weight, wcol = call(
        lambda *r: prep_kernel(n_batch, *r),
        [f32(group_rows, group_rows), f32(n_batch, LANES), f32(LANES, LANES)],
        (ids, logq, counts.reshape(-1, LANES)),
    )
    bank, mem_logit, mem_lse = call(
        lambda *r: bank_kernel(n_batch, *r),
        [jax.ShapeDtypeStruct((LANES, depth), jnp.bfloat16), f32(LANES, LANES), f32(1, LANES)],
        (pack, *shards, ids, *banks),
    )
    packs = {0: pack, 4: far, 2: near, 6: swap(far, "batch", 2)}
    lses = {0: mem_lse}
    for k in (4, 6, 2):
        lses[k] = swap(mem_lse, "batch", k)
    for k in (0, 2, 4, 6):
        packs[k + 1] = swap(packs[k], "batch", 1)
        lses[k + 1] = swap(lses[k], "batch", 1)
    order = range(n_batch)
    loss, query_grad, positive_grad = call(
        lambda *r: main_kernel(n_batch, *r),
        [f32(1, LANES), f32(own_count, depth), f32(own_count, depth)],
        (
            *[packs[k] for k in order],
            *[lses[k] for k in order],
            bias,
            weight,
            wcol,
            bank,
            mem_logit,
        ),
        [pltpu.VMEM((group_rows, depth), jnp.bfloat16)] * 2,
    )
    return loss.reshape(own_count), query_grad, positive_grad


def request_span(counts, positions):
    ends = jnp.cumsum(counts)
    which = jnp.searchsorted(ends, positions, side="right")
    return which, jnp.take(counts, which)


def masked_exp(tile_logits, level):
    return jnp.where(tile_logits > very_low, jnp.exp(tile_logits - level[:, None]), 0.0)


def large_body(
    queries, positives, pos_ids, pos_logq, mem_items, mem_ids, mem_logq, mem_age, counts
):
    own_count = queries.shape[0]
    group_rows = own_count * lax.axis_size("batch")
    bank_rows = mem_items.shape[0] * lax.axis_size("mem")
    batch_index = lax.axis_index("batch")
    group_first = lax.axis_index("mem") * group_rows
    own_first = group_first + batch_index * own_count
    bank_first = batch_index * bank_rows

    def part(array, first, size):
        return lax.dynamic_slice_in_dim(array, first, size, 0)

    def shift_of(array, first, size):
        return -part(array, first, size).astype(jnp.float32) * logq_unit

    own_rows = own_first + jnp.arange(own_count, dtype=jnp.int32)
    col_rows = group_first + jnp.arange(group_rows, dtype=jnp.int32)
    own_req, own_size = request_span(counts, own_rows)
    weight = 1.0 / own_size.astype(jnp.float32)
    cand_req, _ = request_span(counts, col_rows)
    own_ids = part(pos_ids, own_first, own_count)
    cand_ids = part(pos_ids, group_first, group_rows)
    bank_ids = part(mem_ids, bank_first, bank_rows)
    bank_live = part(mem_age, bank_first, bank_rows) < AGE_LIMIT
    bank_items = lax.all_gather(mem_items, "mem", axis=0, tiled=True)
    mem_mask = bank_live[None, :] & (bank_ids[None, :] != own_ids[:, None])
    mem_logits = jnp.where(
        mem_mask,
        inv_temp * nt_dot(queries, bank_items) + shift_of(mem_logq, bank_first, bank_rows)[None, :],
        very_low,
    )
    group_items = lax.all_gather(positives, "batch", axis=0, tiled=True)
    kept = (col_rows[None, :] == own_rows[:, None]) | (
        cand_ids[None, :] != own_ids[:, None]
    ) & (cand_req[None, :] != own_req[:, None])
    logits = jnp.where(
        kept,
        inv_temp * nt_dot(queries, group_items)
        + shift_of(pos_logq, group_first, group_rows)[None, :],
        very_low,
    )
    row_max = jnp.maximum(jnp.max(logits, axis=1), jnp.max(mem_logits, axis=1))
    row_lse = row_max + jnp.log(
        jnp.sum(masked_exp(logits, row_max), axis=1)
        + jnp.sum(masked_exp(mem_logits, row_max), axis=1)
    )
    pos_coef = (weight[:, None] * masked_exp(logits, row_lse)).astype(jnp.bfloat16)
    mem_coef = (weight[:, None] * masked_exp(mem_logits, row_lse)).astype(jnp.bfloat16)
    own_term = inv_temp * weight[:, None]
    query_grad = inv_temp * (
        jnp.dot(pos_coef, group_items, preferred_element_type=jnp.float32)
        + jnp.dot(mem_coef, bank_items, preferred_element_type=jnp.float32)
    ) - own_term * positives.astype(jnp.float32)
    column_share = lax.psum_scatter(
        inv_temp * tn_dot(pos_coef, queries), "batch", scatter_dimension=0, tiled=True
    )
    wide_q = queries.astype(jnp.float32)
    own_logit = inv_temp * jnp.sum(wide_q * positives.astype(jnp.float32), axis=1) + shift_of(
        pos_logq, own_first, own_count
    )
    return row_lse - own_logit, query_grad, column_share - own_term * wide_q


def solution(mesh):
    small = mesh.shape["batch"] == 8 and mesh.shape["mem"] == 4
    own = P(("mem", "batch"), None)
    in_specs = (own, own, P(), P(), P(("batch", "mem"), None), P(), P(), P(), P())
    out_specs = (P(("mem", "batch")), own, own)
    return jax.shard_map(
        small_body if small else large_body,
        mesh=mesh,
        in_specs=in_specs,
        out_specs=out_specs,
        check_vma=False,
    )
```

time: 166 us -> 57.7 us (0.35)
  local copies, waits for them, and re-layouts: 84.8 us -> 4.89 us
  blocking collectives: 24.9 us -> 0 us
  starting transfers between devices: 0.04 us -> 19.3 us
  between operations: 14.2 us -> 0.7 us
  waiting for transfers between devices: 31.3 us -> 26 us
  other arithmetic: 6.58 us -> 1.7 us
  Pallas kernels: 0 us -> 4.59 us
  matrix products: 3.24 us -> 0 us
    gather x21 -> x0, local copies, waits for them, and re-layouts: 82.5 us -> none  [the longest x20 81.3 us: request_of(): return jnp.searchsorted(req_ends, positions, side='right')]
    reduce_scatter x1 -> x0, waiting for transfers between devices: 31.2 us -> none  [body(): lax.psum_scatter(inv_temp * transposed(pos_coef, queries), 'batch', scatt...]
    ppermute x0 -> x17, waiting for transfers between devices: none -> 26 us  [swap(): return lax.ppermute(array, axis, [(s, s ^ mask) for s in range(size)])]
    all_gather x2 -> x0, blocking collectives: 24.9 us -> none  [the longest x1 16.7 us: body(): group_items = lax.all_gather(positives, 'batch', axis=0, tiled=True)]
    ppermute x0 -> x17, starting transfers between devices: none -> 19.3 us  [swap(): return lax.ppermute(array, axis, [(s, s ^ mask) for s in range(size)])]
    pallas_call x0 -> x3, Pallas kernels: none -> 4.59 us  [call(): pl.pallas_call(kernel, out_shape=outs, in_specs=in_vmem(len(args)), out_s...]
    unnamed x10 -> x14, local copies, waits for them, and re-layouts: 0.68 us -> 4.89 us
    dot_general x5 -> x0, matrix products: 3.24 us -> none  [the longest x1 1.41 us: transposed(): lax.dot_general(left_mat, right_mat, (((0,), (0,)), ((), ())), preferred_...]
  transfers between devices with their start and end apart: 1 -> 17, of which waited for: 1 -> 11; matrix products, arithmetic and copies ran while one was open for 1% -> 0% of each run, Pallas kernels for 0% -> 3%
where the time goes in v1:
time: 57.7 us; the launch traced here: 57.1 us
  waiting for transfers between devices  26 us (45%)
  starting transfers between devices  19.3 us (33%)
  local copies, waits for them, and re-layouts  4.89 us (8%)
  Pallas kernels  4.59 us (8%)
  other arithmetic  1.7 us (3%)
  between operations  0.7 us (1%)
    ppermute x17, waiting for transfers between devices, swap(): return lax.ppermute(array, axis, [(s, s ^ mask) for s in range(size)])  26 us
    ppermute x17, starting transfers between devices, swap(): return lax.ppermute(array, axis, [(s, s ^ mask) for s in range(size)])  19.3 us
    unnamed x14, local copies, waits for them, and re-layouts  4.89 us
    pallas_call x3, Pallas kernels, call(): pl.pallas_call(kernel, out_shape=outs, in_specs=in_vmem(len(args)), out_s...  4.59 us
  transfers between devices with their start and end apart: 17, of which 11 were waited for; matrix products, arithmetic and copies ran while one was open for 0% of the time, Pallas kernels for 3%

profile of v1, /device:TPU:0, one launch (start us, length us, event | category | flops | bytes accessed | tf_op | source)
XLA Modules:
  0.0 57.1 jit_solution(2494801861927446430)
XLA Ops:
  0.6 0.8 %broadcast_multiply_fusion = bf16[128,256]{1,0:T(8,128)(2,1)S(1)} fusion(bf16[128,256]{1,0:T(8,128)(2,1)} %param.9), kind=kLoop, calls=%fused_computation.1 | loop fusion | flops 32768 | bytes 131072 | tf_op jit(solution)/shard_map/mul | solution.py:174
  1.5 0.8 %pad_maximum_fusion.r_0_ = bf16[256,256]{1,0:T(8,128)(2,1)S(1)} fusion(bf16[128,256]{1,0:T(8,128)(2,1)} %param.10, bf16[128,256]{1,0:T(8,128)(2,1)S(1)} %broadcast_multiply_fusion), kind=kLoop, calls=%fused_computation | loop fusion | flops 262144 | bytes 262144 | tf_op jit(solution)/shard_map/concatenate | solution.py:174
  2.3 4.1 %collective-permute-start.3 = (bf16[256,256]{1,0:T(8,128)(2,1)S(1)}, bf16[256,256]{1,0:T(8,128)(2,1)S(1)}, u32[]{:S(2)}, u32[]{:S(2)}) collective-permute-start(bf16[256,256]{1,0:T(8,128)(2,1)S(1)} %pad_maximum_fusion.r_0_), channel_id=1, source_target_pairs={{0,16},{4,20},{8,24},{12,28},{16,0},{20,4},{24,8},{28,12},{1,17},{... | collective-permute-start | bytes 393224 | tf_op jit(solution)/shard_map/ppermute | solution.py:161
  6.4 1.6 %collective-permute-start.1 = (bf16[256,256]{1,0:T(8,128)(2,1)S(1)}, bf16[256,256]{1,0:T(8,128)(2,1)S(1)}, u32[]{:S(2)}, u32[]{:S(2)}) collective-permute-start(bf16[256,256]{1,0:T(8,128)(2,1)S(1)} %pad_maximum_fusion.r_0_), channel_id=1, source_target_pairs={{0,8},{4,12},{8,0},{12,4},{16,24},{20,28},{24,16},{28,20},{1,9},{5... | collective-permute-start | bytes 393224 | tf_op jit(solution)/shard_map/ppermute | solution.py:161
  8.0 4.8 %collective-permute-done.3.r_4_ = bf16[256,256]{1,0:T(8,128)(2,1)S(1)} collective-permute-done((bf16[256,256]{1,0:T(8,128)(2,1)S(1)}, bf16[256,256]{1,0:T(8,128)(2,1)S(1)}, u32[]{:S(2)}, u32[]{:S(2)}) %collective-permute-start.3) | collective-permute-done | bytes 131104 | tf_op jit(solution)/shard_map/ppermute | solution.py:161
  12.8 0.6 %collective-permute-start.5 = (bf16[256,256]{1,0:T(8,128)(2,1)S(1)}, bf16[256,256]{1,0:T(8,128)(2,1)S(1)}, u32[]{:S(2)}, u32[]{:S(2)}) collective-permute-start(bf16[256,256]{1,0:T(8,128)(2,1)S(1)} %collective-permute-done.3.r_4_), channel_id=1, source_target_pairs={{0,8},{4,12},{8,0},{12,4},{16,24},{20,28},{24,16},{28,20},{1,9},{5... | collective-permute-start | bytes 393224 | tf_op jit(solution)/shard_map/ppermute | solution.py:161
  13.5 0.5 collective-permute-start.4
  14.0 3.8 %collective-permute-done.5.r_6_ = bf16[256,256]{1,0:T(8,128)(2,1)S(1)} collective-permute-done((bf16[256,256]{1,0:T(8,128)(2,1)S(1)}, bf16[256,256]{1,0:T(8,128)(2,1)S(1)}, u32[]{:S(2)}, u32[]{:S(2)}) %collective-permute-start.5) | collective-permute-done | bytes 131104 | tf_op jit(solution)/shard_map/ppermute | solution.py:161
  17.8 1.6 %collective-permute-start.8 = (bf16[32,256]{1,0:T(8,128)(2,1)}, bf16[32,256]{1,0:T(8,128)(2,1)S(1)}, u32[]{:S(2)}, u32[]{:S(2)}) collective-permute-start(bf16[32,256]{1,0:T(8,128)(2,1)} %r_1_.1), channel_id=1, source_target_pairs={{0,2},{1,3},{2,0},{3,1},{4,6},{5,7},{6,4},{7,5},{8,10},{9,11},{10,... | collective-permute-start | bytes 49160 | tf_op jit(solution)/shard_map/ppermute | solution.py:161
  19.4 2.4 %collective-permute-done.8.r_3_ = bf16[32,256]{1,0:T(8,128)(2,1)S(1)} collective-permute-done((bf16[32,256]{1,0:T(8,128)(2,1)}, bf16[32,256]{1,0:T(8,128)(2,1)S(1)}, u32[]{:S(2)}, u32[]{:S(2)}) %collective-permute-start.8) | collective-permute-done | bytes 16416 | tf_op jit(solution)/shard_map/ppermute | solution.py:161
  21.8 1.5 %collective-permute-start.7 = (bf16[32,256]{1,0:T(8,128)(2,1)}, bf16[32,256]{1,0:T(8,128)(2,1)S(1)}, u32[]{:S(2)}, u32[]{:S(2)}) collective-permute-start(bf16[32,256]{1,0:T(8,128)(2,1)} %r_1_.1), channel_id=1, source_target_pairs={{0,1},{1,0},{2,3},{3,2},{4,5},{5,4},{6,7},{7,6},{8,9},{9,8},{10,11... | collective-permute-start | bytes 49160 | tf_op jit(solution)/shard_map/ppermute | solution.py:161
  23.3 2.4 %collective-permute-done.7.r_2_ = bf16[32,256]{1,0:T(8,128)(2,1)S(1)} collective-permute-done((bf16[32,256]{1,0:T(8,128)(2,1)}, bf16[32,256]{1,0:T(8,128)(2,1)S(1)}, u32[]{:S(2)}, u32[]{:S(2)}) %collective-permute-start.7) | collective-permute-done | bytes 16416 | tf_op jit(solution)/shard_map/ppermute | solution.py:161
  25.7 2.5 %collective-permute-start.9 = (bf16[32,256]{1,0:T(8,128)(2,1)}, bf16[32,256]{1,0:T(8,128)(2,1)S(1)}, u32[]{:S(2)}, u32[]{:S(2)}) collective-permute-start(bf16[32,256]{1,0:T(8,128)(2,1)} %r_1_.1), channel_id=1, source_target_pairs={{0,3},{1,2},{2,1},{3,0},{4,7},{5,6},{6,5},{7,4},{8,11},{9,10},{10,... | collective-permute-start | bytes 49160 | tf_op jit(solution)/shard_map/ppermute | solution.py:161
  28.2 2.4 %collective-permute-done.9.r_4_ = bf16[32,256]{1,0:T(8,128)(2,1)S(1)} collective-permute-done((bf16[32,256]{1,0:T(8,128)(2,1)}, bf16[32,256]{1,0:T(8,128)(2,1)S(1)}, u32[]{:S(2)}, u32[]{:S(2)}) %collective-permute-start.9) | collective-permute-done | bytes 16416 | tf_op jit(solution)/shard_map/ppermute | solution.py:161
  30.6 0.7 %copy-done = s32[4096]{0:T(1024)S(1)} copy-done((s32[4096]{0:T(1024)S(1)}, s32[4096]{0:T(1024)}, u32[]{:S(2)}) %copy-start) | copy-done | bytes 16408
  31.3 0.7 %copy-done.1 = bf16[32,256]{1,0:T(8,128)(2,1)S(1)} copy-done((bf16[32,256]{1,0:T(8,128)(2,1)S(1)}, bf16[32,256]{1,0:T(8,128)(2,1)}, u32[]{:S(2)}) %copy-start.1) | copy-done | bytes 16408
  32.0 0.7 %copy-done.3 = s32[1024]{0:T(1024)S(1)} copy-done((s32[1024]{0:T(1024)S(1)}, s32[1024]{0:T(1024)}, u32[]{:S(2)}) %copy-start.3) | copy-done | bytes 4120
  32.7 0.7 %copy-done.4 = s32[1024]{0:T(1024)S(1)} copy-done((s32[1024]{0:T(1024)S(1)}, s32[1024]{0:T(1024)}, u32[]{:S(2)}) %copy-start.4) | copy-done | bytes 4120
  33.4 0.7 %copy-done.5 = s32[1024]{0:T(1024)S(1)} copy-done((s32[1024]{0:T(1024)S(1)}, s32[1024]{0:T(1024)}, u32[]{:S(2)}) %copy-start.5) | copy-done | bytes 4120
  34.3 3.9 %collective-permute-start.15 = (f32[1,128]{1,0:T(1,128)S(1)}, f32[1,128]{1,0:T(1,128)S(1)}, u32[]{:S(2)}, u32[]{:S(2)}) collective-permute-start(f32[1,128]{1,0:T(1,128)S(1)} %get-tuple-element.12.r_8_), channel_id=1, source_target_pairs={{0,24},{4,28},{8,16},{12,20},{16,8},{20,12},{24,0},{28,4},{1,25},{... | collective-permute-start | bytes 1544 | tf_op jit(solution)/shard_map/ppermute | solution.py:161
  38.2 1.5 %collective-permute-done.15.r_14_ = f32[1,128]{1,0:T(1,128)S(1)} collective-permute-done((f32[1,128]{1,0:T(1,128)S(1)}, f32[1,128]{1,0:T(1,128)S(1)}, u32[]{:S(2)}, u32[]{:S(2)}) %collective-permute-start.15) | collective-permute-done | bytes 544 | tf_op jit(solution)/shard_map/ppermute | solution.py:161
  39.7 0.8 %collective-permute-start.13 = (f32[1,128]{1,0:T(1,128)S(1)}, f32[1,128]{1,0:T(1,128)S(1)}, u32[]{:S(2)}, u32[]{:S(2)}) collective-permute-start(f32[1,128]{1,0:T(1,128)S(1)} %get-tuple-element.12.r_8_), channel_id=1, source_target_pairs={{0,16},{4,20},{8,24},{12,28},{16,0},{20,4},{24,8},{28,12},{1,17},{... | collective-permute-start | bytes 1544 | tf_op jit(solution)/shard_map/ppermute | solution.py:161
  40.6 3.6 %collective-permute-done.13.r_12_ = f32[1,128]{1,0:T(1,128)S(1)} collective-permute-done((f32[1,128]{1,0:T(1,128)S(1)}, f32[1,128]{1,0:T(1,128)S(1)}, u32[]{:S(2)}, u32[]{:S(2)}) %collective-permute-start.13) | collective-permute-done | bytes 544 | tf_op jit(solution)/shard_map/ppermute | solution.py:161
  44.2 1.5 %collective-permute-start.11 = (f32[1,128]{1,0:T(1,128)S(1)}, f32[1,128]{1,0:T(1,128)S(1)}, u32[]{:S(2)}, u32[]{:S(2)}) collective-permute-start(f32[1,128]{1,0:T(1,128)S(1)} %get-tuple-element.12.r_8_), channel_id=1, source_target_pairs={{0,8},{4,12},{8,0},{12,4},{16,24},{20,28},{24,16},{28,20},{1,9},{5... | collective-permute-start | bytes 1544 | tf_op jit(solution)/shard_map/ppermute | solution.py:161
  45.6 2.1 %collective-permute-done.11.r_10_ = f32[1,128]{1,0:T(1,128)S(1)} collective-permute-done((f32[1,128]{1,0:T(1,128)S(1)}, f32[1,128]{1,0:T(1,128)S(1)}, u32[]{:S(2)}, u32[]{:S(2)}) %collective-permute-start.11) | collective-permute-done | bytes 544 | tf_op jit(solution)/shard_map/ppermute | solution.py:161
  47.7 1.1 %collective-permute-done.10.r_9_ = f32[1,128]{1,0:T(1,128)S(1)} collective-permute-done((f32[1,128]{1,0:T(1,128)S(1)}, f32[1,128]{1,0:T(1,128)S(1)}, u32[]{:S(2)}, u32[]{:S(2)}) %collective-permute-start.10) | collective-permute-done | bytes 544 | tf_op jit(solution)/shard_map/ppermute | solution.py:161
  49.1 0.9 %collective-permute-done.16.r_15_ = f32[1,128]{1,0:T(1,128)S(1)} collective-permute-done((f32[1,128]{1,0:T(1,128)S(1)}, f32[1,128]{1,0:T(1,128)S(1)}, u32[]{:S(2)}, u32[]{:S(2)}) %collective-permute-start.16) | collective-permute-done | bytes 544 | tf_op jit(solution)/shard_map/ppermute | solution.py:161
  50.2 0.9 %collective-permute-done.14.r_13_ = f32[1,128]{1,0:T(1,128)S(1)} collective-permute-done((f32[1,128]{1,0:T(1,128)S(1)}, f32[1,128]{1,0:T(1,128)S(1)}, u32[]{:S(2)}, u32[]{:S(2)}) %collective-permute-start.14) | collective-permute-done | bytes 544 | tf_op jit(solution)/shard_map/ppermute | solution.py:161
  51.3 0.7 %copy-done.2 = s32[4096]{0:T(1024)S(1)} copy-done((s32[4096]{0:T(1024)S(1)}, s32[4096]{0:T(1024)}, u32[]{:S(2)}) %copy-start.2) | copy-done | bytes 16408
  52.0 0.7 %copy-done.6 = s32[512]{0:T(512)S(1)} copy-done((s32[512]{0:T(512)S(1)}, s32[512]{0:T(512)}, u32[]{:S(2)}) %copy-start.6) | copy-done | bytes 2072
  52.7 1.6 %shard_map.113 = (f32[1024,1024]{1,0:T(8,128)S(1)}, f32[8,128]{1,0:T(8,128)S(1)}, f32[128,128]{1,0:T(8,128)S(1)}) custom-call(s32[32,128]{1,0:T(8,128)S(1)} %bitcast.8, s32[32,128]{1,0:T(8,128)S(1)} %bitcast.9, s32[4,128]{1,0:T(4,128)S(1)} %bitcast.13), custom_call_target="tpu_custom_call" | custom-call | tf_op jit(solution)/shard_map/pallas_call | solution.py:145
  54.4 2.8 %shard_map.114 = (f32[1,128]{1,0:T(1,128)}, f32[128,256]{1,0:T(8,128)}, f32[128,256]{1,0:T(8,128)}) custom-call(bf16[256,256]{1,0:T(8,128)(2,1)S(1)} %pad_maximum_fusion.r_0_, bf16[256,256]{1,0:T(8,128)(2,1)S(1)} %collective-permute-done.r_1_, bf16[256,256]{1,0:T(8,128)(2,1)S(1)} %collective-permute-done.1.r_2_, ...), custom_call_target="tpu_custom_call" | custom-call | tf_op jit(solution)/shard_map/pallas_call | solution.py:145
  (21 shorter events, 0.9 us)
Async XLA Ops:
  2.3 10.5 %collective-permute-start.3 = (bf16[256,256]{1,0:T(8,128)(2,1)S(1)}, bf16[256,256]{1,0:T(8,128)(2,1)S(1)}, u32[]{:S(2)}, u32[]{:S(2)}) collective-permute-start(bf16[256,256]{1,0:T(8,128)(2,1)S(1)} %pad_maximum_fusion.r_0_), channel_id=1, source_target_pairs={{0,16},{4,20},{8,24},{12,28},{16,0},{20,4},{24,8},{28,12},{1,17},{... | collective-permute-start | bytes 393224 | tf_op jit(solution)/shard_map/ppermute | solution.py:161
  6.4 7.5 %collective-permute-start.1 = (bf16[256,256]{1,0:T(8,128)(2,1)S(1)}, bf16[256,256]{1,0:T(8,128)(2,1)S(1)}, u32[]{:S(2)}, u32[]{:S(2)}) collective-permute-start(bf16[256,256]{1,0:T(8,128)(2,1)S(1)} %pad_maximum_fusion.r_0_), channel_id=1, source_target_pairs={{0,8},{4,12},{8,0},{12,4},{16,24},{20,28},{24,16},{28,20},{1,9},{5... | collective-permute-start | bytes 393224 | tf_op jit(solution)/shard_map/ppermute | solution.py:161
  12.8 5.0 %collective-permute-start.5 = (bf16[256,256]{1,0:T(8,128)(2,1)S(1)}, bf16[256,256]{1,0:T(8,128)(2,1)S(1)}, u32[]{:S(2)}, u32[]{:S(2)}) collective-permute-start(bf16[256,256]{1,0:T(8,128)(2,1)S(1)} %collective-permute-done.3.r_4_), channel_id=1, source_target_pairs={{0,8},{4,12},{8,0},{12,4},{16,24},{20,28},{24,16},{28,20},{1,9},{5... | collective-permute-start | bytes 393224 | tf_op jit(solution)/shard_map/ppermute | solution.py:161
  13.5 40.9 %collective-permute-start = (bf16[256,256]{1,0:T(8,128)(2,1)S(1)}, bf16[256,256]{1,0:T(8,128)(2,1)S(1)}, u32[]{:S(2)}, u32[]{:S(2)}) collective-permute-start(bf16[256,256]{1,0:T(8,128)(2,1)S(1)} %pad_maximum_fusion.r_0_), channel_id=1, source_target_pairs={{0,4},{4,0},{8,12},{12,8},{16,20},{20,16},{24,28},{28,24},{1,5},{5... | collective-permute-start | bytes 393224 | tf_op jit(solution)/shard_map/ppermute | solution.py:161
  13.5 40.9 %collective-permute-start.4 = (bf16[256,256]{1,0:T(8,128)(2,1)S(1)}, bf16[256,256]{1,0:T(8,128)(2,1)S(1)}, u32[]{:S(2)}, u32[]{:S(2)}) collective-permute-start(bf16[256,256]{1,0:T(8,128)(2,1)S(1)} %collective-permute-done.3.r_4_), channel_id=1, source_target_pairs={{0,4},{4,0},{8,12},{12,8},{16,20},{20,16},{24,28},{28,24},{1,5},{5... | collective-permute-start | bytes 393224 | tf_op jit(solution)/shard_map/ppermute | solution.py:161
  14.0 40.4 %collective-permute-start.2 = (bf16[256,256]{1,0:T(8,128)(2,1)S(1)}, bf16[256,256]{1,0:T(8,128)(2,1)S(1)}, u32[]{:S(2)}, u32[]{:S(2)}) collective-permute-start(bf16[256,256]{1,0:T(8,128)(2,1)S(1)} %collective-permute-done.1.r_2_), channel_id=1, source_target_pairs={{0,4},{4,0},{8,12},{12,8},{16,20},{20,16},{24,28},{28,24},{1,5},{5... | collective-permute-start | bytes 393224 | tf_op jit(solution)/shard_map/ppermute | solution.py:161
  17.8 36.5 %collective-permute-start.6 = (bf16[256,256]{1,0:T(8,128)(2,1)S(1)}, bf16[256,256]{1,0:T(8,128)(2,1)S(1)}, u32[]{:S(2)}, u32[]{:S(2)}) collective-permute-start(bf16[256,256]{1,0:T(8,128)(2,1)S(1)} %collective-permute-done.5.r_6_), channel_id=1, source_target_pairs={{0,4},{4,0},{8,12},{12,8},{16,20},{20,16},{24,28},{28,24},{1,5},{5... | collective-permute-start | bytes 393224 | tf_op jit(solution)/shard_map/ppermute | solution.py:161
  17.8 4.0 %collective-permute-start.8 = (bf16[32,256]{1,0:T(8,128)(2,1)}, bf16[32,256]{1,0:T(8,128)(2,1)S(1)}, u32[]{:S(2)}, u32[]{:S(2)}) collective-permute-start(bf16[32,256]{1,0:T(8,128)(2,1)} %r_1_.1), channel_id=1, source_target_pairs={{0,2},{1,3},{2,0},{3,1},{4,6},{5,7},{6,4},{7,5},{8,10},{9,11},{10,... | collective-permute-start | bytes 49160 | tf_op jit(solution)/shard_map/ppermute | solution.py:161
  21.8 3.9 %collective-permute-start.7 = (bf16[32,256]{1,0:T(8,128)(2,1)}, bf16[32,256]{1,0:T(8,128)(2,1)S(1)}, u32[]{:S(2)}, u32[]{:S(2)}) collective-permute-start(bf16[32,256]{1,0:T(8,128)(2,1)} %r_1_.1), channel_id=1, source_target_pairs={{0,1},{1,0},{2,3},{3,2},{4,5},{5,4},{6,7},{7,6},{8,9},{9,8},{10,11... | collective-permute-start | bytes 49160 | tf_op jit(solution)/shard_map/ppermute | solution.py:161
  25.7 4.8 %collective-permute-start.9 = (bf16[32,256]{1,0:T(8,128)(2,1)}, bf16[32,256]{1,0:T(8,128)(2,1)S(1)}, u32[]{:S(2)}, u32[]{:S(2)}) collective-permute-start(bf16[32,256]{1,0:T(8,128)(2,1)} %r_1_.1), channel_id=1, source_target_pairs={{0,3},{1,2},{2,1},{3,0},{4,7},{5,6},{6,5},{7,4},{8,11},{9,10},{10,... | collective-permute-start | bytes 49160 | tf_op jit(solution)/shard_map/ppermute | solution.py:161
  30.6 0.7 %copy-start = (s32[4096]{0:T(1024)S(1)}, s32[4096]{0:T(1024)}, u32[]{:S(2)}) copy-start(s32[4096]{0:T(1024)} %param.11) | copy-start | bytes 49156
  31.3 0.7 %copy-start.1 = (bf16[32,256]{1,0:T(8,128)(2,1)S(1)}, bf16[32,256]{1,0:T(8,128)(2,1)}, u32[]{:S(2)}) copy-start(bf16[32,256]{1,0:T(8,128)(2,1)} %r_1_.1) | copy-start | bytes 49156
  32.0 0.7 %copy-start.3 = (s32[1024]{0:T(1024)S(1)}, s32[1024]{0:T(1024)}, u32[]{:S(2)}) copy-start(s32[1024]{0:T(1024)} %param.14) | copy-start | bytes 12292
  32.7 0.7 %copy-start.4 = (s32[1024]{0:T(1024)S(1)}, s32[1024]{0:T(1024)}, u32[]{:S(2)}) copy-start(s32[1024]{0:T(1024)} %param.15) | copy-start | bytes 12292
  33.4 0.7 %copy-start.5 = (s32[1024]{0:T(1024)S(1)}, s32[1024]{0:T(1024)}, u32[]{:S(2)}) copy-start(s32[1024]{0:T(1024)} %param.16) | copy-start | bytes 12292
  34.3 5.5 %collective-permute-start.15 = (f32[1,128]{1,0:T(1,128)S(1)}, f32[1,128]{1,0:T(1,128)S(1)}, u32[]{:S(2)}, u32[]{:S(2)}) collective-permute-start(f32[1,128]{1,0:T(1,128)S(1)} %get-tuple-element.12.r_8_), channel_id=1, source_target_pairs={{0,24},{4,28},{8,16},{12,20},{16,8},{20,12},{24,0},{28,4},{1,25},{... | collective-permute-start | bytes 1544 | tf_op jit(solution)/shard_map/ppermute | solution.py:161
  39.7 4.4 %collective-permute-start.13 = (f32[1,128]{1,0:T(1,128)S(1)}, f32[1,128]{1,0:T(1,128)S(1)}, u32[]{:S(2)}, u32[]{:S(2)}) collective-permute-start(f32[1,128]{1,0:T(1,128)S(1)} %get-tuple-element.12.r_8_), channel_id=1, source_target_pairs={{0,16},{4,20},{8,24},{12,28},{16,0},{20,4},{24,8},{28,12},{1,17},{... | collective-permute-start | bytes 1544 | tf_op jit(solution)/shard_map/ppermute | solution.py:161
  44.2 3.5 %collective-permute-start.11 = (f32[1,128]{1,0:T(1,128)S(1)}, f32[1,128]{1,0:T(1,128)S(1)}, u32[]{:S(2)}, u32[]{:S(2)}) collective-permute-start(f32[1,128]{1,0:T(1,128)S(1)} %get-tuple-element.12.r_8_), channel_id=1, source_target_pairs={{0,8},{4,12},{8,0},{12,4},{16,24},{20,28},{24,16},{28,20},{1,9},{5... | collective-permute-start | bytes 1544 | tf_op jit(solution)/shard_map/ppermute | solution.py:161
  47.7 1.1 %collective-permute-start.10 = (f32[1,128]{1,0:T(1,128)S(1)}, f32[1,128]{1,0:T(1,128)S(1)}, u32[]{:S(2)}, u32[]{:S(2)}) collective-permute-start(f32[1,128]{1,0:T(1,128)S(1)} %get-tuple-element.12.r_8_), channel_id=1, source_target_pairs={{0,4},{4,0},{8,12},{12,8},{16,20},{20,16},{24,28},{28,24},{1,5},{5... | collective-permute-start | bytes 1544 | tf_op jit(solution)/shard_map/ppermute | solution.py:161
  48.9 1.1 %collective-permute-start.16 = (f32[1,128]{1,0:T(1,128)S(1)}, f32[1,128]{1,0:T(1,128)S(1)}, u32[]{:S(2)}, u32[]{:S(2)}) collective-permute-start(f32[1,128]{1,0:T(1,128)S(1)} %collective-permute-done.15.r_14_), channel_id=1, source_target_pairs={{0,4},{4,0},{8,12},{12,8},{16,20},{20,16},{24,28},{28,24},{1,5},{5... | collective-permute-start | bytes 1544 | tf_op jit(solution)/shard_map/ppermute | solution.py:161
  50.0 1.1 %collective-permute-start.14 = (f32[1,128]{1,0:T(1,128)S(1)}, f32[1,128]{1,0:T(1,128)S(1)}, u32[]{:S(2)}, u32[]{:S(2)}) collective-permute-start(f32[1,128]{1,0:T(1,128)S(1)} %collective-permute-done.13.r_12_), channel_id=1, source_target_pairs={{0,4},{4,0},{8,12},{12,8},{16,20},{20,16},{24,28},{28,24},{1,5},{5... | collective-permute-start | bytes 1544 | tf_op jit(solution)/shard_map/ppermute | solution.py:161
  51.1 3.2 %collective-permute-start.12 = (f32[1,128]{1,0:T(1,128)S(1)}, f32[1,128]{1,0:T(1,128)S(1)}, u32[]{:S(2)}, u32[]{:S(2)}) collective-permute-start(f32[1,128]{1,0:T(1,128)S(1)} %collective-permute-done.11.r_10_), channel_id=1, source_target_pairs={{0,4},{4,0},{8,12},{12,8},{16,20},{20,16},{24,28},{28,24},{1,5},{5... | collective-permute-start | bytes 1544 | tf_op jit(solution)/shard_map/ppermute | solution.py:161
  51.3 0.7 %copy-start.2 = (s32[4096]{0:T(1024)S(1)}, s32[4096]{0:T(1024)}, u32[]{:S(2)}) copy-start(s32[4096]{0:T(1024)} %param.12) | copy-start | bytes 49156
  52.0 0.7 %copy-start.6 = (s32[512]{0:T(512)S(1)}, s32[512]{0:T(512)}, u32[]{:S(2)}) copy-start(s32[512]{0:T(512)} %param.17) | copy-start | bytes 6148

commit v2 on v1

--- a/solution.py
+++ b/solution.py
@@ -29,7 +29,30 @@
     return jnp.broadcast_to(row, (LANES, LANES)).T
 
 
-def prep_kernel(n_batch, ids_ref, logq_ref, counts_ref, bias_ref, weight_ref, wcol_ref):
+def fetch(pairs, sems):
+    copies = [pltpu.make_async_copy(src, dst, sems.at[k]) for k, (src, dst) in enumerate(pairs)]
+    for copy in copies:
+        copy.start()
+    for copy in copies:
+        copy.wait()
+
+
+def prep_kernel(
+    n_batch, ids_hbm, logq_hbm, counts_hbm, mem_ids_hbm, mem_logq_hbm, mem_age_hbm,
+    bias_ref, weight_ref, wcol_ref, mem_bias_ref,
+    ids_ref, logq_ref, counts_ref, mem_ids_ref, mem_logq_ref, mem_age_ref, sems,
+):
+    fetch(
+        [
+            (ids_hbm, ids_ref),
+            (logq_hbm, logq_ref),
+            (counts_hbm, counts_ref),
+            (mem_ids_hbm, mem_ids_ref),
+            (mem_logq_hbm, mem_logq_ref),
+            (mem_age_hbm, mem_age_ref),
+        ],
+        sems,
+    )
     own = lax.axis_index("batch")
     first_block = lax.axis_index("mem") * n_batch
     reqs = counts_ref.shape[0] * LANES
@@ -56,6 +79,11 @@
         if k == 0:
             wcol_ref[...] = as_column(weight)
         rows.append((ids_ref[pl.ds(block, 1), :], start, end))
+    id_col = as_column(mem_ids_ref[pl.ds(own, 1), :])
+    shift_col = as_column(-mem_logq_ref[pl.ds(own, 1), :].astype(jnp.float32) * logq_unit)
+    age_col = as_column(mem_age_ref[pl.ds(own, 1), :])
+    keep = (age_col < AGE_LIMIT) & (id_col != rows[0][0])
+    mem_bias_ref[...] = jnp.where(keep, shift_col, very_low)
     for n in range(n_batch):
         block = first_block + jnp.bitwise_xor(own, n)
         id_col = as_column(ids_ref[pl.ds(block, 1), :])
@@ -72,37 +100,38 @@
 
 
 def bank_kernel(
-    n_batch, pack_ref, s0, s1, s2, s3, ids_ref, mem_ids_ref, mem_logq_ref, mem_age_ref,
-    bank_ref, logit_ref, lse_ref,
+    q_hbm, s0_hbm, s1, s2, s3, mem_bias_ref, bank_ref, logit_ref, lse_ref, q_ref, s0, sems
 ):
-    own = lax.axis_index("batch")
+    fetch([(q_hbm, q_ref), (s0_hbm, s0)], sems)
     group = lax.axis_index("mem")
     slots = s0.shape[0]
     for k, shard in enumerate((s0, s1, s2, s3)):
         at = pl.multiple_of(jnp.bitwise_xor(group, k) * slots, slots)
         bank_ref[pl.ds(at, slots), :] = shard[...]
-    id_row = ids_ref[pl.ds(group * n_batch + own, 1), :]
-    id_col = as_column(mem_ids_ref[pl.ds(own, 1), :])
-    shift_col = as_column(-mem_logq_ref[pl.ds(own, 1), :].astype(jnp.float32) * logq_unit)
-    age_col = as_column(mem_age_ref[pl.ds(own, 1), :])
-    keep = (age_col < AGE_LIMIT) & (id_col != id_row)
-    logit = nt_dot(bank_ref[...], pack_ref[:LANES, :])
-    logit = jnp.where(keep, logit + shift_col, very_low)
+    logit = inv_temp * nt_dot(bank_ref[...], q_ref[...]) + mem_bias_ref[...]
     top = jnp.max(logit, axis=0, keepdims=True)
     total = jnp.sum(jnp.exp(logit - top), axis=0, keepdims=True)
     logit_ref[...] = logit
     lse_ref[...] = top + jnp.log(total)
 
 
+def stack_kernel(*refs):
+    for k, ref in enumerate(refs[:-1]):
+        refs[-1][k : k + 1, :] = ref[...]
+
+
 def main_kernel(n_batch, *refs):
-    packs = refs[:n_batch]
-    lses = refs[n_batch : 2 * n_batch]
-    bias_ref, weight_ref, wcol_ref, bank_ref, mem_logit_ref = refs[2 * n_batch : 2 * n_batch + 5]
-    loss_ref, qgrad_ref, pgrad_ref = refs[2 * n_batch + 5 : 2 * n_batch + 8]
-    items, queries = refs[2 * n_batch + 8 :]
-    for k in range(n_batch):
-        queries[k * LANES : (k + 1) * LANES, :] = packs[k][:LANES, :]
-        items[k * LANES : (k + 1) * LANES, :] = packs[k][LANES:, :]
+    p_refs = refs[:n_batch]
+    q_refs = refs[n_batch : 2 * n_batch]
+    rest = refs[2 * n_batch :]
+    even_ref, odd_ref, bias_ref, weight_ref, wcol_ref, bank_ref, mem_logit_ref = rest[:7]
+    loss_ref, qgrad_ref, pgrad_ref, items, queries, sems = rest[7:]
+    own_rows = pl.ds(0, LANES)
+    fetch([(p_refs[0], items.at[own_rows]), (q_refs[0], queries.at[own_rows])], sems)
+    queries[:LANES, :] = queries[:LANES, :] * jnp.bfloat16(inv_temp)
+    for k in range(1, n_batch):
+        queries[k * LANES : (k + 1) * LANES, :] = q_refs[k][...] * jnp.bfloat16(inv_temp)
+        items[k * LANES : (k + 1) * LANES, :] = p_refs[k][...]
     width = 2 * LANES
     pgrad = -wcol_ref[:, :1] * queries[:LANES, :].astype(jnp.float32)
     for c in range(n_batch // 2):
@@ -111,7 +140,7 @@
         logit = nt_dot(items[...], q_part) + bias_ref[:, at]
         top = jnp.max(logit, axis=0, keepdims=True)
         total = jnp.sum(jnp.exp(logit - top), axis=0, keepdims=True)
-        mem_lse = jnp.concatenate([lses[2 * c][...], lses[2 * c + 1][...]], axis=1)
+        mem_lse = jnp.concatenate([even_ref[c : c + 1, :], odd_ref[c : c + 1, :]], axis=1)
         weight = jnp.concatenate(
             [weight_ref[2 * c : 2 * c + 1, :], weight_ref[2 * c + 1 : 2 * c + 2, :]], axis=1
         )
@@ -137,28 +166,37 @@
     pgrad_ref[...] = pgrad
 
 
-def in_vmem(count):
-    return [pl.BlockSpec(memory_space=pltpu.VMEM)] * count
-
-
-def call(kernel, outs, args, scratch=()):
+def call(kernel, outs, args, hbm=(), scratch=(), cost_us=1):
+    in_vmem = pl.BlockSpec(memory_space=pltpu.VMEM)
+    in_hbm = pl.BlockSpec(memory_space=pltpu.HBM)
     return pl.pallas_call(
         kernel,
         out_shape=outs,
-        in_specs=in_vmem(len(args)),
-        out_specs=in_vmem(len(outs)),
+        in_specs=[in_hbm if k in hbm else in_vmem for k in range(len(args))],
+        out_specs=[in_vmem] * len(outs),
         scratch_shapes=list(scratch),
         compiler_params=pltpu.CompilerParams(vmem_limit_bytes=VMEM_LIMIT),
+        cost_estimate=pl.CostEstimate(
+            flops=int(cost_us * 1e9), bytes_accessed=int(cost_us * 3e6), transcendentals=0
+        ),
     )(*args)
 
 
 def f32(*shape):
     return jax.ShapeDtypeStruct(shape, jnp.float32)
+
+
+def bf16(*shape):
+    return jax.ShapeDtypeStruct(shape, jnp.bfloat16)
 
 
 def swap(array, axis, mask):
     size = lax.axis_size(axis)
     return lax.ppermute(array, axis, [(s, s ^ mask) for s in range(size)])
+
+
+def after(array, *others):
+    return lax.optimization_barrier((array, *others))[0]
 
 
 def small_body(
@@ -167,45 +205,63 @@
     own_count, depth = queries.shape
     n_batch = lax.axis_size("batch")
     group_rows = own_count * n_batch
-    ids = pos_ids.reshape(-1, LANES)
-    logq = pos_logq.reshape(-1, LANES)
-    banks = [a.reshape(-1, LANES) for a in (mem_ids, mem_logq, mem_age)]
-
-    pack = jnp.concatenate([queries * jnp.bfloat16(inv_temp), positives], 0)
-    far = swap(pack, "batch", 4)
-    near = swap(pack, "batch", 2)
+    ints = [
+        a.reshape(-1, LANES) for a in (pos_ids, pos_logq, counts, mem_ids, mem_logq, mem_age)
+    ]
+
+    p, q = {0: positives}, {0: queries}
+    p[4] = swap(positives, "batch", 4)
+    q[4] = swap(queries, "batch", 4)
     shards = [mem_items] + [swap(mem_items, "mem", k) for k in (1, 2, 3)]
-    bias, weight, wcol = call(
+    bias, weight, wcol, mem_bias = call(
         lambda *r: prep_kernel(n_batch, *r),
-        [f32(group_rows, group_rows), f32(n_batch, LANES), f32(LANES, LANES)],
-        (ids, logq, counts.reshape(-1, LANES)),
-    )
-    bank, mem_logit, mem_lse = call(
-        lambda *r: bank_kernel(n_batch, *r),
-        [jax.ShapeDtypeStruct((LANES, depth), jnp.bfloat16), f32(LANES, LANES), f32(1, LANES)],
-        (pack, *shards, ids, *banks),
-    )
-    packs = {0: pack, 4: far, 2: near, 6: swap(far, "batch", 2)}
-    lses = {0: mem_lse}
-    for k in (4, 6, 2):
-        lses[k] = swap(mem_lse, "batch", k)
+        [f32(group_rows, group_rows), f32(n_batch, LANES), f32(LANES, LANES), f32(LANES, LANES)],
+        ints,
+        hbm=range(len(ints)),
+        scratch=[pltpu.VMEM(a.shape, jnp.int32) for a in ints]
+        + [pltpu.SemaphoreType.DMA((len(ints),))],
+        cost_us=3,
+    )
+    bank, mem_logit, lse = call(
+        bank_kernel,
+        [bf16(LANES, depth), f32(LANES, LANES), f32(1, LANES)],
+        (queries, *shards, mem_bias),
+        hbm=(0, 1),
+        scratch=[
+            pltpu.VMEM(queries.shape, jnp.bfloat16),
+            pltpu.VMEM(mem_items.shape, jnp.bfloat16),
+            pltpu.SemaphoreType.DMA((2,)),
+        ],
+    )
+    p[6] = swap(p[4], "batch", 2)
+    p[2] = swap(after(positives, lse), "batch", 2)
+    q[6] = swap(q[4], "batch", 2)
+    q[2] = swap(after(queries, lse), "batch", 2)
+    lses = [lse] + [swap(lse, "batch", k) for k in (2, 4, 6)]
+    (even,) = call(stack_kernel, [f32(4, LANES)], lses)
+    odd = swap(even, "batch", 1)
     for k in (0, 2, 4, 6):
-        packs[k + 1] = swap(packs[k], "batch", 1)
-        lses[k + 1] = swap(lses[k], "batch", 1)
+        for d in (p, q):
+            d[k + 1] = swap(after(d[k], lse) if k == 0 else d[k], "batch", 1)
     order = range(n_batch)
     loss, query_grad, positive_grad = call(
         lambda *r: main_kernel(n_batch, *r),
         [f32(1, LANES), f32(own_count, depth), f32(own_count, depth)],
         (
-            *[packs[k] for k in order],
-            *[lses[k] for k in order],
+            *[p[k] for k in order],
+            *[q[k] for k in order],
+            even,
+            odd,
             bias,
             weight,
             wcol,
             bank,
             mem_logit,
         ),
-        [pltpu.VMEM((group_rows, depth), jnp.bfloat16)] * 2,
+        hbm=(0, n_batch),
+        scratch=[pltpu.VMEM((group_rows, depth), jnp.bfloat16)] * 2
+        + [pltpu.SemaphoreType.DMA((2,))],
+        cost_us=3,
     )
     return loss.reshape(own_count), query_grad, positive_grad
 

time: 57.7 us -> 34.9 us (0.60)
  waiting for transfers between devices: 26 us -> 6.28 us
  other arithmetic: 1.7 us -> 0 us
  starting transfers between devices: 19.3 us -> 18.2 us
  local copies, waits for them, and re-layouts: 4.89 us -> 4.18 us
    ppermute x17 -> x21, waiting for transfers between devices: 26 us -> 6.28 us  [swap(): return lax.ppermute(array, axis, [(s, s ^ mask) for s in range(size)])]
    ppermute x17 -> x21, starting transfers between devices: 19.3 us -> 18.2 us  [swap(): return lax.ppermute(array, axis, [(s, s ^ mask) for s in range(size)])]
    concatenate x1 -> x0, other arithmetic: 0.85 us -> none  [small_body(): pack = jnp.concatenate([queries * jnp.bfloat16(inv_temp), positives], 0)]
    mul x1 -> x0, other arithmetic: 0.85 us -> none  [small_body(): pack = jnp.concatenate([queries * jnp.bfloat16(inv_temp), positives], 0)]
    unnamed x14 -> x18, local copies, waits for them, and re-layouts: 4.89 us -> 4.18 us
    pallas_call x3 -> x4, Pallas kernels: 4.59 us -> 4.98 us  [call(): pl.pallas_call(kernel, out_shape=outs, in_specs=[in_hbm if k in hbm else...]
  transfers between devices with their start and end apart: 17 -> 21, of which waited for: 11 -> 5; matrix products, arithmetic and copies ran while one was open for 0% -> 0% of each run, Pallas kernels for 3% -> 5%
where the time goes in v2:
time: 34.9 us; the launch traced here: 34.4 us
  starting transfers between devices  18.2 us (52%)
  waiting for transfers between devices  6.28 us (18%)
  Pallas kernels  4.98 us (14%)
  local copies, waits for them, and re-layouts  4.18 us (12%)
  between operations  0.75 us (2%)
    ppermute x21, starting transfers between devices, swap(): return lax.ppermute(array, axis, [(s, s ^ mask) for s in range(size)])  18.2 us
    ppermute x21, waiting for transfers between devices, swap(): return lax.ppermute(array, axis, [(s, s ^ mask) for s in range(size)])  6.28 us
    pallas_call x4, Pallas kernels, call(): pl.pallas_call(kernel, out_shape=outs, in_specs=[in_hbm if k in hbm else...  4.98 us
    unnamed x18, local copies, waits for them, and re-layouts  4.18 us
  transfers between devices with their start and end apart: 21, of which 5 were waited for; matrix products, arithmetic and copies ran while one was open for 0% of the time, Pallas kernels for 5%

profile of v2, /device:TPU:0, one launch (start us, length us, event | category | flops | bytes accessed | tf_op | source)
XLA Modules:
  0.0 34.4 jit_solution(11075999821179665803)
XLA Ops:
  0.6 3.0 %collective-permute-start.1 = (bf16[32,256]{1,0:T(8,128)(2,1)}, bf16[32,256]{1,0:T(8,128)(2,1)S(1)}, u32[]{:S(2)}, u32[]{:S(2)}) collective-permute-start(bf16[32,256]{1,0:T(8,128)(2,1)} %s0_hbm.1), channel_id=1, source_target_pairs={{0,2},{1,3},{2,0},{3,1},{4,6},{5,7},{6,4},{7,5},{8,10},{9,11},{10,... | collective-permute-start | bytes 49160 | tf_op jit(solution)/shard_map/ppermute | solution.py:195
  3.7 1.5 %collective-permute-start = (bf16[32,256]{1,0:T(8,128)(2,1)}, bf16[32,256]{1,0:T(8,128)(2,1)S(1)}, u32[]{:S(2)}, u32[]{:S(2)}) collective-permute-start(bf16[32,256]{1,0:T(8,128)(2,1)} %s0_hbm.1), channel_id=1, source_target_pairs={{0,1},{1,0},{2,3},{3,2},{4,5},{5,4},{6,7},{7,6},{8,9},{9,8},{10,11... | collective-permute-start | bytes 49160 | tf_op jit(solution)/shard_map/ppermute | solution.py:195
  5.2 0.0 collective-permute-start.2
  5.2 0.7 %copy-done.2 = s32[4096]{0:T(1024)S(1)} copy-done((s32[4096]{0:T(1024)S(1)}, s32[4096]{0:T(1024)}, u32[]{:S(2)}) %copy-start.2) | copy-done | bytes 16408
  5.9 0.7 %copy-done.3 = s32[4096]{0:T(1024)S(1)} copy-done((s32[4096]{0:T(1024)S(1)}, s32[4096]{0:T(1024)}, u32[]{:S(2)}) %copy-start.3) | copy-done | bytes 16408
  6.6 0.7 %copy-done.5 = s32[1024]{0:T(1024)S(1)} copy-done((s32[1024]{0:T(1024)S(1)}, s32[1024]{0:T(1024)}, u32[]{:S(2)}) %copy-start.5) | copy-done | bytes 4120
  7.3 0.7 %copy-done.6 = s32[1024]{0:T(1024)S(1)} copy-done((s32[1024]{0:T(1024)S(1)}, s32[1024]{0:T(1024)}, u32[]{:S(2)}) %copy-start.6) | copy-done | bytes 4120
  8.0 0.7 %copy-done.7 = s32[1024]{0:T(1024)S(1)} copy-done((s32[1024]{0:T(1024)S(1)}, s32[1024]{0:T(1024)}, u32[]{:S(2)}) %copy-start.7) | copy-done | bytes 4120
  8.7 0.7 %copy-done.8 = s32[512]{0:T(512)S(1)} copy-done((s32[512]{0:T(512)S(1)}, s32[512]{0:T(512)}, u32[]{:S(2)}) %copy-start.8) | copy-done | bytes 2072
  9.4 1.7 %shard_map.112 = (f32[1024,1024]{1,0:T(8,128)S(1)}, f32[8,128]{1,0:T(8,128)S(1)}, f32[128,128]{1,0:T(8,128)S(1)}, f32[128,128]{1,0:T(8,128)S(1)}) custom-call(s32[32,128]{1,0:T(8,128)S(1)} %bitcast.7, s32[32,128]{1,0:T(8,128)S(1)} %bitcast.8, s32[4,128]{1,0:T(4,128)S(1)} %bitcast.12, s32[8,128]{1,0:T(8,128)S(1)} %bitcast.9, s32[8,128]{1,0:T(8,128)S(1)} %bitcast.10, ...), custom_call_target="tpu_custom_call" | custom-call | flops 3000000000 | bytes 9000000 | tf_op jit(solution)/shard_map/pallas_call | solution.py:172
  11.1 0.0 collective-permute-done.s1
  11.1 0.0 collective-permute-done.2.s3
  11.2 0.3 %shard_map.113 = (bf16[128,256]{1,0:T(8,128)(2,1)S(1)}, f32[128,128]{1,0:T(8,128)S(1)}, f32[1,128]{1,0:T(1,128)S(1)}) custom-call(bf16[128,256]{1,0:T(8,128)(2,1)S(1)} %copy-done.1, bf16[32,256]{1,0:T(8,128)(2,1)S(1)} %copy-done.4, bf16[32,256]{1,0:T(8,128)(2,1)S(1)} %collective-permute-done.s1, bf16[32,256]{1,0:T(8,128)(2,1)S(1)} %collective-permute-done.1.s2, ...), custom_call_target="tpu_custom_call" | custom-call | flops 1000000000 | bytes 3000000 | tf_op jit(solution)/shard_map/pallas_call | solution.py:172
  11.5 4.1 %collective-permute-start.19 = (f32[1,128]{1,0:T(1,128)S(1)}, f32[1,128]{1,0:T(1,128)S(1)}, u32[]{:S(2)}, u32[]{:S(2)}) collective-permute-start(f32[1,128]{1,0:T(1,128)S(1)} %get-tuple-element.16.refs_0_), channel_id=1, source_target_pairs={{0,24},{4,28},{8,16},{12,20},{16,8},{20,12},{24,0},{28,4},{1,25},{... | collective-permute-start | bytes 1544 | tf_op jit(solution)/shard_map/ppermute | solution.py:195
  15.6 0.6 %collective-permute-start.17 = (f32[1,128]{1,0:T(1,128)S(1)}, f32[1,128]{1,0:T(1,128)S(1)}, u32[]{:S(2)}, u32[]{:S(2)}) collective-permute-start(f32[1,128]{1,0:T(1,128)S(1)} %get-tuple-element.16.refs_0_), channel_id=1, source_target_pairs={{0,8},{4,12},{8,0},{12,4},{16,24},{20,28},{24,16},{28,20},{1,9},{5... | collective-permute-start | bytes 1544 | tf_op jit(solution)/shard_map/ppermute | solution.py:195
  16.3 2.3 %collective-permute-start.13 = (bf16[128,256]{1,0:T(8,128)(2,1)S(1)}, bf16[128,256]{1,0:T(8,128)(2,1)S(1)}, u32[]{:S(2)}, u32[]{:S(2)}) collective-permute-start(bf16[128,256]{1,0:T(8,128)(2,1)S(1)} %copy-done.1), channel_id=1, source_target_pairs={{0,16},{4,20},{8,24},{12,28},{16,0},{20,4},{24,8},{28,12},{1,17},{... | collective-permute-start | bytes 196616 | tf_op jit(solution)/shard_map/ppermute | solution.py:195
  18.5 0.6 %collective-permute-start.6 = (bf16[128,256]{1,0:T(8,128)(2,1)S(1)}, bf16[128,256]{1,0:T(8,128)(2,1)S(1)}, u32[]{:S(2)}, u32[]{:S(2)}) collective-permute-start(bf16[128,256]{1,0:T(8,128)(2,1)S(1)} %copy-done), channel_id=1, source_target_pairs={{0,16},{4,20},{8,24},{12,28},{16,0},{20,4},{24,8},{28,12},{1,17},{... | collective-permute-start | bytes 196616 | tf_op jit(solution)/shard_map/ppermute | solution.py:195
  19.2 1.5 %collective-permute-start.4 = (bf16[128,256]{1,0:T(8,128)(2,1)S(1)}, bf16[128,256]{1,0:T(8,128)(2,1)S(1)}, u32[]{:S(2)}, u32[]{:S(2)}) collective-permute-start(bf16[128,256]{1,0:T(8,128)(2,1)S(1)} %copy-done), channel_id=1, source_target_pairs={{0,8},{4,12},{8,0},{12,4},{16,24},{20,28},{24,16},{28,20},{1,9},{5... | collective-permute-start | bytes 196616 | tf_op jit(solution)/shard_map/ppermute | solution.py:195
  20.7 0.5 %collective-permute-start.20 = (f32[4,128]{1,0:T(4,128)S(1)}, f32[4,128]{1,0:T(4,128)S(1)}, u32[]{:S(2)}, u32[]{:S(2)}) collective-permute-start(f32[4,128]{1,0:T(4,128)S(1)} %shard_map.114.r_16_), channel_id=1, source_target_pairs={{0,4},{4,0},{8,12},{12,8},{16,20},{20,16},{24,28},{28,24},{1,5},{5... | collective-permute-start | bytes 6152 | tf_op jit(solution)/shard_map/ppermute | solution.py:195
  21.2 0.8 %collective-permute-done.20.r_17_ = f32[4,128]{1,0:T(4,128)S(1)} collective-permute-done((f32[4,128]{1,0:T(4,128)S(1)}, f32[4,128]{1,0:T(4,128)S(1)}, u32[]{:S(2)}, u32[]{:S(2)}) %collective-permute-start.20) | collective-permute-done | bytes 2080 | tf_op jit(solution)/shard_map/ppermute | solution.py:195
  22.0 0.6 %collective-permute-start.11 = (bf16[128,256]{1,0:T(8,128)(2,1)S(1)}, bf16[128,256]{1,0:T(8,128)(2,1)S(1)}, u32[]{:S(2)}, u32[]{:S(2)}) collective-permute-start(bf16[128,256]{1,0:T(8,128)(2,1)S(1)} %copy-done.1), channel_id=1, source_target_pairs={{0,8},{4,12},{8,0},{12,4},{16,24},{20,28},{24,16},{28,20},{1,9},{5... | collective-permute-start | bytes 196616 | tf_op jit(solution)/shard_map/ppermute | solution.py:195
  22.6 1.3 %collective-permute-done.6.r_4_ = bf16[128,256]{1,0:T(8,128)(2,1)S(1)} collective-permute-done((bf16[128,256]{1,0:T(8,128)(2,1)S(1)}, bf16[128,256]{1,0:T(8,128)(2,1)S(1)}, u32[]{:S(2)}, u32[]{:S(2)}) %collective-permute-start.6) | collective-permute-done | bytes 65568 | tf_op jit(solution)/shard_map/ppermute | solution.py:195
  23.9 1.9 %collective-permute-start.8 = (bf16[128,256]{1,0:T(8,128)(2,1)S(1)}, bf16[128,256]{1,0:T(8,128)(2,1)S(1)}, u32[]{:S(2)}, u32[]{:S(2)}) collective-permute-start(bf16[128,256]{1,0:T(8,128)(2,1)S(1)} %collective-permute-done.6.r_4_), channel_id=1, source_target_pairs={{0,8},{4,12},{8,0},{12,4},{16,24},{20,28},{24,16},{28,20},{1,9},{5... | collective-permute-start | bytes 196616 | tf_op jit(solution)/shard_map/ppermute | solution.py:195
  25.7 0.2 collective-permute-start.7
  26.0 0.3 %collective-permute-start.15 = (bf16[128,256]{1,0:T(8,128)(2,1)S(1)}, bf16[128,256]{1,0:T(8,128)(2,1)S(1)}, u32[]{:S(2)}, u32[]{:S(2)}) collective-permute-start(bf16[128,256]{1,0:T(8,128)(2,1)S(1)} %collective-permute-done.13.r_12_), channel_id=1, source_target_pairs={{0,8},{4,12},{8,0},{12,4},{16,24},{20,28},{24,16},{28,20},{1,9},{5... | collective-permute-start | bytes 196616 | tf_op jit(solution)/shard_map/ppermute | solution.py:195
  26.3 0.0 collective-permute-start.14
  26.3 0.5 %collective-permute-start.5 = (bf16[128,256]{1,0:T(8,128)(2,1)S(1)}, bf16[128,256]{1,0:T(8,128)(2,1)S(1)}, u32[]{:S(2)}, u32[]{:S(2)}) collective-permute-start(bf16[128,256]{1,0:T(8,128)(2,1)S(1)} %collective-permute-done.4.r_2_), channel_id=1, source_target_pairs={{0,4},{4,0},{8,12},{12,8},{16,20},{20,16},{24,28},{28,24},{1,5},{5... | collective-permute-start | bytes 196616 | tf_op jit(solution)/shard_map/ppermute | solution.py:195
  26.8 1.7 %collective-permute-done.8.r_6_ = bf16[128,256]{1,0:T(8,128)(2,1)S(1)} collective-permute-done((bf16[128,256]{1,0:T(8,128)(2,1)S(1)}, bf16[128,256]{1,0:T(8,128)(2,1)S(1)}, u32[]{:S(2)}, u32[]{:S(2)}) %collective-permute-start.8) | collective-permute-done | bytes 65568 | tf_op jit(solution)/shard_map/ppermute | solution.py:195
  28.5 0.5 %collective-permute-start.9 = (bf16[128,256]{1,0:T(8,128)(2,1)S(1)}, bf16[128,256]{1,0:T(8,128)(2,1)S(1)}, u32[]{:S(2)}, u32[]{:S(2)}) collective-permute-start(bf16[128,256]{1,0:T(8,128)(2,1)S(1)} %collective-permute-done.8.r_6_), channel_id=1, source_target_pairs={{0,4},{4,0},{8,12},{12,8},{16,20},{20,16},{24,28},{28,24},{1,5},{5... | collective-permute-start | bytes 196616 | tf_op jit(solution)/shard_map/ppermute | solution.py:195
  29.0 1.2 %collective-permute-done.15.r_14_ = bf16[128,256]{1,0:T(8,128)(2,1)S(1)} collective-permute-done((bf16[128,256]{1,0:T(8,128)(2,1)S(1)}, bf16[128,256]{1,0:T(8,128)(2,1)S(1)}, u32[]{:S(2)}, u32[]{:S(2)}) %collective-permute-start.15) | collective-permute-done | bytes 65568 | tf_op jit(solution)/shard_map/ppermute | solution.py:195
  30.3 1.2 %collective-permute-done.16.r_15_ = bf16[128,256]{1,0:T(8,128)(2,1)S(1)} collective-permute-done((bf16[128,256]{1,0:T(8,128)(2,1)S(1)}, bf16[128,256]{1,0:T(8,128)(2,1)S(1)}, u32[]{:S(2)}, u32[]{:S(2)}) %collective-permute-start.16) | collective-permute-done | bytes 65568 | tf_op jit(solution)/shard_map/ppermute | solution.py:195
  31.5 2.9 %shard_map.115 = (f32[1,128]{1,0:T(1,128)}, f32[128,256]{1,0:T(8,128)}, f32[128,256]{1,0:T(8,128)}) custom-call(bf16[128,256]{1,0:T(8,128)(2,1)S(1)} %copy-done, bf16[128,256]{1,0:T(8,128)(2,1)S(1)} %collective-permute-done.3.r_1_, bf16[128,256]{1,0:T(8,128)(2,1)S(1)} %collective-permute-done.4.r_2_, bf16[128,256]{1,0:T(8,128)(2,1)S(1)} %collective-permute-done.5.r_3_, ...), custom_call_target="tpu_custom_call" | custom-call | flops 3000000000 | bytes 9000000 | tf_op jit(solution)/shard_map/pallas_call | solution.py:172
  (32 shorter events, 0.1 us)
Async XLA Ops:
  0.6 10.5 %collective-permute-start.1 = (bf16[32,256]{1,0:T(8,128)(2,1)}, bf16[32,256]{1,0:T(8,128)(2,1)S(1)}, u32[]{:S(2)}, u32[]{:S(2)}) collective-permute-start(bf16[32,256]{1,0:T(8,128)(2,1)} %s0_hbm.1), channel_id=1, source_target_pairs={{0,2},{1,3},{2,0},{3,1},{4,6},{5,7},{6,4},{7,5},{8,10},{9,11},{10,... | collective-permute-start | bytes 49160 | tf_op jit(solution)/shard_map/ppermute | solution.py:195
  3.7 7.5 %collective-permute-start = (bf16[32,256]{1,0:T(8,128)(2,1)}, bf16[32,256]{1,0:T(8,128)(2,1)S(1)}, u32[]{:S(2)}, u32[]{:S(2)}) collective-permute-start(bf16[32,256]{1,0:T(8,128)(2,1)} %s0_hbm.1), channel_id=1, source_target_pairs={{0,1},{1,0},{2,3},{3,2},{4,5},{5,4},{6,7},{7,6},{8,9},{9,8},{10,11... | collective-permute-start | bytes 49160 | tf_op jit(solution)/shard_map/ppermute | solution.py:195
  5.2 6.0 %collective-permute-start.2 = (bf16[32,256]{1,0:T(8,128)(2,1)}, bf16[32,256]{1,0:T(8,128)(2,1)S(1)}, u32[]{:S(2)}, u32[]{:S(2)}) collective-permute-start(bf16[32,256]{1,0:T(8,128)(2,1)} %s0_hbm.1), channel_id=1, source_target_pairs={{0,3},{1,2},{2,1},{3,0},{4,7},{5,6},{6,5},{7,4},{8,11},{9,10},{10,... | collective-permute-start | bytes 49160 | tf_op jit(solution)/shard_map/ppermute | solution.py:195
  5.2 0.7 %copy-start.2 = (s32[4096]{0:T(1024)S(1)}, s32[4096]{0:T(1024)}, u32[]{:S(2)}) copy-start(s32[4096]{0:T(1024)} %param.11) | copy-start | bytes 49156
  5.9 0.7 %copy-start.3 = (s32[4096]{0:T(1024)S(1)}, s32[4096]{0:T(1024)}, u32[]{:S(2)}) copy-start(s32[4096]{0:T(1024)} %param.12) | copy-start | bytes 49156
  6.6 0.7 %copy-start.5 = (s32[1024]{0:T(1024)S(1)}, s32[1024]{0:T(1024)}, u32[]{:S(2)}) copy-start(s32[1024]{0:T(1024)} %param.14) | copy-start | bytes 12292
  7.3 0.7 %copy-start.6 = (s32[1024]{0:T(1024)S(1)}, s32[1024]{0:T(1024)}, u32[]{:S(2)}) copy-start(s32[1024]{0:T(1024)} %param.15) | copy-start | bytes 12292
  8.0 0.7 %copy-start.7 = (s32[1024]{0:T(1024)S(1)}, s32[1024]{0:T(1024)}, u32[]{:S(2)}) copy-start(s32[1024]{0:T(1024)} %param.16) | copy-start | bytes 12292
  8.7 0.7 %copy-start.8 = (s32[512]{0:T(512)S(1)}, s32[512]{0:T(512)}, u32[]{:S(2)}) copy-start(s32[512]{0:T(512)} %param.17) | copy-start | bytes 6148
  9.4 1.8 %copy-start.1 = (bf16[128,256]{1,0:T(8,128)(2,1)S(1)}, bf16[128,256]{1,0:T(8,128)(2,1)}, u32[]{:S(2)}) copy-start(bf16[128,256]{1,0:T(8,128)(2,1)} %r_8_.1) | copy-start | bytes 196612
  9.4 1.8 %copy-start.4 = (bf16[32,256]{1,0:T(8,128)(2,1)S(1)}, bf16[32,256]{1,0:T(8,128)(2,1)}, u32[]{:S(2)}) copy-start(bf16[32,256]{1,0:T(8,128)(2,1)} %s0_hbm.1) | copy-start | bytes 49156
  9.4 9.2 %copy-start = (bf16[128,256]{1,0:T(8,128)(2,1)S(1)}, bf16[128,256]{1,0:T(8,128)(2,1)}, u32[]{:S(2)}) copy-start(bf16[128,256]{1,0:T(8,128)(2,1)} %r_0_.1) | copy-start | bytes 196612
  11.5 7.7 %collective-permute-start.19 = (f32[1,128]{1,0:T(1,128)S(1)}, f32[1,128]{1,0:T(1,128)S(1)}, u32[]{:S(2)}, u32[]{:S(2)}) collective-permute-start(f32[1,128]{1,0:T(1,128)S(1)} %get-tuple-element.16.refs_0_), channel_id=1, source_target_pairs={{0,24},{4,28},{8,16},{12,20},{16,8},{20,12},{24,0},{28,4},{1,25},{... | collective-permute-start | bytes 1544 | tf_op jit(solution)/shard_map/ppermute | solution.py:195
  15.6 5.0 %collective-permute-start.18 = (f32[1,128]{1,0:T(1,128)S(1)}, f32[1,128]{1,0:T(1,128)S(1)}, u32[]{:S(2)}, u32[]{:S(2)}) collective-permute-start(f32[1,128]{1,0:T(1,128)S(1)} %get-tuple-element.16.refs_0_), channel_id=1, source_target_pairs={{0,16},{4,20},{8,24},{12,28},{16,0},{20,4},{24,8},{28,12},{1,17},{... | collective-permute-start | bytes 1544 | tf_op jit(solution)/shard_map/ppermute | solution.py:195
  15.6 5.0 %collective-permute-start.17 = (f32[1,128]{1,0:T(1,128)S(1)}, f32[1,128]{1,0:T(1,128)S(1)}, u32[]{:S(2)}, u32[]{:S(2)}) collective-permute-start(f32[1,128]{1,0:T(1,128)S(1)} %get-tuple-element.16.refs_0_), channel_id=1, source_target_pairs={{0,8},{4,12},{8,0},{12,4},{16,24},{20,28},{24,16},{28,20},{1,9},{5... | collective-permute-start | bytes 1544 | tf_op jit(solution)/shard_map/ppermute | solution.py:195
  16.3 7.6 %collective-permute-start.13 = (bf16[128,256]{1,0:T(8,128)(2,1)S(1)}, bf16[128,256]{1,0:T(8,128)(2,1)S(1)}, u32[]{:S(2)}, u32[]{:S(2)}) collective-permute-start(bf16[128,256]{1,0:T(8,128)(2,1)S(1)} %copy-done.1), channel_id=1, source_target_pairs={{0,16},{4,20},{8,24},{12,28},{16,0},{20,4},{24,8},{28,12},{1,17},{... | collective-permute-start | bytes 196616 | tf_op jit(solution)/shard_map/ppermute | solution.py:195
  18.5 5.3 %collective-permute-start.6 = (bf16[128,256]{1,0:T(8,128)(2,1)S(1)}, bf16[128,256]{1,0:T(8,128)(2,1)S(1)}, u32[]{:S(2)}, u32[]{:S(2)}) collective-permute-start(bf16[128,256]{1,0:T(8,128)(2,1)S(1)} %copy-done), channel_id=1, source_target_pairs={{0,16},{4,20},{8,24},{12,28},{16,0},{20,4},{24,8},{28,12},{1,17},{... | collective-permute-start | bytes 196616 | tf_op jit(solution)/shard_map/ppermute | solution.py:195
  19.2 6.6 %collective-permute-start.4 = (bf16[128,256]{1,0:T(8,128)(2,1)S(1)}, bf16[128,256]{1,0:T(8,128)(2,1)S(1)}, u32[]{:S(2)}, u32[]{:S(2)}) collective-permute-start(bf16[128,256]{1,0:T(8,128)(2,1)S(1)} %copy-done), channel_id=1, source_target_pairs={{0,8},{4,12},{8,0},{12,4},{16,24},{20,28},{24,16},{28,20},{1,9},{5... | collective-permute-start | bytes 196616 | tf_op jit(solution)/shard_map/ppermute | solution.py:195
  20.6 5.3 %collective-permute-start.3 = (bf16[128,256]{1,0:T(8,128)(2,1)S(1)}, bf16[128,256]{1,0:T(8,128)(2,1)S(1)}, u32[]{:S(2)}, u32[]{:S(2)}) collective-permute-start(bf16[128,256]{1,0:T(8,128)(2,1)S(1)} %copy-done), channel_id=1, source_target_pairs={{0,4},{4,0},{8,12},{12,8},{16,20},{20,16},{24,28},{28,24},{1,5},{5... | collective-permute-start | bytes 196616 | tf_op jit(solution)/shard_map/ppermute | solution.py:195
  20.7 1.3 %collective-permute-start.20 = (f32[4,128]{1,0:T(4,128)S(1)}, f32[4,128]{1,0:T(4,128)S(1)}, u32[]{:S(2)}, u32[]{:S(2)}) collective-permute-start(f32[4,128]{1,0:T(4,128)S(1)} %shard_map.114.r_16_), channel_id=1, source_target_pairs={{0,4},{4,0},{8,12},{12,8},{16,20},{20,16},{24,28},{28,24},{1,5},{5... | collective-permute-start | bytes 6152 | tf_op jit(solution)/shard_map/ppermute | solution.py:195
  22.0 4.3 %collective-permute-start.11 = (bf16[128,256]{1,0:T(8,128)(2,1)S(1)}, bf16[128,256]{1,0:T(8,128)(2,1)S(1)}, u32[]{:S(2)}, u32[]{:S(2)}) collective-permute-start(bf16[128,256]{1,0:T(8,128)(2,1)S(1)} %copy-done.1), channel_id=1, source_target_pairs={{0,8},{4,12},{8,0},{12,4},{16,24},{20,28},{24,16},{28,20},{1,9},{5... | collective-permute-start | bytes 196616 | tf_op jit(solution)/shard_map/ppermute | solution.py:195
  23.9 2.5 %collective-permute-start.10 = (bf16[128,256]{1,0:T(8,128)(2,1)S(1)}, bf16[128,256]{1,0:T(8,128)(2,1)S(1)}, u32[]{:S(2)}, u32[]{:S(2)}) collective-permute-start(bf16[128,256]{1,0:T(8,128)(2,1)S(1)} %copy-done.1), channel_id=1, source_target_pairs={{0,4},{4,0},{8,12},{12,8},{16,20},{20,16},{24,28},{28,24},{1,5},{5... | collective-permute-start | bytes 196616 | tf_op jit(solution)/shard_map/ppermute | solution.py:195
  23.9 4.6 %collective-permute-start.8 = (bf16[128,256]{1,0:T(8,128)(2,1)S(1)}, bf16[128,256]{1,0:T(8,128)(2,1)S(1)}, u32[]{:S(2)}, u32[]{:S(2)}) collective-permute-start(bf16[128,256]{1,0:T(8,128)(2,1)S(1)} %collective-permute-done.6.r_4_), channel_id=1, source_target_pairs={{0,8},{4,12},{8,0},{12,4},{16,24},{20,28},{24,16},{28,20},{1,9},{5... | collective-permute-start | bytes 196616 | tf_op jit(solution)/shard_map/ppermute | solution.py:195
  25.7 2.8 %collective-permute-start.7 = (bf16[128,256]{1,0:T(8,128)(2,1)S(1)}, bf16[128,256]{1,0:T(8,128)(2,1)S(1)}, u32[]{:S(2)}, u32[]{:S(2)}) collective-permute-start(bf16[128,256]{1,0:T(8,128)(2,1)S(1)} %collective-permute-done.6.r_4_), channel_id=1, source_target_pairs={{0,4},{4,0},{8,12},{12,8},{16,20},{20,16},{24,28},{28,24},{1,5},{5... | collective-permute-start | bytes 196616 | tf_op jit(solution)/shard_map/ppermute | solution.py:195
  26.0 4.3 %collective-permute-start.15 = (bf16[128,256]{1,0:T(8,128)(2,1)S(1)}, bf16[128,256]{1,0:T(8,128)(2,1)S(1)}, u32[]{:S(2)}, u32[]{:S(2)}) collective-permute-start(bf16[128,256]{1,0:T(8,128)(2,1)S(1)} %collective-permute-done.13.r_12_), channel_id=1, source_target_pairs={{0,8},{4,12},{8,0},{12,4},{16,24},{20,28},{24,16},{28,20},{1,9},{5... | collective-permute-start | bytes 196616 | tf_op jit(solution)/shard_map/ppermute | solution.py:195
  26.3 3.9 %collective-permute-start.14 = (bf16[128,256]{1,0:T(8,128)(2,1)S(1)}, bf16[128,256]{1,0:T(8,128)(2,1)S(1)}, u32[]{:S(2)}, u32[]{:S(2)}) collective-permute-start(bf16[128,256]{1,0:T(8,128)(2,1)S(1)} %collective-permute-done.13.r_12_), channel_id=1, source_target_pairs={{0,4},{4,0},{8,12},{12,8},{16,20},{20,16},{24,28},{28,24},{1,5},{5... | collective-permute-start | bytes 196616 | tf_op jit(solution)/shard_map/ppermute | solution.py:195
  26.3 3.9 %collective-permute-start.5 = (bf16[128,256]{1,0:T(8,128)(2,1)S(1)}, bf16[128,256]{1,0:T(8,128)(2,1)S(1)}, u32[]{:S(2)}, u32[]{:S(2)}) collective-permute-start(bf16[128,256]{1,0:T(8,128)(2,1)S(1)} %collective-permute-done.4.r_2_), channel_id=1, source_target_pairs={{0,4},{4,0},{8,12},{12,8},{16,20},{20,16},{24,28},{28,24},{1,5},{5... | collective-permute-start | bytes 196616 | tf_op jit(solution)/shard_map/ppermute | solution.py:195
  28.5 1.8 %collective-permute-start.12 = (bf16[128,256]{1,0:T(8,128)(2,1)S(1)}, bf16[128,256]{1,0:T(8,128)(2,1)S(1)}, u32[]{:S(2)}, u32[]{:S(2)}) collective-permute-start(bf16[128,256]{1,0:T(8,128)(2,1)S(1)} %collective-permute-done.11.r_10_), channel_id=1, source_target_pairs={{0,4},{4,0},{8,12},{12,8},{16,20},{20,16},{24,28},{28,24},{1,5},{5... | collective-permute-start | bytes 196616 | tf_op jit(solution)/shard_map/ppermute | solution.py:195
  28.5 1.8 %collective-permute-start.9 = (bf16[128,256]{1,0:T(8,128)(2,1)S(1)}, bf16[128,256]{1,0:T(8,128)(2,1)S(1)}, u32[]{:S(2)}, u32[]{:S(2)}) collective-permute-start(bf16[128,256]{1,0:T(8,128)(2,1)S(1)} %collective-permute-done.8.r_6_), channel_id=1, source_target_pairs={{0,4},{4,0},{8,12},{12,8},{16,20},{20,16},{24,28},{28,24},{1,5},{5... | collective-permute-start | bytes 196616 | tf_op jit(solution)/shard_map/ppermute | solution.py:195
  30.3 1.3 %collective-permute-start.16 = (bf16[128,256]{1,0:T(8,128)(2,1)S(1)}, bf16[128,256]{1,0:T(8,128)(2,1)S(1)}, u32[]{:S(2)}, u32[]{:S(2)}) collective-permute-start(bf16[128,256]{1,0:T(8,128)(2,1)S(1)} %collective-permute-done.15.r_14_), channel_id=1, source_target_pairs={{0,4},{4,0},{8,12},{12,8},{16,20},{20,16},{24,28},{28,24},{1,5},{5... | collective-permute-start | bytes 196616 | tf_op jit(solution)/shard_map/ppermute | solution.py:195

commit v3 on v2

--- a/solution.py
+++ b/solution.py
@@ -37,22 +37,19 @@
         copy.wait()
 
 
+def pack_kernel(count, *refs):
+    ins, outs = refs[: count + 2], refs[count + 2 : 2 * count + 3]
+    q_ref, sems = refs[-2:]
+    pack_ref = outs[-1]
+    rows = q_ref.shape[0]
+    fetch([*zip(ins[:count], outs[:count]), (ins[count], q_ref), (ins[count + 1], pack_ref.at[pl.ds(rows, rows)])], sems)
+    pack_ref[:rows, :] = q_ref[...] * jnp.bfloat16(inv_temp)
+
+
 def prep_kernel(
-    n_batch, ids_hbm, logq_hbm, counts_hbm, mem_ids_hbm, mem_logq_hbm, mem_age_hbm,
+    n_batch, ids_ref, logq_ref, counts_ref, mem_ids_ref, mem_logq_ref, mem_age_ref,
     bias_ref, weight_ref, wcol_ref, mem_bias_ref,
-    ids_ref, logq_ref, counts_ref, mem_ids_ref, mem_logq_ref, mem_age_ref, sems,
 ):
-    fetch(
-        [
-            (ids_hbm, ids_ref),
-            (logq_hbm, logq_ref),
-            (counts_hbm, counts_ref),
-            (mem_ids_hbm, mem_ids_ref),
-            (mem_logq_hbm, mem_logq_ref),
-            (mem_age_hbm, mem_age_ref),
-        ],
-        sems,
-    )
     own = lax.axis_index("batch")
     first_block = lax.axis_index("mem") * n_batch
     reqs = counts_ref.shape[0] * LANES
@@ -99,16 +96,13 @@
             )
 
 
-def bank_kernel(
-    q_hbm, s0_hbm, s1, s2, s3, mem_bias_ref, bank_ref, logit_ref, lse_ref, q_ref, s0, sems
-):
-    fetch([(q_hbm, q_ref), (s0_hbm, s0)], sems)
+def bank_kernel(pack_ref, s0, s1, s2, s3, mem_bias_ref, bank_ref, logit_ref, lse_ref):
     group = lax.axis_index("mem")
     slots = s0.shape[0]
     for k, shard in enumerate((s0, s1, s2, s3)):
         at = pl.multiple_of(jnp.bitwise_xor(group, k) * slots, slots)
         bank_ref[pl.ds(at, slots), :] = shard[...]
-    logit = inv_temp * nt_dot(bank_ref[...], q_ref[...]) + mem_bias_ref[...]
+    logit = nt_dot(bank_ref[...], pack_ref[:LANES, :]) + mem_bias_ref[...]
     top = jnp.max(logit, axis=0, keepdims=True)
     total = jnp.sum(jnp.exp(logit - top), axis=0, keepdims=True)
     logit_ref[...] = logit
@@ -116,22 +110,25 @@
 
 
 def stack_kernel(*refs):
-    for k, ref in enumerate(refs[:-1]):
-        refs[-1][k : k + 1, :] = ref[...]
+    first = 0
+    for ref in refs[:-1]:
+        refs[-1][first : first + ref.shape[0], :] = ref[...]
+        first += ref.shape[0]
 
 
 def main_kernel(n_batch, *refs):
-    p_refs = refs[:n_batch]
-    q_refs = refs[n_batch : 2 * n_batch]
-    rest = refs[2 * n_batch :]
-    even_ref, odd_ref, bias_ref, weight_ref, wcol_ref, bank_ref, mem_logit_ref = rest[:7]
-    loss_ref, qgrad_ref, pgrad_ref, items, queries, sems = rest[7:]
-    own_rows = pl.ds(0, LANES)
-    fetch([(p_refs[0], items.at[own_rows]), (q_refs[0], queries.at[own_rows])], sems)
-    queries[:LANES, :] = queries[:LANES, :] * jnp.bfloat16(inv_temp)
-    for k in range(1, n_batch):
-        queries[k * LANES : (k + 1) * LANES, :] = q_refs[k][...] * jnp.bfloat16(inv_temp)
-        items[k * LANES : (k + 1) * LANES, :] = p_refs[k][...]
+    evens = refs[: n_batch // 2]
+    odd_ref, odd_last_ref = refs[n_batch // 2 : n_batch // 2 + 2]
+    rest = refs[n_batch // 2 + 2 :]
+    even_ref, odd_lse_ref, bias_ref, weight_ref, wcol_ref, bank_ref, mem_logit_ref = rest[:7]
+    loss_ref, qgrad_ref, pgrad_ref, items, queries = rest[7:]
+    block = evens[0].shape[0]
+    for k in range(n_batch // 2):
+        odd = odd_last_ref if k == n_batch // 2 - 1 else odd_ref.at[pl.ds(k * block, block)]
+        for parity, ref in enumerate((evens[k], odd)):
+            at = (2 * k + parity) * LANES
+            queries[at : at + LANES, :] = ref[:LANES, :]
+            items[at : at + LANES, :] = ref[LANES:, :]
     width = 2 * LANES
     pgrad = -wcol_ref[:, :1] * queries[:LANES, :].astype(jnp.float32)
     for c in range(n_batch // 2):
@@ -140,7 +137,7 @@
         logit = nt_dot(items[...], q_part) + bias_ref[:, at]
         top = jnp.max(logit, axis=0, keepdims=True)
         total = jnp.sum(jnp.exp(logit - top), axis=0, keepdims=True)
-        mem_lse = jnp.concatenate([even_ref[c : c + 1, :], odd_ref[c : c + 1, :]], axis=1)
+        mem_lse = jnp.concatenate([even_ref[c : c + 1, :], odd_lse_ref[c : c + 1, :]], axis=1)
         weight = jnp.concatenate(
             [weight_ref[2 * c : 2 * c + 1, :], weight_ref[2 * c + 1 : 2 * c + 2, :]], axis=1
         )
@@ -169,6 +166,10 @@
 def call(kernel, outs, args, hbm=(), scratch=(), cost_us=1):
     in_vmem = pl.BlockSpec(memory_space=pltpu.VMEM)
     in_hbm = pl.BlockSpec(memory_space=pltpu.HBM)
+    args = [
+        pltpu.with_memory_space_constraint(a, pltpu.HBM) if k in hbm else a
+        for k, a in enumerate(args)
+    ]
     return pl.pallas_call(
         kernel,
         out_shape=outs,
@@ -209,58 +210,44 @@
         a.reshape(-1, LANES) for a in (pos_ids, pos_logq, counts, mem_ids, mem_logq, mem_age)
     ]
 
-    p, q = {0: positives}, {0: queries}
-    p[4] = swap(positives, "batch", 4)
-    q[4] = swap(queries, "batch", 4)
-    shards = [mem_items] + [swap(mem_items, "mem", k) for k in (1, 2, 3)]
+    small = (*ints, mem_items)
+    *ints, shard, pack = call(
+        lambda *r: pack_kernel(len(small), *r),
+        [jax.ShapeDtypeStruct(a.shape, a.dtype) for a in small] + [bf16(2 * own_count, depth)],
+        (*small, queries, positives),
+        hbm=range(len(small) + 2),
+        scratch=[
+            pltpu.VMEM(queries.shape, queries.dtype),
+            pltpu.SemaphoreType.DMA((len(small) + 2,)),
+        ],
+    )
+    far = swap(pack, "batch", 4)
+    shards = [shard] + [swap(shard, "mem", k) for k in (1, 2, 3)]
+    near = swap(pack, "batch", 2)
     bias, weight, wcol, mem_bias = call(
         lambda *r: prep_kernel(n_batch, *r),
         [f32(group_rows, group_rows), f32(n_batch, LANES), f32(LANES, LANES), f32(LANES, LANES)],
         ints,
-        hbm=range(len(ints)),
-        scratch=[pltpu.VMEM(a.shape, jnp.int32) for a in ints]
-        + [pltpu.SemaphoreType.DMA((len(ints),))],
         cost_us=3,
     )
     bank, mem_logit, lse = call(
         bank_kernel,
         [bf16(LANES, depth), f32(LANES, LANES), f32(1, LANES)],
-        (queries, *shards, mem_bias),
-        hbm=(0, 1),
-        scratch=[
-            pltpu.VMEM(queries.shape, jnp.bfloat16),
-            pltpu.VMEM(mem_items.shape, jnp.bfloat16),
-            pltpu.SemaphoreType.DMA((2,)),
-        ],
-    )
-    p[6] = swap(p[4], "batch", 2)
-    p[2] = swap(after(positives, lse), "batch", 2)
-    q[6] = swap(q[4], "batch", 2)
-    q[2] = swap(after(queries, lse), "batch", 2)
+        (pack, *shards, mem_bias),
+    )
+    last = swap(after(far, lse), "batch", 2)
     lses = [lse] + [swap(lse, "batch", k) for k in (2, 4, 6)]
     (even,) = call(stack_kernel, [f32(4, LANES)], lses)
     odd = swap(even, "batch", 1)
-    for k in (0, 2, 4, 6):
-        for d in (p, q):
-            d[k + 1] = swap(after(d[k], lse) if k == 0 else d[k], "batch", 1)
-    order = range(n_batch)
+    (early,) = call(stack_kernel, [bf16(6 * own_count, depth)], (pack, near, far))
+    odd_early = swap(early, "batch", 1)
+    odd_last = swap(after(last, *lses), "batch", 1)
     loss, query_grad, positive_grad = call(
         lambda *r: main_kernel(n_batch, *r),
         [f32(1, LANES), f32(own_count, depth), f32(own_count, depth)],
-        (
-            *[p[k] for k in order],
-            *[q[k] for k in order],
-            even,
-            odd,
-            bias,
-            weight,
-            wcol,
-            bank,
-            mem_logit,
-        ),
-        hbm=(0, n_batch),
-        scratch=[pltpu.VMEM((group_rows, depth), jnp.bfloat16)] * 2
-        + [pltpu.SemaphoreType.DMA((2,))],
+        (pack, near, far, last, odd_early, odd_last)
+        + (even, odd, bias, weight, wcol, bank, mem_logit),
+        scratch=[pltpu.VMEM((group_rows, depth), jnp.bfloat16)] * 2,
         cost_us=3,
     )
     return loss.reshape(own_count), query_grad, positive_grad

time: 34.9 us -> 26.5 us (0.76)
  local copies, waits for them, and re-layouts: 4.18 us -> 0 us
  starting transfers between devices: 18.2 us -> 15.6 us
  waiting for transfers between devices: 6.28 us -> 4.33 us
  Pallas kernels: 4.98 us -> 5.63 us
    unnamed x18 -> x0, local copies, waits for them, and re-layouts: 4.18 us -> none
    ppermute x21 -> x12, starting transfers between devices: 18.2 us -> 15.6 us  [swap(): return lax.ppermute(array, axis, [(s, s ^ mask) for s in range(size)])]
    ppermute x21 -> x12, waiting for transfers between devices: 6.28 us -> 4.33 us  [swap(): return lax.ppermute(array, axis, [(s, s ^ mask) for s in range(size)])]
    pallas_call x4 -> x6, Pallas kernels: 4.98 us -> 5.63 us  [call(): pl.pallas_call(kernel, out_shape=outs, in_specs=[in_hbm if k in hbm else...]
  transfers between devices with their start and end apart: 21 -> 12, of which waited for: 5 -> 5; matrix products, arithmetic and copies ran while one was open for 0% -> 0% of each run, Pallas kernels for 5% -> 7%
where the time goes in v3:
time: 26.5 us; the launch traced here: 26.3 us
  starting transfers between devices  15.6 us (59%)
  Pallas kernels  5.63 us (21%)
  waiting for transfers between devices  4.33 us (16%)
  between operations  0.71 us (3%)
    ppermute x12, starting transfers between devices, swap(): return lax.ppermute(array, axis, [(s, s ^ mask) for s in range(size)])  15.6 us
    pallas_call x6, Pallas kernels, call(): pl.pallas_call(kernel, out_shape=outs, in_specs=[in_hbm if k in hbm else...  5.63 us
    ppermute x12, waiting for transfers between devices, swap(): return lax.ppermute(array, axis, [(s, s ^ mask) for s in range(size)])  4.33 us
  transfers between devices with their start and end apart: 12, of which 5 were waited for; matrix products, arithmetic and copies ran while one was open for 0% of the time, Pallas kernels for 7%

profile of v3, /device:TPU:0, one launch (start us, length us, event | category | flops | bytes accessed | tf_op | source)
XLA Modules:
  0.0 26.3 jit_solution(5629848635315893708)
XLA Ops:
  0.6 1.1 %shard_map.112 = (s32[32,128]{1,0:T(8,128)S(1)}, s32[32,128]{1,0:T(8,128)S(1)}, s32[4,128]{1,0:T(4,128)S(1)}, s32[8,128]{1,0:T(8,128)S(1)}, s32[8,128]{1,0:T(8,1...) custom-call(s32[32,128]{1,0:T(8,128)} %bitcast.7, s32[32,128]{1,0:T(8,128)} %bitcast.8, ...), custom_call_target="tpu_custom_call" | custom-call | flops 1000000000 | bytes 3000000 | tf_op jit(solution)/shard_map/pallas_call | solution.py:173
  1.7 4.1 %collective-permute-start.1 = (bf16[256,256]{1,0:T(8,128)(2,1)S(1)}, bf16[256,256]{1,0:T(8,128)(2,1)S(1)}, u32[]{:S(2)}, u32[]{:S(2)}) collective-permute-start(bf16[256,256]{1,0:T(8,128)(2,1)S(1)} %get-tuple-element.23.pack_ref.refs_0_.r_0_), channel_id=1, source_target_pairs={{0,16},{4,20},{8,24},{12,28},{16,0},{20,4},{24,8},{28,12},{1,17},{... | collective-permute-start | bytes 393224 | tf_op jit(solution)/shard_map/ppermute | solution.py:196
  5.8 1.6 %collective-permute-start = (bf16[256,256]{1,0:T(8,128)(2,1)S(1)}, bf16[256,256]{1,0:T(8,128)(2,1)S(1)}, u32[]{:S(2)}, u32[]{:S(2)}) collective-permute-start(bf16[256,256]{1,0:T(8,128)(2,1)S(1)} %get-tuple-element.23.pack_ref.refs_0_.r_0_), channel_id=1, source_target_pairs={{0,8},{4,12},{8,0},{12,4},{16,24},{20,28},{24,16},{28,20},{1,9},{5... | collective-permute-start | bytes 393224 | tf_op jit(solution)/shard_map/ppermute | solution.py:196
  7.4 2.4 %collective-permute-start.4 = (bf16[32,256]{1,0:T(8,128)(2,1)S(1)}, bf16[32,256]{1,0:T(8,128)(2,1)S(1)}, u32[]{:S(2)}, u32[]{:S(2)}) collective-permute-start(bf16[32,256]{1,0:T(8,128)(2,1)S(1)} %get-tuple-element.24.s0), channel_id=1, source_target_pairs={{0,3},{1,2},{2,1},{3,0},{4,7},{5,6},{6,5},{7,4},{8,11},{9,10},{10,... | collective-permute-start | bytes 49160 | tf_op jit(solution)/shard_map/ppermute | solution.py:196
  9.8 0.5 %collective-permute-start.3 = (bf16[32,256]{1,0:T(8,128)(2,1)S(1)}, bf16[32,256]{1,0:T(8,128)(2,1)S(1)}, u32[]{:S(2)}, u32[]{:S(2)}) collective-permute-start(bf16[32,256]{1,0:T(8,128)(2,1)S(1)} %get-tuple-element.24.s0), channel_id=1, source_target_pairs={{0,2},{1,3},{2,0},{3,1},{4,6},{5,7},{6,4},{7,5},{8,10},{9,11},{10,... | collective-permute-start | bytes 49160 | tf_op jit(solution)/shard_map/ppermute | solution.py:196
  10.4 0.5 %collective-permute-start.2 = (bf16[32,256]{1,0:T(8,128)(2,1)S(1)}, bf16[32,256]{1,0:T(8,128)(2,1)S(1)}, u32[]{:S(2)}, u32[]{:S(2)}) collective-permute-start(bf16[32,256]{1,0:T(8,128)(2,1)S(1)} %get-tuple-element.24.s0), channel_id=1, source_target_pairs={{0,1},{1,0},{2,3},{3,2},{4,5},{5,4},{6,7},{7,6},{8,9},{9,8},{10,11... | collective-permute-start | bytes 49160 | tf_op jit(solution)/shard_map/ppermute | solution.py:196
  10.9 1.3 %collective-permute-done.1.refs_2_.r_2_ = bf16[256,256]{1,0:T(8,128)(2,1)S(1)} collective-permute-done((bf16[256,256]{1,0:T(8,128)(2,1)S(1)}, bf16[256,256]{1,0:T(8,128)(2,1)S(1)}, u32[]{:S(2)}, u32[]{:S(2)}) %collective-permute-start.1) | collective-permute-done | bytes 131104 | tf_op jit(solution)/shard_map/ppermute | solution.py:196
  12.2 0.2 collective-permute-done.refs_1_.r_1_
  12.5 0.1 collective-permute-start.6
  12.5 1.6 %shard_map.113 = (f32[1024,1024]{1,0:T(8,128)S(1)}, f32[8,128]{1,0:T(8,128)S(1)}, f32[128,128]{1,0:T(8,128)S(1)}, f32[128,128]{1,0:T(8,128)S(1)}) custom-call(s32[32,128]{1,0:T(8,128)S(1)} %get-tuple-element.25.r_0_, s32[32,128]{1,0:T(8,128)S(1)} %get-tuple-element.26.r_1_, s32[4,128]{1,0:T(4,128)S(1)} %get-tuple-element.27.r_2_, ...), custom_call_target="tpu_custom_call" | custom-call | flops 3000000000 | bytes 9000000 | tf_op jit(solution)/shard_map/pallas_call | solution.py:173
  14.1 0.0 collective-permute-done.4.s3
  14.1 0.0 collective-permute-done.3.s2
  14.2 0.0 collective-permute-done.2.s1
  14.2 0.2 shard_map.114
  14.4 1.5 %collective-permute-start.5 = (bf16[256,256]{1,0:T(8,128)(2,1)S(1)}, bf16[256,256]{1,0:T(8,128)(2,1)S(1)}, u32[]{:S(2)}, u32[]{:S(2)}) collective-permute-start(bf16[256,256]{1,0:T(8,128)(2,1)S(1)} %collective-permute-done.1.refs_2_.r_2_), channel_id=1, source_target_pairs={{0,8},{4,12},{8,0},{12,4},{16,24},{20,28},{24,16},{28,20},{1,9},{5... | collective-permute-start | bytes 393224 | tf_op jit(solution)/shard_map/ppermute | solution.py:196
  15.9 1.9 %collective-permute-start.9 = (f32[1,128]{1,0:T(1,128)S(1)}, f32[1,128]{1,0:T(1,128)S(1)}, u32[]{:S(2)}, u32[]{:S(2)}) collective-permute-start(f32[1,128]{1,0:T(1,128)S(1)} %get-tuple-element.32.refs_0_), channel_id=1, source_target_pairs={{0,24},{4,28},{8,16},{12,20},{16,8},{20,12},{24,0},{28,4},{1,25},{... | collective-permute-start | bytes 1544 | tf_op jit(solution)/shard_map/ppermute | solution.py:196
  17.8 0.5 %collective-permute-start.8 = (f32[1,128]{1,0:T(1,128)S(1)}, f32[1,128]{1,0:T(1,128)S(1)}, u32[]{:S(2)}, u32[]{:S(2)}) collective-permute-start(f32[1,128]{1,0:T(1,128)S(1)} %get-tuple-element.32.refs_0_), channel_id=1, source_target_pairs={{0,16},{4,20},{8,24},{12,28},{16,0},{20,4},{24,8},{28,12},{1,17},{... | collective-permute-start | bytes 1544 | tf_op jit(solution)/shard_map/ppermute | solution.py:196
  18.2 2.0 %collective-permute-start.7 = (f32[1,128]{1,0:T(1,128)S(1)}, f32[1,128]{1,0:T(1,128)S(1)}, u32[]{:S(2)}, u32[]{:S(2)}) collective-permute-start(f32[1,128]{1,0:T(1,128)S(1)} %get-tuple-element.32.refs_0_), channel_id=1, source_target_pairs={{0,8},{4,12},{8,0},{12,4},{16,24},{20,28},{24,16},{28,20},{1,9},{5... | collective-permute-start | bytes 1544 | tf_op jit(solution)/shard_map/ppermute | solution.py:196
  20.3 1.6 %collective-permute-done.9.refs_3_ = f32[1,128]{1,0:T(1,128)S(1)} collective-permute-done((f32[1,128]{1,0:T(1,128)S(1)}, f32[1,128]{1,0:T(1,128)S(1)}, u32[]{:S(2)}, u32[]{:S(2)}) %collective-permute-start.9) | collective-permute-done | bytes 544 | tf_op jit(solution)/shard_map/ppermute | solution.py:196
  21.8 0.4 %collective-permute-done.8.refs_2_ = f32[1,128]{1,0:T(1,128)S(1)} collective-permute-done((f32[1,128]{1,0:T(1,128)S(1)}, f32[1,128]{1,0:T(1,128)S(1)}, u32[]{:S(2)}, u32[]{:S(2)}) %collective-permute-start.8) | collective-permute-done | bytes 544 | tf_op jit(solution)/shard_map/ppermute | solution.py:196
  22.2 0.0 collective-permute-done.7.refs_1_
  22.2 0.0 collective-permute-done.5.r_3_
  22.2 0.0 collective-permute-start.10
  22.2 0.5 %collective-permute-start.11 = (f32[4,128]{1,0:T(4,128)S(1)}, f32[4,128]{1,0:T(4,128)S(1)}, u32[]{:S(2)}, u32[]{:S(2)}) collective-permute-start(f32[4,128]{1,0:T(4,128)S(1)} %shard_map.116.r_6_), channel_id=1, source_target_pairs={{0,4},{4,0},{8,12},{12,8},{16,20},{20,16},{24,28},{28,24},{1,5},{5... | collective-permute-start | bytes 6152 | tf_op jit(solution)/shard_map/ppermute | solution.py:196
  22.7 0.8 %collective-permute-done.11.r_7_ = f32[4,128]{1,0:T(4,128)S(1)} collective-permute-done((f32[4,128]{1,0:T(4,128)S(1)}, f32[4,128]{1,0:T(4,128)S(1)}, u32[]{:S(2)}, u32[]{:S(2)}) %collective-permute-start.11) | collective-permute-done | bytes 2080 | tf_op jit(solution)/shard_map/ppermute | solution.py:196
  23.5 0.0 collective-permute-done.10.r_5_
  23.6 0.0 collective-permute-done.6.r_4_
  23.6 2.7 %shard_map.117 = (f32[1,128]{1,0:T(1,128)}, f32[128,256]{1,0:T(8,128)}, f32[128,256]{1,0:T(8,128)}) custom-call(bf16[256,256]{1,0:T(8,128)(2,1)S(1)} %get-tuple-element.23.pack_ref.refs_0_.r_0_, bf16[256,256]{1,0:T(8,128)(2,1)S(1)} %collective-permute-done.refs_1_.r_1_, bf16[256,256]{1,0:T(8,128)(2,1)S(1)} %collective-permute-done.1.refs_2_.r_2_, ...), custom_call_target="tpu_custom_call" | custom-call | flops 3000000000 | bytes 9000000 | tf_op jit(solution)/shard_map/pallas_call | solution.py:173
  (2 shorter events, 0.0 us)
Async XLA Ops:
  1.7 10.5 %collective-permute-start.1 = (bf16[256,256]{1,0:T(8,128)(2,1)S(1)}, bf16[256,256]{1,0:T(8,128)(2,1)S(1)}, u32[]{:S(2)}, u32[]{:S(2)}) collective-permute-start(bf16[256,256]{1,0:T(8,128)(2,1)S(1)} %get-tuple-element.23.pack_ref.refs_0_.r_0_), channel_id=1, source_target_pairs={{0,16},{4,20},{8,24},{12,28},{16,0},{20,4},{24,8},{28,12},{1,17},{... | collective-permute-start | bytes 393224 | tf_op jit(solution)/shard_map/ppermute | solution.py:196
  5.8 6.6 %collective-permute-start = (bf16[256,256]{1,0:T(8,128)(2,1)S(1)}, bf16[256,256]{1,0:T(8,128)(2,1)S(1)}, u32[]{:S(2)}, u32[]{:S(2)}) collective-permute-start(bf16[256,256]{1,0:T(8,128)(2,1)S(1)} %get-tuple-element.23.pack_ref.refs_0_.r_0_), channel_id=1, source_target_pairs={{0,8},{4,12},{8,0},{12,4},{16,24},{20,28},{24,16},{28,20},{1,9},{5... | collective-permute-start | bytes 393224 | tf_op jit(solution)/shard_map/ppermute | solution.py:196
  7.4 6.7 %collective-permute-start.4 = (bf16[32,256]{1,0:T(8,128)(2,1)S(1)}, bf16[32,256]{1,0:T(8,128)(2,1)S(1)}, u32[]{:S(2)}, u32[]{:S(2)}) collective-permute-start(bf16[32,256]{1,0:T(8,128)(2,1)S(1)} %get-tuple-element.24.s0), channel_id=1, source_target_pairs={{0,3},{1,2},{2,1},{3,0},{4,7},{5,6},{6,5},{7,4},{8,11},{9,10},{10,... | collective-permute-start | bytes 49160 | tf_op jit(solution)/shard_map/ppermute | solution.py:196
  9.8 4.3 %collective-permute-start.3 = (bf16[32,256]{1,0:T(8,128)(2,1)S(1)}, bf16[32,256]{1,0:T(8,128)(2,1)S(1)}, u32[]{:S(2)}, u32[]{:S(2)}) collective-permute-start(bf16[32,256]{1,0:T(8,128)(2,1)S(1)} %get-tuple-element.24.s0), channel_id=1, source_target_pairs={{0,2},{1,3},{2,0},{3,1},{4,6},{5,7},{6,4},{7,5},{8,10},{9,11},{10,... | collective-permute-start | bytes 49160 | tf_op jit(solution)/shard_map/ppermute | solution.py:196
  10.4 3.8 %collective-permute-start.2 = (bf16[32,256]{1,0:T(8,128)(2,1)S(1)}, bf16[32,256]{1,0:T(8,128)(2,1)S(1)}, u32[]{:S(2)}, u32[]{:S(2)}) collective-permute-start(bf16[32,256]{1,0:T(8,128)(2,1)S(1)} %get-tuple-element.24.s0), channel_id=1, source_target_pairs={{0,1},{1,0},{2,3},{3,2},{4,5},{5,4},{6,7},{7,6},{8,9},{9,8},{10,11... | collective-permute-start | bytes 49160 | tf_op jit(solution)/shard_map/ppermute | solution.py:196
  12.5 11.1 %collective-permute-start.6 = (bf16[768,256]{1,0:T(8,128)(2,1)S(1)}, bf16[768,256]{1,0:T(8,128)(2,1)S(1)}, u32[]{:S(2)}, u32[]{:S(2)}) collective-permute-start(bf16[768,256]{1,0:T(8,128)(2,1)S(1)} %shard_map.115), channel_id=1, source_target_pairs={{0,4},{4,0},{8,12},{12,8},{16,20},{20,16},{24,28},{28,24},{1,5},{5... | collective-permute-start | bytes 1179656 | tf_op jit(solution)/shard_map/ppermute | solution.py:196
  14.4 7.8 %collective-permute-start.5 = (bf16[256,256]{1,0:T(8,128)(2,1)S(1)}, bf16[256,256]{1,0:T(8,128)(2,1)S(1)}, u32[]{:S(2)}, u32[]{:S(2)}) collective-permute-start(bf16[256,256]{1,0:T(8,128)(2,1)S(1)} %collective-permute-done.1.refs_2_.r_2_), channel_id=1, source_target_pairs={{0,8},{4,12},{8,0},{12,4},{16,24},{20,28},{24,16},{28,20},{1,9},{5... | collective-permute-start | bytes 393224 | tf_op jit(solution)/shard_map/ppermute | solution.py:196
  15.9 5.9 %collective-permute-start.9 = (f32[1,128]{1,0:T(1,128)S(1)}, f32[1,128]{1,0:T(1,128)S(1)}, u32[]{:S(2)}, u32[]{:S(2)}) collective-permute-start(f32[1,128]{1,0:T(1,128)S(1)} %get-tuple-element.32.refs_0_), channel_id=1, source_target_pairs={{0,24},{4,28},{8,16},{12,20},{16,8},{20,12},{24,0},{28,4},{1,25},{... | collective-permute-start | bytes 1544 | tf_op jit(solution)/shard_map/ppermute | solution.py:196
  17.8 4.4 %collective-permute-start.8 = (f32[1,128]{1,0:T(1,128)S(1)}, f32[1,128]{1,0:T(1,128)S(1)}, u32[]{:S(2)}, u32[]{:S(2)}) collective-permute-start(f32[1,128]{1,0:T(1,128)S(1)} %get-tuple-element.32.refs_0_), channel_id=1, source_target_pairs={{0,16},{4,20},{8,24},{12,28},{16,0},{20,4},{24,8},{28,12},{1,17},{... | collective-permute-start | bytes 1544 | tf_op jit(solution)/shard_map/ppermute | solution.py:196
  18.2 4.0 %collective-permute-start.7 = (f32[1,128]{1,0:T(1,128)S(1)}, f32[1,128]{1,0:T(1,128)S(1)}, u32[]{:S(2)}, u32[]{:S(2)}) collective-permute-start(f32[1,128]{1,0:T(1,128)S(1)} %get-tuple-element.32.refs_0_), channel_id=1, source_target_pairs={{0,8},{4,12},{8,0},{12,4},{16,24},{20,28},{24,16},{28,20},{1,9},{5... | collective-permute-start | bytes 1544 | tf_op jit(solution)/shard_map/ppermute | solution.py:196
  22.2 1.4 %collective-permute-start.10 = (bf16[256,256]{1,0:T(8,128)(2,1)S(1)}, bf16[256,256]{1,0:T(8,128)(2,1)S(1)}, u32[]{:S(2)}, u32[]{:S(2)}) collective-permute-start(bf16[256,256]{1,0:T(8,128)(2,1)S(1)} %collective-permute-done.5.r_3_), channel_id=1, source_target_pairs={{0,4},{4,0},{8,12},{12,8},{16,20},{20,16},{24,28},{28,24},{1,5},{5... | collective-permute-start | bytes 393224 | tf_op jit(solution)/shard_map/ppermute | solution.py:196
  22.2 1.3 %collective-permute-start.11 = (f32[4,128]{1,0:T(4,128)S(1)}, f32[4,128]{1,0:T(4,128)S(1)}, u32[]{:S(2)}, u32[]{:S(2)}) collective-permute-start(f32[4,128]{1,0:T(4,128)S(1)} %shard_map.116.r_6_), channel_id=1, source_target_pairs={{0,4},{4,0},{8,12},{12,8},{16,20},{20,16},{24,28},{28,24},{1,5},{5... | collective-permute-start | bytes 6152 | tf_op jit(solution)/shard_map/ppermute | solution.py:196

commit v4 on v3

--- a/solution.py
+++ b/solution.py
@@ -42,13 +42,14 @@
     q_ref, sems = refs[-2:]
     pack_ref = outs[-1]
     rows = q_ref.shape[0]
-    fetch([*zip(ins[:count], outs[:count]), (ins[count], q_ref), (ins[count + 1], pack_ref.at[pl.ds(rows, rows)])], sems)
+    pairs = [*zip(ins[:count], outs[:count])]
+    pairs += [(ins[count], q_ref), (ins[count + 1], pack_ref.at[pl.ds(rows, rows)])]
+    fetch(pairs, sems)
     pack_ref[:rows, :] = q_ref[...] * jnp.bfloat16(inv_temp)
 
 
 def prep_kernel(
-    n_batch, ids_ref, logq_ref, counts_ref, mem_ids_ref, mem_logq_ref, mem_age_ref,
-    bias_ref, weight_ref, wcol_ref, mem_bias_ref,
+    n_batch, ids_ref, logq_ref, counts_ref, bias_ref, weight_ref, wcol_ref
 ):
     own = lax.axis_index("batch")
     first_block = lax.axis_index("mem") * n_batch
@@ -75,20 +76,14 @@
         weight_ref[k : k + 1, :] = weight
         if k == 0:
             wcol_ref[...] = as_column(weight)
-        rows.append((ids_ref[pl.ds(block, 1), :], start, end))
-    id_col = as_column(mem_ids_ref[pl.ds(own, 1), :])
-    shift_col = as_column(-mem_logq_ref[pl.ds(own, 1), :].astype(jnp.float32) * logq_unit)
-    age_col = as_column(mem_age_ref[pl.ds(own, 1), :])
-    keep = (age_col < AGE_LIMIT) & (id_col != rows[0][0])
-    mem_bias_ref[...] = jnp.where(keep, shift_col, very_low)
+        rows.append((ids_ref[pl.ds(block, 1), :], start))
     for n in range(n_batch):
         block = first_block + jnp.bitwise_xor(own, n)
-        id_col = as_column(ids_ref[pl.ds(block, 1), :])
+        id_col, start_col = as_column(rows[n][0]), as_column(rows[n][1])
         shift_col = as_column(-logq_ref[pl.ds(block, 1), :].astype(jnp.float32) * logq_unit)
-        pos_col = block * LANES + sub
         for k in range(n_batch):
-            id_row, start, end = rows[k]
-            keep = (id_col != id_row) & ((pos_col < start) | (pos_col >= end))
+            id_row, start = rows[k]
+            keep = (id_col != id_row) & (start_col != start)
             if n == k:
                 keep = keep | (sub == lane)
             bias_ref[n * LANES : (n + 1) * LANES, k * LANES : (k + 1) * LANES] = jnp.where(
@@ -96,13 +91,23 @@
             )
 
 
-def bank_kernel(pack_ref, s0, s1, s2, s3, mem_bias_ref, bank_ref, logit_ref, lse_ref):
+def bank_kernel(
+    n_batch, pack_ref, s0, s1, s2, s3, ids_ref, mem_ids_ref, mem_logq_ref, mem_age_ref,
+    bank_ref, logit_ref, lse_ref,
+):
+    own = lax.axis_index("batch")
     group = lax.axis_index("mem")
     slots = s0.shape[0]
     for k, shard in enumerate((s0, s1, s2, s3)):
         at = pl.multiple_of(jnp.bitwise_xor(group, k) * slots, slots)
         bank_ref[pl.ds(at, slots), :] = shard[...]
-    logit = nt_dot(bank_ref[...], pack_ref[:LANES, :]) + mem_bias_ref[...]
+    id_row = ids_ref[pl.ds(group * n_batch + own, 1), :]
+    id_col = as_column(mem_ids_ref[pl.ds(own, 1), :])
+    shift_col = as_column(-mem_logq_ref[pl.ds(own, 1), :].astype(jnp.float32) * logq_unit)
+    age_col = as_column(mem_age_ref[pl.ds(own, 1), :])
+    keep = (age_col < AGE_LIMIT) & (id_col != id_row)
+    bias = jnp.where(keep, shift_col, very_low)
+    logit = nt_dot(bank_ref[...], pack_ref[:LANES, :]) + bias
     top = jnp.max(logit, axis=0, keepdims=True)
     total = jnp.sum(jnp.exp(logit - top), axis=0, keepdims=True)
     logit_ref[...] = logit
@@ -222,26 +227,27 @@
         ],
     )
     far = swap(pack, "batch", 4)
+    near = swap(pack, "batch", 2)
     shards = [shard] + [swap(shard, "mem", k) for k in (1, 2, 3)]
-    near = swap(pack, "batch", 2)
-    bias, weight, wcol, mem_bias = call(
+    bias, weight, wcol = call(
         lambda *r: prep_kernel(n_batch, *r),
-        [f32(group_rows, group_rows), f32(n_batch, LANES), f32(LANES, LANES), f32(LANES, LANES)],
-        ints,
+        [f32(group_rows, group_rows), f32(n_batch, LANES), f32(LANES, LANES)],
+        ints[:3],
         cost_us=3,
     )
     bank, mem_logit, lse = call(
-        bank_kernel,
+        lambda *r: bank_kernel(n_batch, *r),
         [bf16(LANES, depth), f32(LANES, LANES), f32(1, LANES)],
-        (pack, *shards, mem_bias),
-    )
-    last = swap(after(far, lse), "batch", 2)
-    lses = [lse] + [swap(lse, "batch", k) for k in (2, 4, 6)]
-    (even,) = call(stack_kernel, [f32(4, LANES)], lses)
-    odd = swap(even, "batch", 1)
+        (pack, *shards, ints[0], *ints[3:]),
+    )
+    last = swap(far, "batch", 2)
+    (even,) = call(
+        stack_kernel, [f32(4, LANES)], [lse] + [swap(lse, "batch", k) for k in (2, 4, 6)]
+    )
+    odd = swap(after(even, weight), "batch", 1)
     (early,) = call(stack_kernel, [bf16(6 * own_count, depth)], (pack, near, far))
     odd_early = swap(early, "batch", 1)
-    odd_last = swap(after(last, *lses), "batch", 1)
+    odd_last = swap(last, "batch", 1)
     loss, query_grad, positive_grad = call(
         lambda *r: main_kernel(n_batch, *r),
         [f32(1, LANES), f32(own_count, depth), f32(own_count, depth)],

time: 26.5 us -> 24.7 us (0.932)
  starting transfers between devices: 15.6 us -> 14.5 us
  waiting for transfers between devices: 4.33 us -> 3.76 us
    ppermute x12, starting transfers between devices: 15.6 us -> 14.5 us  [swap(): return lax.ppermute(array, axis, [(s, s ^ mask) for s in range(size)])]
    ppermute x12, waiting for transfers between devices: 4.33 us -> 3.76 us  [swap(): return lax.ppermute(array, axis, [(s, s ^ mask) for s in range(size)])]
where the time goes in v4:
time: 24.7 us; the launch traced here: 24.4 us
  starting transfers between devices  14.5 us (59%)
  Pallas kernels  5.45 us (22%)
  waiting for transfers between devices  3.76 us (15%)
  between operations  0.69 us (3%)
    ppermute x12, starting transfers between devices, swap(): return lax.ppermute(array, axis, [(s, s ^ mask) for s in range(size)])  14.5 us
    pallas_call x6, Pallas kernels, call(): pl.pallas_call(kernel, out_shape=outs, in_specs=[in_hbm if k in hbm else...  5.45 us
    ppermute x12, waiting for transfers between devices, swap(): return lax.ppermute(array, axis, [(s, s ^ mask) for s in range(size)])  3.76 us
  transfers between devices with their start and end apart: 12, of which 5 were waited for; matrix products, arithmetic and copies ran while one was open for 0% of the time, Pallas kernels for 7%

profile of v4, /device:TPU:0, one launch (start us, length us, event | category | flops | bytes accessed | tf_op | source)
XLA Modules:
  0.0 24.4 jit_solution(15642291268731764463)
XLA Ops:
  0.6 1.1 %shard_map.112 = (s32[32,128]{1,0:T(8,128)S(1)}, s32[32,128]{1,0:T(8,128)S(1)}, s32[4,128]{1,0:T(4,128)S(1)}, s32[8,128]{1,0:T(8,128)S(1)}, s32[8,128]{1,0:T(8,1...) custom-call(s32[32,128]{1,0:T(8,128)} %bitcast.7, s32[32,128]{1,0:T(8,128)} %bitcast.8, ...), custom_call_target="tpu_custom_call" | custom-call | flops 1000000000 | bytes 3000000 | tf_op jit(solution)/shard_map/pallas_call | solution.py:178
  1.7 4.1 %collective-permute-start.1 = (bf16[256,256]{1,0:T(8,128)(2,1)S(1)}, bf16[256,256]{1,0:T(8,128)(2,1)S(1)}, u32[]{:S(2)}, u32[]{:S(2)}) collective-permute-start(bf16[256,256]{1,0:T(8,128)(2,1)S(1)} %get-tuple-element.21.refs_0_.r_0_), channel_id=1, source_target_pairs={{0,16},{4,20},{8,24},{12,28},{16,0},{20,4},{24,8},{28,12},{1,17},{... | collective-permute-start | bytes 393224 | tf_op jit(solution)/shard_map/ppermute | solution.py:201
  5.8 1.6 %collective-permute-start = (bf16[256,256]{1,0:T(8,128)(2,1)S(1)}, bf16[256,256]{1,0:T(8,128)(2,1)S(1)}, u32[]{:S(2)}, u32[]{:S(2)}) collective-permute-start(bf16[256,256]{1,0:T(8,128)(2,1)S(1)} %get-tuple-element.21.refs_0_.r_0_), channel_id=1, source_target_pairs={{0,8},{4,12},{8,0},{12,4},{16,24},{20,28},{24,16},{28,20},{1,9},{5... | collective-permute-start | bytes 393224 | tf_op jit(solution)/shard_map/ppermute | solution.py:201
  7.4 2.4 %collective-permute-start.7 = (bf16[32,256]{1,0:T(8,128)(2,1)S(1)}, bf16[32,256]{1,0:T(8,128)(2,1)S(1)}, u32[]{:S(2)}, u32[]{:S(2)}) collective-permute-start(bf16[32,256]{1,0:T(8,128)(2,1)S(1)} %get-tuple-element.22.r_1_), channel_id=1, source_target_pairs={{0,3},{1,2},{2,1},{3,0},{4,7},{5,6},{6,5},{7,4},{8,11},{9,10},{10,... | collective-permute-start | bytes 49160 | tf_op jit(solution)/shard_map/ppermute | solution.py:201
  9.8 0.5 %collective-permute-start.6 = (bf16[32,256]{1,0:T(8,128)(2,1)S(1)}, bf16[32,256]{1,0:T(8,128)(2,1)S(1)}, u32[]{:S(2)}, u32[]{:S(2)}) collective-permute-start(bf16[32,256]{1,0:T(8,128)(2,1)S(1)} %get-tuple-element.22.r_1_), channel_id=1, source_target_pairs={{0,2},{1,3},{2,0},{3,1},{4,6},{5,7},{6,4},{7,5},{8,10},{9,11},{10,... | collective-permute-start | bytes 49160 | tf_op jit(solution)/shard_map/ppermute | solution.py:201
  10.4 0.5 %collective-permute-start.5 = (bf16[32,256]{1,0:T(8,128)(2,1)S(1)}, bf16[32,256]{1,0:T(8,128)(2,1)S(1)}, u32[]{:S(2)}, u32[]{:S(2)}) collective-permute-start(bf16[32,256]{1,0:T(8,128)(2,1)S(1)} %get-tuple-element.22.r_1_), channel_id=1, source_target_pairs={{0,1},{1,0},{2,3},{3,2},{4,5},{5,4},{6,7},{7,6},{8,9},{9,8},{10,11... | collective-permute-start | bytes 49160 | tf_op jit(solution)/shard_map/ppermute | solution.py:201
  10.9 1.3 %collective-permute-done.1.refs_2_.r_2_ = bf16[256,256]{1,0:T(8,128)(2,1)S(1)} collective-permute-done((bf16[256,256]{1,0:T(8,128)(2,1)S(1)}, bf16[256,256]{1,0:T(8,128)(2,1)S(1)}, u32[]{:S(2)}, u32[]{:S(2)}) %collective-permute-start.1) | collective-permute-done | bytes 131104 | tf_op jit(solution)/shard_map/ppermute | solution.py:201
  12.2 0.6 %collective-permute-start.2 = (bf16[256,256]{1,0:T(8,128)(2,1)S(1)}, bf16[256,256]{1,0:T(8,128)(2,1)S(1)}, u32[]{:S(2)}, u32[]{:S(2)}) collective-permute-start(bf16[256,256]{1,0:T(8,128)(2,1)S(1)} %collective-permute-done.1.refs_2_.r_2_), channel_id=1, source_target_pairs={{0,8},{4,12},{8,0},{12,4},{16,24},{20,28},{24,16},{28,20},{1,9},{5... | collective-permute-start | bytes 393224 | tf_op jit(solution)/shard_map/ppermute | solution.py:201
  12.8 0.0 collective-permute-done.refs_1_.r_1_
  12.9 0.1 collective-permute-start.3
  13.0 0.0 collective-permute-done.7.r_4_
  13.0 0.6 %collective-permute-done.6.r_3_ = bf16[32,256]{1,0:T(8,128)(2,1)S(1)} collective-permute-done((bf16[32,256]{1,0:T(8,128)(2,1)S(1)}, bf16[32,256]{1,0:T(8,128)(2,1)S(1)}, u32[]{:S(2)}, u32[]{:S(2)}) %collective-permute-start.6) | collective-permute-done | bytes 16416 | tf_op jit(solution)/shard_map/ppermute | solution.py:201
  13.6 0.5 %collective-permute-done.5.r_2_ = bf16[32,256]{1,0:T(8,128)(2,1)S(1)} collective-permute-done((bf16[32,256]{1,0:T(8,128)(2,1)S(1)}, bf16[32,256]{1,0:T(8,128)(2,1)S(1)}, u32[]{:S(2)}, u32[]{:S(2)}) %collective-permute-start.5) | collective-permute-done | bytes 16416 | tf_op jit(solution)/shard_map/ppermute | solution.py:201
  14.1 0.2 shard_map.114
  14.3 1.8 %collective-permute-start.10 = (f32[1,128]{1,0:T(1,128)S(1)}, f32[1,128]{1,0:T(1,128)S(1)}, u32[]{:S(2)}, u32[]{:S(2)}) collective-permute-start(f32[1,128]{1,0:T(1,128)S(1)} %get-tuple-element.27.refs_0_), channel_id=1, source_target_pairs={{0,24},{4,28},{8,16},{12,20},{16,8},{20,12},{24,0},{28,4},{1,25},{... | collective-permute-start | bytes 1544 | tf_op jit(solution)/shard_map/ppermute | solution.py:201
  16.1 0.6 %collective-permute-start.9 = (f32[1,128]{1,0:T(1,128)S(1)}, f32[1,128]{1,0:T(1,128)S(1)}, u32[]{:S(2)}, u32[]{:S(2)}) collective-permute-start(f32[1,128]{1,0:T(1,128)S(1)} %get-tuple-element.27.refs_0_), channel_id=1, source_target_pairs={{0,16},{4,20},{8,24},{12,28},{16,0},{20,4},{24,8},{28,12},{1,17},{... | collective-permute-start | bytes 1544 | tf_op jit(solution)/shard_map/ppermute | solution.py:201
  16.7 2.0 %collective-permute-start.8 = (f32[1,128]{1,0:T(1,128)S(1)}, f32[1,128]{1,0:T(1,128)S(1)}, u32[]{:S(2)}, u32[]{:S(2)}) collective-permute-start(f32[1,128]{1,0:T(1,128)S(1)} %get-tuple-element.27.refs_0_), channel_id=1, source_target_pairs={{0,8},{4,12},{8,0},{12,4},{16,24},{20,28},{24,16},{28,20},{1,9},{5... | collective-permute-start | bytes 1544 | tf_op jit(solution)/shard_map/ppermute | solution.py:201
  18.8 0.0 collective-permute-done.2.r_3_
  18.8 0.0 collective-permute-start.4
  18.8 1.4 %shard_map.116 = (f32[1024,1024]{1,0:T(8,128)S(1)}, f32[8,128]{1,0:T(8,128)S(1)}, f32[128,128]{1,0:T(8,128)S(1)}) custom-call(s32[32,128]{1,0:T(8,128)S(1)} %get-tuple-element.23.r_5_.r_0_, s32[32,128]{1,0:T(8,128)S(1)} %get-tuple-element.28.r_1_, s32[4,128]{1,0:T(4,128)S(1)} %get-tuple-element.29.r_2_), custom_call_target="tpu_custom_call" | custom-call | flops 3000000000 | bytes 9000000 | tf_op jit(solution)/shard_map/pallas_call | solution.py:178
  20.2 0.0 collective-permute-done.10.refs_3_
  20.2 0.4 %collective-permute-done.9.refs_2_ = f32[1,128]{1,0:T(1,128)S(1)} collective-permute-done((f32[1,128]{1,0:T(1,128)S(1)}, f32[1,128]{1,0:T(1,128)S(1)}, u32[]{:S(2)}, u32[]{:S(2)}) %collective-permute-start.9) | collective-permute-done | bytes 544 | tf_op jit(solution)/shard_map/ppermute | solution.py:201
  20.5 0.0 collective-permute-done.8.refs_1_
  20.5 0.2 collective-permute-start.11
  20.8 0.9 %collective-permute-done.11.r_7_ = f32[4,128]{1,0:T(4,128)S(1)} collective-permute-done((f32[4,128]{1,0:T(4,128)S(1)}, f32[4,128]{1,0:T(4,128)S(1)}, u32[]{:S(2)}, u32[]{:S(2)}) %collective-permute-start.11) | collective-permute-done | bytes 2080 | tf_op jit(solution)/shard_map/ppermute | solution.py:201
  21.7 0.0 collective-permute-done.4.r_5_
  21.7 0.0 collective-permute-done.3.r_4_
  21.7 2.7 %shard_map.117 = (f32[1,128]{1,0:T(1,128)}, f32[128,256]{1,0:T(8,128)}, f32[128,256]{1,0:T(8,128)}) custom-call(bf16[256,256]{1,0:T(8,128)(2,1)S(1)} %get-tuple-element.21.refs_0_.r_0_, bf16[256,256]{1,0:T(8,128)(2,1)S(1)} %collective-permute-done.refs_1_.r_1_, bf16[256,256]{1,0:T(8,128)(2,1)S(1)} %collective-permute-done.1.refs_2_.r_2_, ...), custom_call_target="tpu_custom_call" | custom-call | flops 3000000000 | bytes 9000000 | tf_op jit(solution)/shard_map/pallas_call | solution.py:178
  (2 shorter events, 0.0 us)
Async XLA Ops:
  1.7 10.5 %collective-permute-start.1 = (bf16[256,256]{1,0:T(8,128)(2,1)S(1)}, bf16[256,256]{1,0:T(8,128)(2,1)S(1)}, u32[]{:S(2)}, u32[]{:S(2)}) collective-permute-start(bf16[256,256]{1,0:T(8,128)(2,1)S(1)} %get-tuple-element.21.refs_0_.r_0_), channel_id=1, source_target_pairs={{0,16},{4,20},{8,24},{12,28},{16,0},{20,4},{24,8},{28,12},{1,17},{... | collective-permute-start | bytes 393224 | tf_op jit(solution)/shard_map/ppermute | solution.py:201
  5.8 7.0 %collective-permute-start = (bf16[256,256]{1,0:T(8,128)(2,1)S(1)}, bf16[256,256]{1,0:T(8,128)(2,1)S(1)}, u32[]{:S(2)}, u32[]{:S(2)}) collective-permute-start(bf16[256,256]{1,0:T(8,128)(2,1)S(1)} %get-tuple-element.21.refs_0_.r_0_), channel_id=1, source_target_pairs={{0,8},{4,12},{8,0},{12,4},{16,24},{20,28},{24,16},{28,20},{1,9},{5... | collective-permute-start | bytes 393224 | tf_op jit(solution)/shard_map/ppermute | solution.py:201
  7.4 5.6 %collective-permute-start.7 = (bf16[32,256]{1,0:T(8,128)(2,1)S(1)}, bf16[32,256]{1,0:T(8,128)(2,1)S(1)}, u32[]{:S(2)}, u32[]{:S(2)}) collective-permute-start(bf16[32,256]{1,0:T(8,128)(2,1)S(1)} %get-tuple-element.22.r_1_), channel_id=1, source_target_pairs={{0,3},{1,2},{2,1},{3,0},{4,7},{5,6},{6,5},{7,4},{8,11},{9,10},{10,... | collective-permute-start | bytes 49160 | tf_op jit(solution)/shard_map/ppermute | solution.py:201
  9.8 3.7 %collective-permute-start.6 = (bf16[32,256]{1,0:T(8,128)(2,1)S(1)}, bf16[32,256]{1,0:T(8,128)(2,1)S(1)}, u32[]{:S(2)}, u32[]{:S(2)}) collective-permute-start(bf16[32,256]{1,0:T(8,128)(2,1)S(1)} %get-tuple-element.22.r_1_), channel_id=1, source_target_pairs={{0,2},{1,3},{2,0},{3,1},{4,6},{5,7},{6,4},{7,5},{8,10},{9,11},{10,... | collective-permute-start | bytes 49160 | tf_op jit(solution)/shard_map/ppermute | solution.py:201
  10.4 3.7 %collective-permute-start.5 = (bf16[32,256]{1,0:T(8,128)(2,1)S(1)}, bf16[32,256]{1,0:T(8,128)(2,1)S(1)}, u32[]{:S(2)}, u32[]{:S(2)}) collective-permute-start(bf16[32,256]{1,0:T(8,128)(2,1)S(1)} %get-tuple-element.22.r_1_), channel_id=1, source_target_pairs={{0,1},{1,0},{2,3},{3,2},{4,5},{5,4},{6,7},{7,6},{8,9},{9,8},{10,11... | collective-permute-start | bytes 49160 | tf_op jit(solution)/shard_map/ppermute | solution.py:201
  12.2 6.5 %collective-permute-start.2 = (bf16[256,256]{1,0:T(8,128)(2,1)S(1)}, bf16[256,256]{1,0:T(8,128)(2,1)S(1)}, u32[]{:S(2)}, u32[]{:S(2)}) collective-permute-start(bf16[256,256]{1,0:T(8,128)(2,1)S(1)} %collective-permute-done.1.refs_2_.r_2_), channel_id=1, source_target_pairs={{0,8},{4,12},{8,0},{12,4},{16,24},{20,28},{24,16},{28,20},{1,9},{5... | collective-permute-start | bytes 393224 | tf_op jit(solution)/shard_map/ppermute | solution.py:201
  12.9 8.8 %collective-permute-start.3 = (bf16[768,256]{1,0:T(8,128)(2,1)S(1)}, bf16[768,256]{1,0:T(8,128)(2,1)S(1)}, u32[]{:S(2)}, u32[]{:S(2)}) collective-permute-start(bf16[768,256]{1,0:T(8,128)(2,1)S(1)} %shard_map.113), channel_id=1, source_target_pairs={{0,4},{4,0},{8,12},{12,8},{16,20},{20,16},{24,28},{28,24},{1,5},{5... | collective-permute-start | bytes 1179656 | tf_op jit(solution)/shard_map/ppermute | solution.py:201
  14.3 5.9 %collective-permute-start.10 = (f32[1,128]{1,0:T(1,128)S(1)}, f32[1,128]{1,0:T(1,128)S(1)}, u32[]{:S(2)}, u32[]{:S(2)}) collective-permute-start(f32[1,128]{1,0:T(1,128)S(1)} %get-tuple-element.27.refs_0_), channel_id=1, source_target_pairs={{0,24},{4,28},{8,16},{12,20},{16,8},{20,12},{24,0},{28,4},{1,25},{... | collective-permute-start | bytes 1544 | tf_op jit(solution)/shard_map/ppermute | solution.py:201
  16.1 4.4 %collective-permute-start.9 = (f32[1,128]{1,0:T(1,128)S(1)}, f32[1,128]{1,0:T(1,128)S(1)}, u32[]{:S(2)}, u32[]{:S(2)}) collective-permute-start(f32[1,128]{1,0:T(1,128)S(1)} %get-tuple-element.27.refs_0_), channel_id=1, source_target_pairs={{0,16},{4,20},{8,24},{12,28},{16,0},{20,4},{24,8},{28,12},{1,17},{... | collective-permute-start | bytes 1544 | tf_op jit(solution)/shard_map/ppermute | solution.py:201
  16.7 3.8 %collective-permute-start.8 = (f32[1,128]{1,0:T(1,128)S(1)}, f32[1,128]{1,0:T(1,128)S(1)}, u32[]{:S(2)}, u32[]{:S(2)}) collective-permute-start(f32[1,128]{1,0:T(1,128)S(1)} %get-tuple-element.27.refs_0_), channel_id=1, source_target_pairs={{0,8},{4,12},{8,0},{12,4},{16,24},{20,28},{24,16},{28,20},{1,9},{5... | collective-permute-start | bytes 1544 | tf_op jit(solution)/shard_map/ppermute | solution.py:201
  18.8 2.9 %collective-permute-start.4 = (bf16[256,256]{1,0:T(8,128)(2,1)S(1)}, bf16[256,256]{1,0:T(8,128)(2,1)S(1)}, u32[]{:S(2)}, u32[]{:S(2)}) collective-permute-start(bf16[256,256]{1,0:T(8,128)(2,1)S(1)} %collective-permute-done.2.r_3_), channel_id=1, source_target_pairs={{0,4},{4,0},{8,12},{12,8},{16,20},{20,16},{24,28},{28,24},{1,5},{5... | collective-permute-start | bytes 393224 | tf_op jit(solution)/shard_map/ppermute | solution.py:201
  20.5 1.2 %collective-permute-start.11 = (f32[4,128]{1,0:T(4,128)S(1)}, f32[4,128]{1,0:T(4,128)S(1)}, u32[]{:S(2)}, u32[]{:S(2)}) collective-permute-start(f32[4,128]{1,0:T(4,128)S(1)} %shard_map.115.r_6_), channel_id=1, source_target_pairs={{0,4},{4,0},{8,12},{12,8},{16,20},{20,16},{24,28},{28,24},{1,5},{5... | collective-permute-start | bytes 6152 | tf_op jit(solution)/shard_map/ppermute | solution.py:201

commit v5 on v4

--- a/solution.py
+++ b/solution.py
@@ -11,6 +11,8 @@
 very_low = -1e30
 LANES = 128
 VMEM_LIMIT = 32 * 1024 * 1024
+BANK_ORDER = (3, 1, 2)
+SUM_ORDER = (6, 4, 2)
 
 
 def nt_dot(left_mat, right_mat):
@@ -92,13 +94,13 @@
 
 
 def bank_kernel(
-    n_batch, pack_ref, s0, s1, s2, s3, ids_ref, mem_ids_ref, mem_logq_ref, mem_age_ref,
+    n_batch, order, pack_ref, s0, s1, s2, s3, ids_ref, mem_ids_ref, mem_logq_ref, mem_age_ref,
     bank_ref, logit_ref, lse_ref,
 ):
     own = lax.axis_index("batch")
     group = lax.axis_index("mem")
     slots = s0.shape[0]
-    for k, shard in enumerate((s0, s1, s2, s3)):
+    for k, shard in zip((0, *order), (s0, s1, s2, s3)):
         at = pl.multiple_of(jnp.bitwise_xor(group, k) * slots, slots)
         bank_ref[pl.ds(at, slots), :] = shard[...]
     id_row = ids_ref[pl.ds(group * n_batch + own, 1), :]
@@ -114,6 +116,11 @@
     lse_ref[...] = top + jnp.log(total)
 
 
+def order_kernel(order, *refs):
+    for k, ref in zip(order, refs[:-1]):
+        refs[-1][k // 2 : k // 2 + 1, :] = ref[...]
+
+
 def stack_kernel(*refs):
     first = 0
     for ref in refs[:-1]:
@@ -121,12 +128,11 @@
         first += ref.shape[0]
 
 
-def main_kernel(n_batch, *refs):
+def stats_kernel(n_batch, *refs):
     evens = refs[: n_batch // 2]
-    odd_ref, odd_last_ref = refs[n_batch // 2 : n_batch // 2 + 2]
-    rest = refs[n_batch // 2 + 2 :]
-    even_ref, odd_lse_ref, bias_ref, weight_ref, wcol_ref, bank_ref, mem_logit_ref = rest[:7]
-    loss_ref, qgrad_ref, pgrad_ref, items, queries = rest[7:]
+    odd_ref, odd_last_ref, bias_ref, queries, items, own_ref, row_ref, top_ref, total_ref = refs[
+        n_batch // 2 :
+    ]
     block = evens[0].shape[0]
     for k in range(n_batch // 2):
         odd = odd_last_ref if k == n_batch // 2 - 1 else odd_ref.at[pl.ds(k * block, block)]
@@ -135,31 +141,43 @@
             queries[at : at + LANES, :] = ref[:LANES, :]
             items[at : at + LANES, :] = ref[LANES:, :]
     width = 2 * LANES
+    for c in range(n_batch // 2):
+        at = slice(c * width, (c + 1) * width)
+        logit = nt_dot(items[...], queries[at, :]) + bias_ref[:, at]
+        top = jnp.max(logit, axis=0, keepdims=True)
+        top_ref[:, at] = top
+        total_ref[:, at] = jnp.sum(jnp.exp(logit - top), axis=0, keepdims=True)
+        own_ref[:, at] = logit[:LANES]
+        if c == 0:
+            row_ref[...] = logit[:, :LANES]
+
+
+def grad_kernel(
+    n_batch, queries, items, own_ref, row_ref, top_ref, total_ref, even_ref, odd_ref,
+    weight_ref, wcol_ref, bank_ref, mem_logit_ref, loss_ref, qgrad_ref, pgrad_ref,
+):
+    width = 2 * LANES
     pgrad = -wcol_ref[:, :1] * queries[:LANES, :].astype(jnp.float32)
     for c in range(n_batch // 2):
         at = slice(c * width, (c + 1) * width)
-        q_part = queries[at, :]
-        logit = nt_dot(items[...], q_part) + bias_ref[:, at]
-        top = jnp.max(logit, axis=0, keepdims=True)
-        total = jnp.sum(jnp.exp(logit - top), axis=0, keepdims=True)
-        mem_lse = jnp.concatenate([even_ref[c : c + 1, :], odd_lse_ref[c : c + 1, :]], axis=1)
+        top = top_ref[:, at]
+        mem_lse = jnp.concatenate([even_ref[c : c + 1, :], odd_ref[c : c + 1, :]], axis=1)
         weight = jnp.concatenate(
             [weight_ref[2 * c : 2 * c + 1, :], weight_ref[2 * c + 1 : 2 * c + 2, :]], axis=1
         )
         high = jnp.maximum(top, mem_lse)
-        lse = high + jnp.log(total * jnp.exp(top - high) + jnp.exp(mem_lse - high))
-        coef = (weight * jnp.exp(logit[:LANES] - lse)).astype(jnp.bfloat16)
-        pgrad = pgrad + jnp.dot(coef, q_part, preferred_element_type=jnp.float32)
+        lse = high + jnp.log(total_ref[:, at] * jnp.exp(top - high) + jnp.exp(mem_lse - high))
+        coef = (weight * jnp.exp(own_ref[:, at] - lse)).astype(jnp.bfloat16)
+        pgrad = pgrad + jnp.dot(coef, queries[at, :], preferred_element_type=jnp.float32)
         if c == 0:
             own_lse = lse[:, :LANES]
             own_weight = weight[:, :LANES]
-            own = logit[:, :LANES]
             diag = lax.broadcasted_iota(jnp.int32, (LANES, LANES), 0) == (
                 lax.broadcasted_iota(jnp.int32, (LANES, LANES), 1)
             )
-            own_logit = jnp.sum(jnp.where(diag, own[:LANES], 0.0), axis=0, keepdims=True)
+            own_logit = jnp.sum(jnp.where(diag, row_ref[:LANES, :], 0.0), axis=0, keepdims=True)
             loss_ref[...] = own_lse - own_logit
-            row_coef = (own_weight * jnp.exp(own - own_lse)).astype(jnp.bfloat16)
+            row_coef = (own_weight * jnp.exp(row_ref[...] - own_lse)).astype(jnp.bfloat16)
             mem_coef = (own_weight * jnp.exp(mem_logit_ref[...] - own_lse)).astype(jnp.bfloat16)
             qgrad = tn_dot(row_coef, items[...]) + tn_dot(mem_coef, bank_ref[...])
             qgrad_ref[...] = inv_temp * (
@@ -228,7 +246,8 @@
     )
     far = swap(pack, "batch", 4)
     near = swap(pack, "batch", 2)
-    shards = [shard] + [swap(shard, "mem", k) for k in (1, 2, 3)]
+    arrived = {k: swap(shard, "mem", k) for k in BANK_ORDER}
+    shards = [shard] + [arrived[k] for k in BANK_ORDER]
     bias, weight, wcol = call(
         lambda *r: prep_kernel(n_batch, *r),
         [f32(group_rows, group_rows), f32(n_batch, LANES), f32(LANES, LANES)],
@@ -236,25 +255,33 @@
         cost_us=3,
     )
     bank, mem_logit, lse = call(
-        lambda *r: bank_kernel(n_batch, *r),
+        lambda *r: bank_kernel(n_batch, BANK_ORDER, *r),
         [bf16(LANES, depth), f32(LANES, LANES), f32(1, LANES)],
         (pack, *shards, ints[0], *ints[3:]),
     )
     last = swap(far, "batch", 2)
+    sums = {k: swap(lse, "batch", k) for k in SUM_ORDER}
     (even,) = call(
-        stack_kernel, [f32(4, LANES)], [lse] + [swap(lse, "batch", k) for k in (2, 4, 6)]
+        lambda *r: order_kernel((0, *SUM_ORDER), *r),
+        [f32(4, LANES)],
+        [lse] + [sums[k] for k in SUM_ORDER],
     )
     odd = swap(after(even, weight), "batch", 1)
     (early,) = call(stack_kernel, [bf16(6 * own_count, depth)], (pack, near, far))
     odd_early = swap(early, "batch", 1)
     odd_last = swap(last, "batch", 1)
+    stats = call(
+        lambda *r: stats_kernel(n_batch, *r),
+        [bf16(group_rows, depth), bf16(group_rows, depth), f32(own_count, group_rows)]
+        + [f32(group_rows, own_count), f32(1, group_rows), f32(1, group_rows)],
+        (pack, near, far, last, odd_early, odd_last, bias),
+        cost_us=3,
+    )
     loss, query_grad, positive_grad = call(
-        lambda *r: main_kernel(n_batch, *r),
+        lambda *r: grad_kernel(n_batch, *r),
         [f32(1, LANES), f32(own_count, depth), f32(own_count, depth)],
-        (pack, near, far, last, odd_early, odd_last)
-        + (even, odd, bias, weight, wcol, bank, mem_logit),
-        scratch=[pltpu.VMEM((group_rows, depth), jnp.bfloat16)] * 2,
-        cost_us=3,
+        (*stats, even, odd, weight, wcol, bank, mem_logit),
+        cost_us=1,
     )
     return loss.reshape(own_count), query_grad, positive_grad
 

time: 24.7 us -> 23.7 us (0.960)
  waiting for transfers between devices: 3.76 us -> 2.84 us
    ppermute x12, waiting for transfers between devices: 3.76 us -> 2.84 us  [swap(): return lax.ppermute(array, axis, [(s, s ^ mask) for s in range(size)])]
    pallas_call x6 -> x7, Pallas kernels: 5.45 us -> 5.35 us  [call(): pl.pallas_call(kernel, out_shape=outs, in_specs=[in_hbm if k in hbm else...]
  transfers between devices with their start and end apart: 12 -> 12, of which waited for: 5 -> 4; matrix products, arithmetic and copies ran while one was open for 0% -> 0% of each run, Pallas kernels for 7% -> 13%
where the time goes in v5:
time: 23.7 us; the launch traced here: 23.5 us
  starting transfers between devices  14.6 us (62%)
  Pallas kernels  5.35 us (23%)
  waiting for transfers between devices  2.84 us (12%)
  between operations  0.7 us (3%)
    ppermute x12, starting transfers between devices, swap(): return lax.ppermute(array, axis, [(s, s ^ mask) for s in range(size)])  14.6 us
    pallas_call x7, Pallas kernels, call(): pl.pallas_call(kernel, out_shape=outs, in_specs=[in_hbm if k in hbm else...  5.35 us
    ppermute x12, waiting for transfers between devices, swap(): return lax.ppermute(array, axis, [(s, s ^ mask) for s in range(size)])  2.84 us
  transfers between devices with their start and end apart: 12, of which 4 were waited for; matrix products, arithmetic and copies ran while one was open for 0% of the time, Pallas kernels for 13%

profile of v5, /device:TPU:0, one launch (start us, length us, event | category | flops | bytes accessed | tf_op | source)
XLA Modules:
  0.0 23.5 jit_solution(18211193544538845853)
XLA Ops:
  0.6 1.1 %shard_map.112 = (s32[32,128]{1,0:T(8,128)S(1)}, s32[32,128]{1,0:T(8,128)S(1)}, s32[4,128]{1,0:T(4,128)S(1)}, s32[8,128]{1,0:T(8,128)S(1)}, s32[8,128]{1,0:T(8,1...) custom-call(s32[32,128]{1,0:T(8,128)} %bitcast.7, s32[32,128]{1,0:T(8,128)} %bitcast.8, ...), custom_call_target="tpu_custom_call" | custom-call | flops 1000000000 | bytes 3000000 | tf_op jit(solution)/shard_map/pallas_call | solution.py:196
  1.7 4.1 %collective-permute-start.1 = (bf16[256,256]{1,0:T(8,128)(2,1)S(1)}, bf16[256,256]{1,0:T(8,128)(2,1)S(1)}, u32[]{:S(2)}, u32[]{:S(2)}) collective-permute-start(bf16[256,256]{1,0:T(8,128)(2,1)S(1)} %get-tuple-element.27.refs_0_.r_0_), channel_id=1, source_target_pairs={{0,16},{4,20},{8,24},{12,28},{16,0},{20,4},{24,8},{28,12},{1,17},{... | collective-permute-start | bytes 393224 | tf_op jit(solution)/shard_map/ppermute | solution.py:219
  5.8 1.6 %collective-permute-start = (bf16[256,256]{1,0:T(8,128)(2,1)S(1)}, bf16[256,256]{1,0:T(8,128)(2,1)S(1)}, u32[]{:S(2)}, u32[]{:S(2)}) collective-permute-start(bf16[256,256]{1,0:T(8,128)(2,1)S(1)} %get-tuple-element.27.refs_0_.r_0_), channel_id=1, source_target_pairs={{0,8},{4,12},{8,0},{12,4},{16,24},{20,28},{24,16},{28,20},{1,9},{5... | collective-permute-start | bytes 393224 | tf_op jit(solution)/shard_map/ppermute | solution.py:219
  7.4 2.4 %collective-permute-start.5 = (bf16[32,256]{1,0:T(8,128)(2,1)S(1)}, bf16[32,256]{1,0:T(8,128)(2,1)S(1)}, u32[]{:S(2)}, u32[]{:S(2)}) collective-permute-start(bf16[32,256]{1,0:T(8,128)(2,1)S(1)} %get-tuple-element.38.r_1_), channel_id=1, source_target_pairs={{0,3},{1,2},{2,1},{3,0},{4,7},{5,6},{6,5},{7,4},{8,11},{9,10},{10,... | collective-permute-start | bytes 49160 | tf_op jit(solution)/shard_map/ppermute | solution.py:219
  9.8 0.5 %collective-permute-start.6 = (bf16[32,256]{1,0:T(8,128)(2,1)S(1)}, bf16[32,256]{1,0:T(8,128)(2,1)S(1)}, u32[]{:S(2)}, u32[]{:S(2)}) collective-permute-start(bf16[32,256]{1,0:T(8,128)(2,1)S(1)} %get-tuple-element.38.r_1_), channel_id=1, source_target_pairs={{0,1},{1,0},{2,3},{3,2},{4,5},{5,4},{6,7},{7,6},{8,9},{9,8},{10,11... | collective-permute-start | bytes 49160 | tf_op jit(solution)/shard_map/ppermute | solution.py:219
  10.4 0.5 %collective-permute-start.7 = (bf16[32,256]{1,0:T(8,128)(2,1)S(1)}, bf16[32,256]{1,0:T(8,128)(2,1)S(1)}, u32[]{:S(2)}, u32[]{:S(2)}) collective-permute-start(bf16[32,256]{1,0:T(8,128)(2,1)S(1)} %get-tuple-element.38.r_1_), channel_id=1, source_target_pairs={{0,2},{1,3},{2,0},{3,1},{4,6},{5,7},{6,4},{7,5},{8,10},{9,11},{10,... | collective-permute-start | bytes 49160 | tf_op jit(solution)/shard_map/ppermute | solution.py:219
  10.9 1.3 %collective-permute-done.1.refs_2_.r_2_ = bf16[256,256]{1,0:T(8,128)(2,1)S(1)} collective-permute-done((bf16[256,256]{1,0:T(8,128)(2,1)S(1)}, bf16[256,256]{1,0:T(8,128)(2,1)S(1)}, u32[]{:S(2)}, u32[]{:S(2)}) %collective-permute-start.1) | collective-permute-done | bytes 131104 | tf_op jit(solution)/shard_map/ppermute | solution.py:219
  12.2 0.6 %collective-permute-start.2 = (bf16[256,256]{1,0:T(8,128)(2,1)S(1)}, bf16[256,256]{1,0:T(8,128)(2,1)S(1)}, u32[]{:S(2)}, u32[]{:S(2)}) collective-permute-start(bf16[256,256]{1,0:T(8,128)(2,1)S(1)} %collective-permute-done.1.refs_2_.r_2_), channel_id=1, source_target_pairs={{0,8},{4,12},{8,0},{12,4},{16,24},{20,28},{24,16},{28,20},{1,9},{5... | collective-permute-start | bytes 393224 | tf_op jit(solution)/shard_map/ppermute | solution.py:219
  12.8 0.0 collective-permute-done.refs_1_.r_1_
  12.9 0.1 collective-permute-start.3
  13.0 0.0 collective-permute-done.5.r_2_
  13.0 0.6 %collective-permute-done.6.r_3_ = bf16[32,256]{1,0:T(8,128)(2,1)S(1)} collective-permute-done((bf16[32,256]{1,0:T(8,128)(2,1)S(1)}, bf16[32,256]{1,0:T(8,128)(2,1)S(1)}, u32[]{:S(2)}, u32[]{:S(2)}) %collective-permute-start.6) | collective-permute-done | bytes 16416 | tf_op jit(solution)/shard_map/ppermute | solution.py:219
  13.6 0.5 %collective-permute-done.7.r_4_ = bf16[32,256]{1,0:T(8,128)(2,1)S(1)} collective-permute-done((bf16[32,256]{1,0:T(8,128)(2,1)S(1)}, bf16[32,256]{1,0:T(8,128)(2,1)S(1)}, u32[]{:S(2)}, u32[]{:S(2)}) %collective-permute-start.7) | collective-permute-done | bytes 16416 | tf_op jit(solution)/shard_map/ppermute | solution.py:219
  14.1 0.2 shard_map.116
  14.3 1.8 %collective-permute-start.8 = (f32[1,128]{1,0:T(1,128)S(1)}, f32[1,128]{1,0:T(1,128)S(1)}, u32[]{:S(2)}, u32[]{:S(2)}) collective-permute-start(f32[1,128]{1,0:T(1,128)S(1)} %get-tuple-element.42.r_0_), channel_id=1, source_target_pairs={{0,24},{4,28},{8,16},{12,20},{16,8},{20,12},{24,0},{28,4},{1,25},{... | collective-permute-start | bytes 1544 | tf_op jit(solution)/shard_map/ppermute | solution.py:219
  16.1 0.6 %collective-permute-start.9 = (f32[1,128]{1,0:T(1,128)S(1)}, f32[1,128]{1,0:T(1,128)S(1)}, u32[]{:S(2)}, u32[]{:S(2)}) collective-permute-start(f32[1,128]{1,0:T(1,128)S(1)} %get-tuple-element.42.r_0_), channel_id=1, source_target_pairs={{0,16},{4,20},{8,24},{12,28},{16,0},{20,4},{24,8},{28,12},{1,17},{... | collective-permute-start | bytes 1544 | tf_op jit(solution)/shard_map/ppermute | solution.py:219
  16.7 2.1 %collective-permute-start.10 = (f32[1,128]{1,0:T(1,128)S(1)}, f32[1,128]{1,0:T(1,128)S(1)}, u32[]{:S(2)}, u32[]{:S(2)}) collective-permute-start(f32[1,128]{1,0:T(1,128)S(1)} %get-tuple-element.42.r_0_), channel_id=1, source_target_pairs={{0,8},{4,12},{8,0},{12,4},{16,24},{20,28},{24,16},{28,20},{1,9},{5... | collective-permute-start | bytes 1544 | tf_op jit(solution)/shard_map/ppermute | solution.py:219
  18.8 0.0 collective-permute-done.2.r_3_
  18.8 0.0 collective-permute-start.4
  18.8 1.4 %shard_map.114 = (f32[1024,1024]{1,0:T(8,128)S(1)}, f32[8,128]{1,0:T(8,128)S(1)}, f32[128,128]{1,0:T(8,128)S(1)}) custom-call(s32[32,128]{1,0:T(8,128)S(1)} %get-tuple-element.28.r_0_.r_5_, s32[32,128]{1,0:T(8,128)S(1)} %get-tuple-element.29.r_1_, s32[4,128]{1,0:T(4,128)S(1)} %get-tuple-element.30.r_2_), custom_call_target="tpu_custom_call" | custom-call | flops 3000000000 | bytes 9000000 | tf_op jit(solution)/shard_map/pallas_call | solution.py:196
  20.2 0.0 collective-permute-done.8.r_1_
  20.2 0.3 %collective-permute-done.9.r_2_ = f32[1,128]{1,0:T(1,128)S(1)} collective-permute-done((f32[1,128]{1,0:T(1,128)S(1)}, f32[1,128]{1,0:T(1,128)S(1)}, u32[]{:S(2)}, u32[]{:S(2)}) %collective-permute-start.9) | collective-permute-done | bytes 544 | tf_op jit(solution)/shard_map/ppermute | solution.py:219
  20.5 0.0 collective-permute-done.10.r_3_
  20.5 0.3 %collective-permute-start.11 = (f32[4,128]{1,0:T(4,128)S(1)}, f32[4,128]{1,0:T(4,128)S(1)}, u32[]{:S(2)}, u32[]{:S(2)}) collective-permute-start(f32[4,128]{1,0:T(4,128)S(1)} %shard_map.117.r_6_), channel_id=1, source_target_pairs={{0,4},{4,0},{8,12},{12,8},{16,20},{20,16},{24,28},{28,24},{1,5},{5... | collective-permute-start | bytes 6152 | tf_op jit(solution)/shard_map/ppermute | solution.py:219
  20.8 0.0 collective-permute-done.4.r_5_
  20.8 0.0 collective-permute-done.3.r_4_
  20.8 1.5 %shard_map.115 = (bf16[1024,256]{1,0:T(8,128)(2,1)S(1)}, bf16[1024,256]{1,0:T(8,128)(2,1)S(1)}, f32[128,1024]{1,0:T(8,128)S(1)}, f32[1024,128]{1,0:T(8,128)S(1)}...) custom-call(bf16[256,256]{1,0:T(8,128)(2,1)S(1)} %get-tuple-element.27.refs_0_.r_0_, ...), custom_call_target="tpu_custom_call" | custom-call | flops 3000000000 | bytes 9000000 | tf_op jit(solution)/shard_map/pallas_call | solution.py:196
  22.3 0.0 collective-permute-done.11.r_7_
  22.3 1.1 %shard_map.118 = (f32[1,128]{1,0:T(1,128)}, f32[128,256]{1,0:T(8,128)}, f32[128,256]{1,0:T(8,128)}) custom-call(bf16[1024,256]{1,0:T(8,128)(2,1)S(1)} %get-tuple-element.32.r_0_, bf16[1024,256]{1,0:T(8,128)(2,1)S(1)} %get-tuple-element.33.r_1_, f32[128,1024]{1,0:T(8,128)S(1)} %get-tuple-element.34.r_2_, f32[1024,128]{1,0:T(8,128)S(1)} %get-tuple-element.35.r_3_, ...), custom_call_target="tpu_custom_call" | custom-call | flops 1000000000 | bytes 3000000 | tf_op jit(solution)/shard_map/pallas_call | solution.py:196
  (2 shorter events, 0.0 us)
Async XLA Ops:
  1.7 10.5 %collective-permute-start.1 = (bf16[256,256]{1,0:T(8,128)(2,1)S(1)}, bf16[256,256]{1,0:T(8,128)(2,1)S(1)}, u32[]{:S(2)}, u32[]{:S(2)}) collective-permute-start(bf16[256,256]{1,0:T(8,128)(2,1)S(1)} %get-tuple-element.27.refs_0_.r_0_), channel_id=1, source_target_pairs={{0,16},{4,20},{8,24},{12,28},{16,0},{20,4},{24,8},{28,12},{1,17},{... | collective-permute-start | bytes 393224 | tf_op jit(solution)/shard_map/ppermute | solution.py:219
  5.8 7.0 %collective-permute-start = (bf16[256,256]{1,0:T(8,128)(2,1)S(1)}, bf16[256,256]{1,0:T(8,128)(2,1)S(1)}, u32[]{:S(2)}, u32[]{:S(2)}) collective-permute-start(bf16[256,256]{1,0:T(8,128)(2,1)S(1)} %get-tuple-element.27.refs_0_.r_0_), channel_id=1, source_target_pairs={{0,8},{4,12},{8,0},{12,4},{16,24},{20,28},{24,16},{28,20},{1,9},{5... | collective-permute-start | bytes 393224 | tf_op jit(solution)/shard_map/ppermute | solution.py:219
  7.4 5.6 %collective-permute-start.5 = (bf16[32,256]{1,0:T(8,128)(2,1)S(1)}, bf16[32,256]{1,0:T(8,128)(2,1)S(1)}, u32[]{:S(2)}, u32[]{:S(2)}) collective-permute-start(bf16[32,256]{1,0:T(8,128)(2,1)S(1)} %get-tuple-element.38.r_1_), channel_id=1, source_target_pairs={{0,3},{1,2},{2,1},{3,0},{4,7},{5,6},{6,5},{7,4},{8,11},{9,10},{10,... | collective-permute-start | bytes 49160 | tf_op jit(solution)/shard_map/ppermute | solution.py:219
  9.8 3.7 %collective-permute-start.6 = (bf16[32,256]{1,0:T(8,128)(2,1)S(1)}, bf16[32,256]{1,0:T(8,128)(2,1)S(1)}, u32[]{:S(2)}, u32[]{:S(2)}) collective-permute-start(bf16[32,256]{1,0:T(8,128)(2,1)S(1)} %get-tuple-element.38.r_1_), channel_id=1, source_target_pairs={{0,1},{1,0},{2,3},{3,2},{4,5},{5,4},{6,7},{7,6},{8,9},{9,8},{10,11... | collective-permute-start | bytes 49160 | tf_op jit(solution)/shard_map/ppermute | solution.py:219
  10.4 3.7 %collective-permute-start.7 = (bf16[32,256]{1,0:T(8,128)(2,1)S(1)}, bf16[32,256]{1,0:T(8,128)(2,1)S(1)}, u32[]{:S(2)}, u32[]{:S(2)}) collective-permute-start(bf16[32,256]{1,0:T(8,128)(2,1)S(1)} %get-tuple-element.38.r_1_), channel_id=1, source_target_pairs={{0,2},{1,3},{2,0},{3,1},{4,6},{5,7},{6,4},{7,5},{8,10},{9,11},{10,... | collective-permute-start | bytes 49160 | tf_op jit(solution)/shard_map/ppermute | solution.py:219
  12.2 6.6 %collective-permute-start.2 = (bf16[256,256]{1,0:T(8,128)(2,1)S(1)}, bf16[256,256]{1,0:T(8,128)(2,1)S(1)}, u32[]{:S(2)}, u32[]{:S(2)}) collective-permute-start(bf16[256,256]{1,0:T(8,128)(2,1)S(1)} %collective-permute-done.1.refs_2_.r_2_), channel_id=1, source_target_pairs={{0,8},{4,12},{8,0},{12,4},{16,24},{20,28},{24,16},{28,20},{1,9},{5... | collective-permute-start | bytes 393224 | tf_op jit(solution)/shard_map/ppermute | solution.py:219
  12.9 7.9 %collective-permute-start.3 = (bf16[768,256]{1,0:T(8,128)(2,1)S(1)}, bf16[768,256]{1,0:T(8,128)(2,1)S(1)}, u32[]{:S(2)}, u32[]{:S(2)}) collective-permute-start(bf16[768,256]{1,0:T(8,128)(2,1)S(1)} %shard_map.113), channel_id=1, source_target_pairs={{0,4},{4,0},{8,12},{12,8},{16,20},{20,16},{24,28},{28,24},{1,5},{5... | collective-permute-start | bytes 1179656 | tf_op jit(solution)/shard_map/ppermute | solution.py:219
  14.3 5.9 %collective-permute-start.8 = (f32[1,128]{1,0:T(1,128)S(1)}, f32[1,128]{1,0:T(1,128)S(1)}, u32[]{:S(2)}, u32[]{:S(2)}) collective-permute-start(f32[1,128]{1,0:T(1,128)S(1)} %get-tuple-element.42.r_0_), channel_id=1, source_target_pairs={{0,24},{4,28},{8,16},{12,20},{16,8},{20,12},{24,0},{28,4},{1,25},{... | collective-permute-start | bytes 1544 | tf_op jit(solution)/shard_map/ppermute | solution.py:219
  16.1 4.4 %collective-permute-start.9 = (f32[1,128]{1,0:T(1,128)S(1)}, f32[1,128]{1,0:T(1,128)S(1)}, u32[]{:S(2)}, u32[]{:S(2)}) collective-permute-start(f32[1,128]{1,0:T(1,128)S(1)} %get-tuple-element.42.r_0_), channel_id=1, source_target_pairs={{0,16},{4,20},{8,24},{12,28},{16,0},{20,4},{24,8},{28,12},{1,17},{... | collective-permute-start | bytes 1544 | tf_op jit(solution)/shard_map/ppermute | solution.py:219
  16.7 3.8 %collective-permute-start.10 = (f32[1,128]{1,0:T(1,128)S(1)}, f32[1,128]{1,0:T(1,128)S(1)}, u32[]{:S(2)}, u32[]{:S(2)}) collective-permute-start(f32[1,128]{1,0:T(1,128)S(1)} %get-tuple-element.42.r_0_), channel_id=1, source_target_pairs={{0,8},{4,12},{8,0},{12,4},{16,24},{20,28},{24,16},{28,20},{1,9},{5... | collective-permute-start | bytes 1544 | tf_op jit(solution)/shard_map/ppermute | solution.py:219
  18.8 2.0 %collective-permute-start.4 = (bf16[256,256]{1,0:T(8,128)(2,1)S(1)}, bf16[256,256]{1,0:T(8,128)(2,1)S(1)}, u32[]{:S(2)}, u32[]{:S(2)}) collective-permute-start(bf16[256,256]{1,0:T(8,128)(2,1)S(1)} %collective-permute-done.2.r_3_), channel_id=1, source_target_pairs={{0,4},{4,0},{8,12},{12,8},{16,20},{20,16},{24,28},{28,24},{1,5},{5... | collective-permute-start | bytes 393224 | tf_op jit(solution)/shard_map/ppermute | solution.py:219
  20.5 1.8 %collective-permute-start.11 = (f32[4,128]{1,0:T(4,128)S(1)}, f32[4,128]{1,0:T(4,128)S(1)}, u32[]{:S(2)}, u32[]{:S(2)}) collective-permute-start(f32[4,128]{1,0:T(4,128)S(1)} %shard_map.117.r_6_), channel_id=1, source_target_pairs={{0,4},{4,0},{8,12},{12,8},{16,20},{20,16},{24,28},{28,24},{1,5},{5... | collective-permute-start | bytes 6152 | tf_op jit(solution)/shard_map/ppermute | solution.py:219

commit v6 on v5

--- a/solution.py
+++ b/solution.py
@@ -44,8 +44,8 @@
     q_ref, sems = refs[-2:]
     pack_ref = outs[-1]
     rows = q_ref.shape[0]
-    pairs = [*zip(ins[:count], outs[:count])]
-    pairs += [(ins[count], q_ref), (ins[count + 1], pack_ref.at[pl.ds(rows, rows)])]
+    pairs = [(ins[count], q_ref), (ins[count + 1], pack_ref.at[pl.ds(rows, rows)])]
+    pairs += [*zip(ins[:count], outs[:count])]
     fetch(pairs, sems)
     pack_ref[:rows, :] = q_ref[...] * jnp.bfloat16(inv_temp)
 
@@ -64,17 +64,16 @@
         part = counts_ref[c : c + 1, :].astype(jnp.float32)
         tri = jnp.where(lane + c * LANES <= sub, part, 0.0).astype(jnp.bfloat16)
         ends = ends + jnp.dot(tri, ones, preferred_element_type=jnp.float32)
-    ends = ends.astype(jnp.int32)
     sub = sub[:LANES]
     lane = lane[:LANES]
     rows = []
     for k in range(n_batch):
         block = first_block + jnp.bitwise_xor(own, k)
-        pos = block * LANES + lane[:1]
+        pos = (block * LANES + lane[:1]).astype(jnp.float32)
         done = ends <= pos
-        start = jnp.max(jnp.where(done, ends, 0), axis=0, keepdims=True)
-        end = jnp.min(jnp.where(done, jnp.int32(2**30), ends), axis=0, keepdims=True)
-        weight = 1.0 / (end - start).astype(jnp.float32)
+        start = jnp.max(jnp.where(done, ends, 0.0), axis=0, keepdims=True)
+        end = jnp.min(jnp.where(done, -very_low, ends), axis=0, keepdims=True)
+        weight = 1.0 / (end - start)
         weight_ref[k : k + 1, :] = weight
         if k == 0:
             wcol_ref[...] = as_column(weight)
@@ -130,9 +129,8 @@
 
 def stats_kernel(n_batch, *refs):
     evens = refs[: n_batch // 2]
-    odd_ref, odd_last_ref, bias_ref, queries, items, own_ref, row_ref, top_ref, total_ref = refs[
-        n_batch // 2 :
-    ]
+    odd_ref, odd_last_ref, bias_ref = refs[n_batch // 2 : n_batch // 2 + 3]
+    queries, items, own_ref, pull_ref, top_ref, total_ref, diag_ref = refs[n_batch // 2 + 3 :]
     block = evens[0].shape[0]
     for k in range(n_batch // 2):
         odd = odd_last_ref if k == n_batch // 2 - 1 else odd_ref.at[pl.ds(k * block, block)]
@@ -140,50 +138,44 @@
             at = (2 * k + parity) * LANES
             queries[at : at + LANES, :] = ref[:LANES, :]
             items[at : at + LANES, :] = ref[LANES:, :]
-    width = 2 * LANES
-    for c in range(n_batch // 2):
-        at = slice(c * width, (c + 1) * width)
-        logit = nt_dot(items[...], queries[at, :]) + bias_ref[:, at]
-        top = jnp.max(logit, axis=0, keepdims=True)
-        top_ref[:, at] = top
-        total_ref[:, at] = jnp.sum(jnp.exp(logit - top), axis=0, keepdims=True)
-        own_ref[:, at] = logit[:LANES]
-        if c == 0:
-            row_ref[...] = logit[:, :LANES]
+    logit = nt_dot(items[...], queries[...]) + bias_ref[...]
+    top = jnp.max(logit, axis=0, keepdims=True)
+    exps = jnp.exp(logit - top)
+    top_ref[...] = top
+    total_ref[...] = jnp.sum(exps, axis=0, keepdims=True)
+    own_ref[...] = exps[:LANES]
+    pull_ref[...] = tn_dot(exps[:, :LANES].astype(jnp.bfloat16), items[...])
+    diag = lax.broadcasted_iota(jnp.int32, (LANES, LANES), 0) == (
+        lax.broadcasted_iota(jnp.int32, (LANES, LANES), 1)
+    )
+    diag_ref[...] = jnp.sum(
+        jnp.where(diag, logit[:LANES, :LANES], 0.0), axis=0, keepdims=True
+    )
 
 
 def grad_kernel(
-    n_batch, queries, items, own_ref, row_ref, top_ref, total_ref, even_ref, odd_ref,
+    n_batch, queries, items, own_ref, pull_ref, top_ref, total_ref, diag_ref, even_ref, odd_ref,
     weight_ref, wcol_ref, bank_ref, mem_logit_ref, loss_ref, qgrad_ref, pgrad_ref,
 ):
-    width = 2 * LANES
-    pgrad = -wcol_ref[:, :1] * queries[:LANES, :].astype(jnp.float32)
-    for c in range(n_batch // 2):
-        at = slice(c * width, (c + 1) * width)
-        top = top_ref[:, at]
-        mem_lse = jnp.concatenate([even_ref[c : c + 1, :], odd_ref[c : c + 1, :]], axis=1)
-        weight = jnp.concatenate(
-            [weight_ref[2 * c : 2 * c + 1, :], weight_ref[2 * c + 1 : 2 * c + 2, :]], axis=1
-        )
-        high = jnp.maximum(top, mem_lse)
-        lse = high + jnp.log(total_ref[:, at] * jnp.exp(top - high) + jnp.exp(mem_lse - high))
-        coef = (weight * jnp.exp(own_ref[:, at] - lse)).astype(jnp.bfloat16)
-        pgrad = pgrad + jnp.dot(coef, queries[at, :], preferred_element_type=jnp.float32)
-        if c == 0:
-            own_lse = lse[:, :LANES]
-            own_weight = weight[:, :LANES]
-            diag = lax.broadcasted_iota(jnp.int32, (LANES, LANES), 0) == (
-                lax.broadcasted_iota(jnp.int32, (LANES, LANES), 1)
-            )
-            own_logit = jnp.sum(jnp.where(diag, row_ref[:LANES, :], 0.0), axis=0, keepdims=True)
-            loss_ref[...] = own_lse - own_logit
-            row_coef = (own_weight * jnp.exp(row_ref[...] - own_lse)).astype(jnp.bfloat16)
-            mem_coef = (own_weight * jnp.exp(mem_logit_ref[...] - own_lse)).astype(jnp.bfloat16)
-            qgrad = tn_dot(row_coef, items[...]) + tn_dot(mem_coef, bank_ref[...])
-            qgrad_ref[...] = inv_temp * (
-                qgrad - wcol_ref[:, :1] * items[:LANES, :].astype(jnp.float32)
-            )
-    pgrad_ref[...] = pgrad
+    def in_line(even, odd):
+        return [ref[c : c + 1, :] for c in range(n_batch // 2) for ref in (even, odd)]
+
+    mem_lse = jnp.concatenate(in_line(even_ref, odd_ref), axis=1)
+    weight = jnp.concatenate([weight_ref[k : k + 1, :] for k in range(n_batch)], axis=1)
+    top = top_ref[...]
+    high = jnp.maximum(top, mem_lse)
+    below = jnp.exp(top - high)
+    lse = high + jnp.log(total_ref[...] * below + jnp.exp(mem_lse - high))
+    scale = weight * jnp.exp(top - lse)
+    own_lse = lse[:, :LANES]
+    loss_ref[...] = own_lse - diag_ref[...]
+    weight_col = wcol_ref[:, :1]
+    mem_coef = (weight[:, :LANES] * jnp.exp(mem_logit_ref[...] - own_lse)).astype(jnp.bfloat16)
+    pull = as_column(scale[:, :LANES])[:, :1] * pull_ref[...] + tn_dot(mem_coef, bank_ref[...])
+    qgrad_ref[...] = inv_temp * (pull - weight_col * items[:LANES, :].astype(jnp.float32))
+    coef = (own_ref[...] * scale).astype(jnp.bfloat16)
+    pgrad = jnp.dot(coef, queries[...], preferred_element_type=jnp.float32)
+    pgrad_ref[...] = pgrad - weight_col * queries[:LANES, :].astype(jnp.float32)
 
 
 def call(kernel, outs, args, hbm=(), scratch=(), cost_us=1):
@@ -273,7 +265,7 @@
     stats = call(
         lambda *r: stats_kernel(n_batch, *r),
         [bf16(group_rows, depth), bf16(group_rows, depth), f32(own_count, group_rows)]
-        + [f32(group_rows, own_count), f32(1, group_rows), f32(1, group_rows)],
+        + [f32(own_count, depth), f32(1, group_rows), f32(1, group_rows), f32(1, LANES)],
         (pack, near, far, last, odd_early, odd_last, bias),
         cost_us=3,
     )

time: 23.7 us -> 23.2 us (0.979)
  Pallas kernels: 5.35 us -> 4.93 us
    pallas_call x7, Pallas kernels: 5.35 us -> 4.93 us  [call(): pl.pallas_call(kernel, out_shape=outs, in_specs=[in_hbm if k in hbm else...]
where the time goes in v6:
time: 23.2 us; the launch traced here: 23 us
  starting transfers between devices  14.4 us (62%)
  Pallas kernels  4.93 us (21%)
  waiting for transfers between devices  3.02 us (13%)
  between operations  0.7 us (3%)
    ppermute x12, starting transfers between devices, swap(): return lax.ppermute(array, axis, [(s, s ^ mask) for s in range(size)])  14.4 us
    pallas_call x7, Pallas kernels, call(): pl.pallas_call(kernel, out_shape=outs, in_specs=[in_hbm if k in hbm else...  4.93 us
    ppermute x12, waiting for transfers between devices, swap(): return lax.ppermute(array, axis, [(s, s ^ mask) for s in range(size)])  3.02 us
  transfers between devices with their start and end apart: 12, of which 4 were waited for; matrix products, arithmetic and copies ran while one was open for 0% of the time, Pallas kernels for 13%

profile of v6, /device:TPU:0, one launch (start us, length us, event | category | flops | bytes accessed | tf_op | source)
XLA Modules:
  0.0 23.0 jit_solution(1237917190817371636)
XLA Ops:
  0.6 1.0 %shard_map.112 = (s32[32,128]{1,0:T(8,128)S(1)}, s32[32,128]{1,0:T(8,128)S(1)}, s32[4,128]{1,0:T(4,128)S(1)}, s32[8,128]{1,0:T(8,128)S(1)}, s32[8,128]{1,0:T(8,1...) custom-call(s32[32,128]{1,0:T(8,128)} %bitcast.7, s32[32,128]{1,0:T(8,128)} %bitcast.8, ...), custom_call_target="tpu_custom_call" | custom-call | flops 1000000000 | bytes 3000000 | tf_op jit(solution)/shard_map/pallas_call | solution.py:188
  1.6 4.1 %collective-permute-start.1 = (bf16[256,256]{1,0:T(8,128)(2,1)S(1)}, bf16[256,256]{1,0:T(8,128)(2,1)S(1)}, u32[]{:S(2)}, u32[]{:S(2)}) collective-permute-start(bf16[256,256]{1,0:T(8,128)(2,1)S(1)} %get-tuple-element.28.refs_0_.r_0_), channel_id=1, source_target_pairs={{0,16},{4,20},{8,24},{12,28},{16,0},{20,4},{24,8},{28,12},{1,17},{... | collective-permute-start | bytes 393224 | tf_op jit(solution)/shard_map/ppermute | solution.py:211
  5.7 1.6 %collective-permute-start = (bf16[256,256]{1,0:T(8,128)(2,1)S(1)}, bf16[256,256]{1,0:T(8,128)(2,1)S(1)}, u32[]{:S(2)}, u32[]{:S(2)}) collective-permute-start(bf16[256,256]{1,0:T(8,128)(2,1)S(1)} %get-tuple-element.28.refs_0_.r_0_), channel_id=1, source_target_pairs={{0,8},{4,12},{8,0},{12,4},{16,24},{20,28},{24,16},{28,20},{1,9},{5... | collective-permute-start | bytes 393224 | tf_op jit(solution)/shard_map/ppermute | solution.py:211
  7.3 2.4 %collective-permute-start.5 = (bf16[32,256]{1,0:T(8,128)(2,1)S(1)}, bf16[32,256]{1,0:T(8,128)(2,1)S(1)}, u32[]{:S(2)}, u32[]{:S(2)}) collective-permute-start(bf16[32,256]{1,0:T(8,128)(2,1)S(1)} %get-tuple-element.40.r_1_), channel_id=1, source_target_pairs={{0,3},{1,2},{2,1},{3,0},{4,7},{5,6},{6,5},{7,4},{8,11},{9,10},{10,... | collective-permute-start | bytes 49160 | tf_op jit(solution)/shard_map/ppermute | solution.py:211
  9.7 0.5 %collective-permute-start.6 = (bf16[32,256]{1,0:T(8,128)(2,1)S(1)}, bf16[32,256]{1,0:T(8,128)(2,1)S(1)}, u32[]{:S(2)}, u32[]{:S(2)}) collective-permute-start(bf16[32,256]{1,0:T(8,128)(2,1)S(1)} %get-tuple-element.40.r_1_), channel_id=1, source_target_pairs={{0,1},{1,0},{2,3},{3,2},{4,5},{5,4},{6,7},{7,6},{8,9},{9,8},{10,11... | collective-permute-start | bytes 49160 | tf_op jit(solution)/shard_map/ppermute | solution.py:211
  10.3 0.5 %collective-permute-start.7 = (bf16[32,256]{1,0:T(8,128)(2,1)S(1)}, bf16[32,256]{1,0:T(8,128)(2,1)S(1)}, u32[]{:S(2)}, u32[]{:S(2)}) collective-permute-start(bf16[32,256]{1,0:T(8,128)(2,1)S(1)} %get-tuple-element.40.r_1_), channel_id=1, source_target_pairs={{0,2},{1,3},{2,0},{3,1},{4,6},{5,7},{6,4},{7,5},{8,10},{9,11},{10,... | collective-permute-start | bytes 49160 | tf_op jit(solution)/shard_map/ppermute | solution.py:211
  10.8 1.3 %collective-permute-done.1.refs_2_.r_2_ = bf16[256,256]{1,0:T(8,128)(2,1)S(1)} collective-permute-done((bf16[256,256]{1,0:T(8,128)(2,1)S(1)}, bf16[256,256]{1,0:T(8,128)(2,1)S(1)}, u32[]{:S(2)}, u32[]{:S(2)}) %collective-permute-start.1) | collective-permute-done | bytes 131104 | tf_op jit(solution)/shard_map/ppermute | solution.py:211
  12.1 0.6 %collective-permute-start.2 = (bf16[256,256]{1,0:T(8,128)(2,1)S(1)}, bf16[256,256]{1,0:T(8,128)(2,1)S(1)}, u32[]{:S(2)}, u32[]{:S(2)}) collective-permute-start(bf16[256,256]{1,0:T(8,128)(2,1)S(1)} %collective-permute-done.1.refs_2_.r_2_), channel_id=1, source_target_pairs={{0,8},{4,12},{8,0},{12,4},{16,24},{20,28},{24,16},{28,20},{1,9},{5... | collective-permute-start | bytes 393224 | tf_op jit(solution)/shard_map/ppermute | solution.py:211
  12.7 0.0 collective-permute-done.refs_1_.r_1_
  12.8 0.1 collective-permute-start.3
  12.9 0.0 collective-permute-done.5.r_2_
  12.9 0.6 %collective-permute-done.6.r_3_ = bf16[32,256]{1,0:T(8,128)(2,1)S(1)} collective-permute-done((bf16[32,256]{1,0:T(8,128)(2,1)S(1)}, bf16[32,256]{1,0:T(8,128)(2,1)S(1)}, u32[]{:S(2)}, u32[]{:S(2)}) %collective-permute-start.6) | collective-permute-done | bytes 16416 | tf_op jit(solution)/shard_map/ppermute | solution.py:211
  13.5 0.5 %collective-permute-done.7.r_4_ = bf16[32,256]{1,0:T(8,128)(2,1)S(1)} collective-permute-done((bf16[32,256]{1,0:T(8,128)(2,1)S(1)}, bf16[32,256]{1,0:T(8,128)(2,1)S(1)}, u32[]{:S(2)}, u32[]{:S(2)}) %collective-permute-start.7) | collective-permute-done | bytes 16416 | tf_op jit(solution)/shard_map/ppermute | solution.py:211
  14.0 0.2 shard_map.116
  14.2 1.8 %collective-permute-start.8 = (f32[1,128]{1,0:T(1,128)S(1)}, f32[1,128]{1,0:T(1,128)S(1)}, u32[]{:S(2)}, u32[]{:S(2)}) collective-permute-start(f32[1,128]{1,0:T(1,128)S(1)} %get-tuple-element.44.r_0_), channel_id=1, source_target_pairs={{0,24},{4,28},{8,16},{12,20},{16,8},{20,12},{24,0},{28,4},{1,25},{... | collective-permute-start | bytes 1544 | tf_op jit(solution)/shard_map/ppermute | solution.py:211
  16.0 0.6 %collective-permute-start.9 = (f32[1,128]{1,0:T(1,128)S(1)}, f32[1,128]{1,0:T(1,128)S(1)}, u32[]{:S(2)}, u32[]{:S(2)}) collective-permute-start(f32[1,128]{1,0:T(1,128)S(1)} %get-tuple-element.44.r_0_), channel_id=1, source_target_pairs={{0,16},{4,20},{8,24},{12,28},{16,0},{20,4},{24,8},{28,12},{1,17},{... | collective-permute-start | bytes 1544 | tf_op jit(solution)/shard_map/ppermute | solution.py:211
  16.6 2.1 %collective-permute-start.10 = (f32[1,128]{1,0:T(1,128)S(1)}, f32[1,128]{1,0:T(1,128)S(1)}, u32[]{:S(2)}, u32[]{:S(2)}) collective-permute-start(f32[1,128]{1,0:T(1,128)S(1)} %get-tuple-element.44.r_0_), channel_id=1, source_target_pairs={{0,8},{4,12},{8,0},{12,4},{16,24},{20,28},{24,16},{28,20},{1,9},{5... | collective-permute-start | bytes 1544 | tf_op jit(solution)/shard_map/ppermute | solution.py:211
  18.7 0.0 collective-permute-done.2.r_3_
  18.7 0.0 collective-permute-start.4
  18.7 1.2 %shard_map.114 = (f32[1024,1024]{1,0:T(8,128)S(1)}, f32[8,128]{1,0:T(8,128)S(1)}, f32[128,128]{1,0:T(8,128)S(1)}) custom-call(s32[32,128]{1,0:T(8,128)S(1)} %get-tuple-element.29.r_0_.r_5_, s32[32,128]{1,0:T(8,128)S(1)} %get-tuple-element.30.r_1_, s32[4,128]{1,0:T(4,128)S(1)} %get-tuple-element.31.r_2_), custom_call_target="tpu_custom_call" | custom-call | flops 3000000000 | bytes 9000000 | tf_op jit(solution)/shard_map/pallas_call | solution.py:188
  19.9 0.0 collective-permute-done.8.r_1_
  19.9 0.5 %collective-permute-done.9.r_2_ = f32[1,128]{1,0:T(1,128)S(1)} collective-permute-done((f32[1,128]{1,0:T(1,128)S(1)}, f32[1,128]{1,0:T(1,128)S(1)}, u32[]{:S(2)}, u32[]{:S(2)}) %collective-permute-start.9) | collective-permute-done | bytes 544 | tf_op jit(solution)/shard_map/ppermute | solution.py:211
  20.4 0.0 collective-permute-done.10.r_3_
  20.4 0.1 collective-permute-start.11
  20.5 0.0 collective-permute-done.4.r_5_
  20.5 0.0 collective-permute-done.3.r_4_
  20.5 1.5 %shard_map.115 = (bf16[1024,256]{1,0:T(8,128)(2,1)S(1)}, bf16[1024,256]{1,0:T(8,128)(2,1)S(1)}, f32[128,1024]{1,0:T(8,128)S(1)}, f32[128,256]{1,0:T(8,128)S(1)},...) custom-call(bf16[256,256]{1,0:T(8,128)(2,1)S(1)} %get-tuple-element.28.refs_0_.r_0_, ...), custom_call_target="tpu_custom_call" | custom-call | flops 3000000000 | bytes 9000000 | tf_op jit(solution)/shard_map/pallas_call | solution.py:188
  22.1 0.0 collective-permute-done.11.r_8_
  22.1 1.0 %shard_map.118 = (f32[1,128]{1,0:T(1,128)}, f32[128,256]{1,0:T(8,128)}, f32[128,256]{1,0:T(8,128)}) custom-call(bf16[1024,256]{1,0:T(8,128)(2,1)S(1)} %get-tuple-element.33.r_0_, bf16[1024,256]{1,0:T(8,128)(2,1)S(1)} %get-tuple-element.34.r_1_, f32[128,1024]{1,0:T(8,128)S(1)} %get-tuple-element.35.r_2_, f32[128,256]{1,0:T(8,128)S(1)} %get-tuple-element.36.r_3_, ...), custom_call_target="tpu_custom_call" | custom-call | flops 1000000000 | bytes 3000000 | tf_op jit(solution)/shard_map/pallas_call | solution.py:188
  (2 shorter events, 0.0 us)
Async XLA Ops:
  1.6 10.5 %collective-permute-start.1 = (bf16[256,256]{1,0:T(8,128)(2,1)S(1)}, bf16[256,256]{1,0:T(8,128)(2,1)S(1)}, u32[]{:S(2)}, u32[]{:S(2)}) collective-permute-start(bf16[256,256]{1,0:T(8,128)(2,1)S(1)} %get-tuple-element.28.refs_0_.r_0_), channel_id=1, source_target_pairs={{0,16},{4,20},{8,24},{12,28},{16,0},{20,4},{24,8},{28,12},{1,17},{... | collective-permute-start | bytes 393224 | tf_op jit(solution)/shard_map/ppermute | solution.py:211
  5.7 7.0 %collective-permute-start = (bf16[256,256]{1,0:T(8,128)(2,1)S(1)}, bf16[256,256]{1,0:T(8,128)(2,1)S(1)}, u32[]{:S(2)}, u32[]{:S(2)}) collective-permute-start(bf16[256,256]{1,0:T(8,128)(2,1)S(1)} %get-tuple-element.28.refs_0_.r_0_), channel_id=1, source_target_pairs={{0,8},{4,12},{8,0},{12,4},{16,24},{20,28},{24,16},{28,20},{1,9},{5... | collective-permute-start | bytes 393224 | tf_op jit(solution)/shard_map/ppermute | solution.py:211
  7.3 5.6 %collective-permute-start.5 = (bf16[32,256]{1,0:T(8,128)(2,1)S(1)}, bf16[32,256]{1,0:T(8,128)(2,1)S(1)}, u32[]{:S(2)}, u32[]{:S(2)}) collective-permute-start(bf16[32,256]{1,0:T(8,128)(2,1)S(1)} %get-tuple-element.40.r_1_), channel_id=1, source_target_pairs={{0,3},{1,2},{2,1},{3,0},{4,7},{5,6},{6,5},{7,4},{8,11},{9,10},{10,... | collective-permute-start | bytes 49160 | tf_op jit(solution)/shard_map/ppermute | solution.py:211
  9.7 3.7 %collective-permute-start.6 = (bf16[32,256]{1,0:T(8,128)(2,1)S(1)}, bf16[32,256]{1,0:T(8,128)(2,1)S(1)}, u32[]{:S(2)}, u32[]{:S(2)}) collective-permute-start(bf16[32,256]{1,0:T(8,128)(2,1)S(1)} %get-tuple-element.40.r_1_), channel_id=1, source_target_pairs={{0,1},{1,0},{2,3},{3,2},{4,5},{5,4},{6,7},{7,6},{8,9},{9,8},{10,11... | collective-permute-start | bytes 49160 | tf_op jit(solution)/shard_map/ppermute | solution.py:211
  10.3 3.7 %collective-permute-start.7 = (bf16[32,256]{1,0:T(8,128)(2,1)S(1)}, bf16[32,256]{1,0:T(8,128)(2,1)S(1)}, u32[]{:S(2)}, u32[]{:S(2)}) collective-permute-start(bf16[32,256]{1,0:T(8,128)(2,1)S(1)} %get-tuple-element.40.r_1_), channel_id=1, source_target_pairs={{0,2},{1,3},{2,0},{3,1},{4,6},{5,7},{6,4},{7,5},{8,10},{9,11},{10,... | collective-permute-start | bytes 49160 | tf_op jit(solution)/shard_map/ppermute | solution.py:211
  12.1 6.6 %collective-permute-start.2 = (bf16[256,256]{1,0:T(8,128)(2,1)S(1)}, bf16[256,256]{1,0:T(8,128)(2,1)S(1)}, u32[]{:S(2)}, u32[]{:S(2)}) collective-permute-start(bf16[256,256]{1,0:T(8,128)(2,1)S(1)} %collective-permute-done.1.refs_2_.r_2_), channel_id=1, source_target_pairs={{0,8},{4,12},{8,0},{12,4},{16,24},{20,28},{24,16},{28,20},{1,9},{5... | collective-permute-start | bytes 393224 | tf_op jit(solution)/shard_map/ppermute | solution.py:211
  12.8 7.8 %collective-permute-start.3 = (bf16[768,256]{1,0:T(8,128)(2,1)S(1)}, bf16[768,256]{1,0:T(8,128)(2,1)S(1)}, u32[]{:S(2)}, u32[]{:S(2)}) collective-permute-start(bf16[768,256]{1,0:T(8,128)(2,1)S(1)} %shard_map.113), channel_id=1, source_target_pairs={{0,4},{4,0},{8,12},{12,8},{16,20},{20,16},{24,28},{28,24},{1,5},{5... | collective-permute-start | bytes 1179656 | tf_op jit(solution)/shard_map/ppermute | solution.py:211
  14.2 5.7 %collective-permute-start.8 = (f32[1,128]{1,0:T(1,128)S(1)}, f32[1,128]{1,0:T(1,128)S(1)}, u32[]{:S(2)}, u32[]{:S(2)}) collective-permute-start(f32[1,128]{1,0:T(1,128)S(1)} %get-tuple-element.44.r_0_), channel_id=1, source_target_pairs={{0,24},{4,28},{8,16},{12,20},{16,8},{20,12},{24,0},{28,4},{1,25},{... | collective-permute-start | bytes 1544 | tf_op jit(solution)/shard_map/ppermute | solution.py:211
  16.0 4.4 %collective-permute-start.9 = (f32[1,128]{1,0:T(1,128)S(1)}, f32[1,128]{1,0:T(1,128)S(1)}, u32[]{:S(2)}, u32[]{:S(2)}) collective-permute-start(f32[1,128]{1,0:T(1,128)S(1)} %get-tuple-element.44.r_0_), channel_id=1, source_target_pairs={{0,16},{4,20},{8,24},{12,28},{16,0},{20,4},{24,8},{28,12},{1,17},{... | collective-permute-start | bytes 1544 | tf_op jit(solution)/shard_map/ppermute | solution.py:211
  16.6 3.8 %collective-permute-start.10 = (f32[1,128]{1,0:T(1,128)S(1)}, f32[1,128]{1,0:T(1,128)S(1)}, u32[]{:S(2)}, u32[]{:S(2)}) collective-permute-start(f32[1,128]{1,0:T(1,128)S(1)} %get-tuple-element.44.r_0_), channel_id=1, source_target_pairs={{0,8},{4,12},{8,0},{12,4},{16,24},{20,28},{24,16},{28,20},{1,9},{5... | collective-permute-start | bytes 1544 | tf_op jit(solution)/shard_map/ppermute | solution.py:211
  18.7 1.8 %collective-permute-start.4 = (bf16[256,256]{1,0:T(8,128)(2,1)S(1)}, bf16[256,256]{1,0:T(8,128)(2,1)S(1)}, u32[]{:S(2)}, u32[]{:S(2)}) collective-permute-start(bf16[256,256]{1,0:T(8,128)(2,1)S(1)} %collective-permute-done.2.r_3_), channel_id=1, source_target_pairs={{0,4},{4,0},{8,12},{12,8},{16,20},{20,16},{24,28},{28,24},{1,5},{5... | collective-permute-start | bytes 393224 | tf_op jit(solution)/shard_map/ppermute | solution.py:211
  20.4 1.6 %collective-permute-start.11 = (f32[4,128]{1,0:T(4,128)S(1)}, f32[4,128]{1,0:T(4,128)S(1)}, u32[]{:S(2)}, u32[]{:S(2)}) collective-permute-start(f32[4,128]{1,0:T(4,128)S(1)} %shard_map.117.r_7_), channel_id=1, source_target_pairs={{0,4},{4,0},{8,12},{12,8},{16,20},{20,16},{24,28},{28,24},{1,5},{5... | collective-permute-start | bytes 6152 | tf_op jit(solution)/shard_map/ppermute | solution.py:211

commit v7 on v6

--- a/solution.py
+++ b/solution.py
@@ -127,17 +127,13 @@
         first += ref.shape[0]
 
 
-def stats_kernel(n_batch, *refs):
-    evens = refs[: n_batch // 2]
-    odd_ref, odd_last_ref, bias_ref = refs[n_batch // 2 : n_batch // 2 + 3]
-    queries, items, own_ref, pull_ref, top_ref, total_ref, diag_ref = refs[n_batch // 2 + 3 :]
-    block = evens[0].shape[0]
-    for k in range(n_batch // 2):
-        odd = odd_last_ref if k == n_batch // 2 - 1 else odd_ref.at[pl.ds(k * block, block)]
-        for parity, ref in enumerate((evens[k], odd)):
-            at = (2 * k + parity) * LANES
-            queries[at : at + LANES, :] = ref[:LANES, :]
-            items[at : at + LANES, :] = ref[LANES:, :]
+def stats_kernel(places, *refs):
+    count = 1 + max(operand for operand, _, _ in places)
+    bias_ref, queries, items, own_ref, pull_ref, top_ref, total_ref, diag_ref = refs[count:]
+    for operand, first, k in places:
+        at = slice(k * LANES, (k + 1) * LANES)
+        queries[at, :] = refs[operand][first : first + LANES, :]
+        items[at, :] = refs[operand][first + LANES : first + 2 * LANES, :]
     logit = nt_dot(items[...], queries[...]) + bias_ref[...]
     top = jnp.max(logit, axis=0, keepdims=True)
     exps = jnp.exp(logit - top)
@@ -237,9 +233,9 @@
         ],
     )
     far = swap(pack, "batch", 4)
-    near = swap(pack, "batch", 2)
     arrived = {k: swap(shard, "mem", k) for k in BANK_ORDER}
     shards = [shard] + [arrived[k] for k in BANK_ORDER]
+    near = swap(after(pack, arrived[2]), "batch", 2)
     bias, weight, wcol = call(
         lambda *r: prep_kernel(n_batch, *r),
         [f32(group_rows, group_rows), f32(n_batch, LANES), f32(LANES, LANES)],
@@ -258,15 +254,18 @@
         [f32(4, LANES)],
         [lse] + [sums[k] for k in SUM_ORDER],
     )
-    odd = swap(after(even, weight), "batch", 1)
-    (early,) = call(stack_kernel, [bf16(6 * own_count, depth)], (pack, near, far))
-    odd_early = swap(early, "batch", 1)
-    odd_last = swap(last, "batch", 1)
+    odd = swap(even, "batch", 1)
+    block = pack.shape[0]
+    pair = [bf16(2 * block, depth)]
+    odd_early = swap(call(stack_kernel, pair, (pack, far))[0], "batch", 1)
+    odd_late = swap(call(stack_kernel, pair, (near, last))[0], "batch", 1)
+    places = [(0, 0, 0), (1, 0, 2), (2, 0, 4), (3, 0, 6)]
+    places += [(4, 0, 1), (4, block, 5), (5, 0, 3), (5, block, 7)]
     stats = call(
-        lambda *r: stats_kernel(n_batch, *r),
+        lambda *r: stats_kernel(places, *r),
         [bf16(group_rows, depth), bf16(group_rows, depth), f32(own_count, group_rows)]
         + [f32(own_count, depth), f32(1, group_rows), f32(1, group_rows), f32(1, LANES)],
-        (pack, near, far, last, odd_early, odd_last, bias),
+        (pack, near, far, last, odd_early, odd_late, bias),
         cost_us=3,
     )
     loss, query_grad, positive_grad = call(

time: 23.2 us -> 23.1 us (level)
  waiting for transfers between devices: 3.02 us -> 2.43 us
  starting transfers between devices: 14.4 us -> 14.9 us
    ppermute x12, waiting for transfers between devices: 3.02 us -> 2.43 us  [swap(): return lax.ppermute(array, axis, [(s, s ^ mask) for s in range(size)])]
    ppermute x12, starting transfers between devices: 14.4 us -> 14.9 us  [swap(): return lax.ppermute(array, axis, [(s, s ^ mask) for s in range(size)])]
    pallas_call x7 -> x8, Pallas kernels: 4.93 us -> 4.93 us  [call(): pl.pallas_call(kernel, out_shape=outs, in_specs=[in_hbm if k in hbm else...]
where the time goes in v7:
time: 23.1 us; the launch traced here: 23 us
  starting transfers between devices  14.9 us (65%)
  Pallas kernels  4.93 us (21%)
  waiting for transfers between devices  2.43 us (11%)
  between operations  0.72 us (3%)
    ppermute x12, starting transfers between devices, swap(): return lax.ppermute(array, axis, [(s, s ^ mask) for s in range(size)])  14.9 us
    pallas_call x8, Pallas kernels, call(): pl.pallas_call(kernel, out_shape=outs, in_specs=[in_hbm if k in hbm else...  4.93 us
    ppermute x12, waiting for transfers between devices, swap(): return lax.ppermute(array, axis, [(s, s ^ mask) for s in range(size)])  2.43 us
  transfers between devices with their start and end apart: 12, of which 4 were waited for; matrix products, arithmetic and copies ran while one was open for 0% of the time, Pallas kernels for 13%

profile of v7, /device:TPU:0, one launch (start us, length us, event | category | flops | bytes accessed | tf_op | source)
XLA Modules:
  0.0 23.0 jit_solution(2971730197582934898)
XLA Ops:
  0.6 1.0 %shard_map.112 = (s32[32,128]{1,0:T(8,128)S(1)}, s32[32,128]{1,0:T(8,128)S(1)}, s32[4,128]{1,0:T(4,128)S(1)}, s32[8,128]{1,0:T(8,128)S(1)}, s32[8,128]{1,0:T(8,1...) custom-call(s32[32,128]{1,0:T(8,128)} %bitcast.7, s32[32,128]{1,0:T(8,128)} %bitcast.8, ...), custom_call_target="tpu_custom_call" | custom-call | flops 1000000000 | bytes 3000000 | tf_op jit(solution)/shard_map/pallas_call | solution.py:184
  1.6 4.1 %collective-permute-start.2 = (bf16[256,256]{1,0:T(8,128)(2,1)S(1)}, bf16[256,256]{1,0:T(8,128)(2,1)S(1)}, u32[]{:S(2)}, u32[]{:S(2)}) collective-permute-start(bf16[256,256]{1,0:T(8,128)(2,1)S(1)} %get-tuple-element.30.refs_0_.r_0_), channel_id=1, source_target_pairs={{0,16},{4,20},{8,24},{12,28},{16,0},{20,4},{24,8},{28,12},{1,17},{... | collective-permute-start | bytes 393224 | tf_op jit(solution)/shard_map/ppermute | solution.py:207
  5.7 1.5 %collective-permute-start = (bf16[32,256]{1,0:T(8,128)(2,1)S(1)}, bf16[32,256]{1,0:T(8,128)(2,1)S(1)}, u32[]{:S(2)}, u32[]{:S(2)}) collective-permute-start(bf16[32,256]{1,0:T(8,128)(2,1)S(1)} %get-tuple-element.29.r_1_), channel_id=1, source_target_pairs={{0,2},{1,3},{2,0},{3,1},{4,6},{5,7},{6,4},{7,5},{8,10},{9,11},{10,... | collective-permute-start | bytes 49160 | tf_op jit(solution)/shard_map/ppermute | solution.py:207
  7.2 1.4 %collective-permute-start.6 = (bf16[32,256]{1,0:T(8,128)(2,1)S(1)}, bf16[32,256]{1,0:T(8,128)(2,1)S(1)}, u32[]{:S(2)}, u32[]{:S(2)}) collective-permute-start(bf16[32,256]{1,0:T(8,128)(2,1)S(1)} %get-tuple-element.29.r_1_), channel_id=1, source_target_pairs={{0,3},{1,2},{2,1},{3,0},{4,7},{5,6},{6,5},{7,4},{8,11},{9,10},{10,... | collective-permute-start | bytes 49160 | tf_op jit(solution)/shard_map/ppermute | solution.py:207
  8.7 0.5 %collective-permute-start.7 = (bf16[32,256]{1,0:T(8,128)(2,1)S(1)}, bf16[32,256]{1,0:T(8,128)(2,1)S(1)}, u32[]{:S(2)}, u32[]{:S(2)}) collective-permute-start(bf16[32,256]{1,0:T(8,128)(2,1)S(1)} %get-tuple-element.29.r_1_), channel_id=1, source_target_pairs={{0,1},{1,0},{2,3},{3,2},{4,5},{5,4},{6,7},{7,6},{8,9},{9,8},{10,11... | collective-permute-start | bytes 49160 | tf_op jit(solution)/shard_map/ppermute | solution.py:207
  9.2 0.2 %collective-permute-done.r_4_ = bf16[32,256]{1,0:T(8,128)(2,1)S(1)} collective-permute-done((bf16[32,256]{1,0:T(8,128)(2,1)S(1)}, bf16[32,256]{1,0:T(8,128)(2,1)S(1)}, u32[]{:S(2)}, u32[]{:S(2)}) %collective-permute-start) | collective-permute-done | bytes 16416 | tf_op jit(solution)/shard_map/ppermute | solution.py:207
  9.5 1.6 %collective-permute-start.1 = (bf16[256,256]{1,0:T(8,128)(2,1)S(1)}, bf16[256,256]{1,0:T(8,128)(2,1)S(1)}, u32[]{:S(2)}, u32[]{:S(2)}) collective-permute-start(bf16[256,256]{1,0:T(8,128)(2,1)S(1)} %get-tuple-element.30.refs_0_.r_0_), channel_id=1, source_target_pairs={{0,8},{4,12},{8,0},{12,4},{16,24},{20,28},{24,16},{28,20},{1,9},{5... | collective-permute-start | bytes 393224 | tf_op jit(solution)/shard_map/ppermute | solution.py:207
  11.0 1.1 %collective-permute-done.2.refs_1_.r_2_ = bf16[256,256]{1,0:T(8,128)(2,1)S(1)} collective-permute-done((bf16[256,256]{1,0:T(8,128)(2,1)S(1)}, bf16[256,256]{1,0:T(8,128)(2,1)S(1)}, u32[]{:S(2)}, u32[]{:S(2)}) %collective-permute-start.2) | collective-permute-done | bytes 131104 | tf_op jit(solution)/shard_map/ppermute | solution.py:207
  12.1 0.7 %collective-permute-start.3 = (bf16[256,256]{1,0:T(8,128)(2,1)S(1)}, bf16[256,256]{1,0:T(8,128)(2,1)S(1)}, u32[]{:S(2)}, u32[]{:S(2)}) collective-permute-start(bf16[256,256]{1,0:T(8,128)(2,1)S(1)} %collective-permute-done.2.refs_1_.r_2_), channel_id=1, source_target_pairs={{0,8},{4,12},{8,0},{12,4},{16,24},{20,28},{24,16},{28,20},{1,9},{5... | collective-permute-start | bytes 393224 | tf_op jit(solution)/shard_map/ppermute | solution.py:207
  12.8 0.0 collective-permute-done.6.r_2_
  12.8 0.0 collective-permute-done.7.r_3_
  12.8 0.2 shard_map.117
  13.0 3.0 %collective-permute-start.8 = (f32[1,128]{1,0:T(1,128)S(1)}, f32[1,128]{1,0:T(1,128)S(1)}, u32[]{:S(2)}, u32[]{:S(2)}) collective-permute-start(f32[1,128]{1,0:T(1,128)S(1)} %get-tuple-element.45.r_0_), channel_id=1, source_target_pairs={{0,24},{4,28},{8,16},{12,20},{16,8},{20,12},{24,0},{28,4},{1,25},{... | collective-permute-start | bytes 1544 | tf_op jit(solution)/shard_map/ppermute | solution.py:207
  16.0 0.6 %collective-permute-start.9 = (f32[1,128]{1,0:T(1,128)S(1)}, f32[1,128]{1,0:T(1,128)S(1)}, u32[]{:S(2)}, u32[]{:S(2)}) collective-permute-start(f32[1,128]{1,0:T(1,128)S(1)} %get-tuple-element.45.r_0_), channel_id=1, source_target_pairs={{0,16},{4,20},{8,24},{12,28},{16,0},{20,4},{24,8},{28,12},{1,17},{... | collective-permute-start | bytes 1544 | tf_op jit(solution)/shard_map/ppermute | solution.py:207
  16.6 0.9 %collective-permute-start.10 = (f32[1,128]{1,0:T(1,128)S(1)}, f32[1,128]{1,0:T(1,128)S(1)}, u32[]{:S(2)}, u32[]{:S(2)}) collective-permute-start(f32[1,128]{1,0:T(1,128)S(1)} %get-tuple-element.45.r_0_), channel_id=1, source_target_pairs={{0,8},{4,12},{8,0},{12,4},{16,24},{20,28},{24,16},{28,20},{1,9},{5... | collective-permute-start | bytes 1544 | tf_op jit(solution)/shard_map/ppermute | solution.py:207
  17.5 0.0 collective-permute-done.1.refs_0_.r_1_
  17.5 0.1 collective-permute-start.4
  17.6 0.1 collective-permute-done.3.refs_1_.r_3_
  17.7 0.5 %collective-permute-start.5 = (bf16[512,256]{1,0:T(8,128)(2,1)S(1)}, bf16[512,256]{1,0:T(8,128)(2,1)S(1)}, u32[]{:S(2)}, u32[]{:S(2)}) collective-permute-start(bf16[512,256]{1,0:T(8,128)(2,1)S(1)} %shard_map.114), channel_id=1, source_target_pairs={{0,4},{4,0},{8,12},{12,8},{16,20},{20,16},{24,28},{28,24},{1,5},{5... | collective-permute-start | bytes 786440 | tf_op jit(solution)/shard_map/ppermute | solution.py:207
  18.2 1.2 %shard_map.115 = (f32[1024,1024]{1,0:T(8,128)S(1)}, f32[8,128]{1,0:T(8,128)S(1)}, f32[128,128]{1,0:T(8,128)S(1)}) custom-call(s32[32,128]{1,0:T(8,128)S(1)} %get-tuple-element.31.r_0_.r_5_, s32[32,128]{1,0:T(8,128)S(1)} %get-tuple-element.32.r_1_, s32[4,128]{1,0:T(4,128)S(1)} %get-tuple-element.33.r_2_), custom_call_target="tpu_custom_call" | custom-call | flops 3000000000 | bytes 9000000 | tf_op jit(solution)/shard_map/pallas_call | solution.py:184
  19.4 0.0 collective-permute-done.8.r_1_
  19.4 1.0 %collective-permute-done.9.r_2_ = f32[1,128]{1,0:T(1,128)S(1)} collective-permute-done((f32[1,128]{1,0:T(1,128)S(1)}, f32[1,128]{1,0:T(1,128)S(1)}, u32[]{:S(2)}, u32[]{:S(2)}) %collective-permute-start.9) | collective-permute-done | bytes 544 | tf_op jit(solution)/shard_map/ppermute | solution.py:207
  20.4 0.0 collective-permute-done.10.r_3_
  20.4 0.0 collective-permute-start.11
  20.4 0.0 collective-permute-done.4.r_4_
  20.4 0.0 collective-permute-done.5.r_5_
  20.4 1.5 %shard_map.116 = (bf16[1024,256]{1,0:T(8,128)(2,1)S(1)}, bf16[1024,256]{1,0:T(8,128)(2,1)S(1)}, f32[128,1024]{1,0:T(8,128)S(1)}, f32[128,256]{1,0:T(8,128)S(1)},...) custom-call(bf16[256,256]{1,0:T(8,128)(2,1)S(1)} %get-tuple-element.30.refs_0_.r_0_, ...), custom_call_target="tpu_custom_call" | custom-call | flops 3000000000 | bytes 9000000 | tf_op jit(solution)/shard_map/pallas_call | solution.py:184
  22.0 0.0 collective-permute-done.11.r_8_
  22.0 1.0 %shard_map.119 = (f32[1,128]{1,0:T(1,128)}, f32[128,256]{1,0:T(8,128)}, f32[128,256]{1,0:T(8,128)}) custom-call(bf16[1024,256]{1,0:T(8,128)(2,1)S(1)} %get-tuple-element.35.r_0_, bf16[1024,256]{1,0:T(8,128)(2,1)S(1)} %get-tuple-element.36.r_1_, f32[128,1024]{1,0:T(8,128)S(1)} %get-tuple-element.37.r_2_, f32[128,256]{1,0:T(8,128)S(1)} %get-tuple-element.38.r_3_, ...), custom_call_target="tpu_custom_call" | custom-call | flops 1000000000 | bytes 3000000 | tf_op jit(solution)/shard_map/pallas_call | solution.py:184
  (3 shorter events, 0.0 us)
Async XLA Ops:
  1.6 10.5 %collective-permute-start.2 = (bf16[256,256]{1,0:T(8,128)(2,1)S(1)}, bf16[256,256]{1,0:T(8,128)(2,1)S(1)}, u32[]{:S(2)}, u32[]{:S(2)}) collective-permute-start(bf16[256,256]{1,0:T(8,128)(2,1)S(1)} %get-tuple-element.30.refs_0_.r_0_), channel_id=1, source_target_pairs={{0,16},{4,20},{8,24},{12,28},{16,0},{20,4},{24,8},{28,12},{1,17},{... | collective-permute-start | bytes 393224 | tf_op jit(solution)/shard_map/ppermute | solution.py:207
  5.7 3.7 %collective-permute-start = (bf16[32,256]{1,0:T(8,128)(2,1)S(1)}, bf16[32,256]{1,0:T(8,128)(2,1)S(1)}, u32[]{:S(2)}, u32[]{:S(2)}) collective-permute-start(bf16[32,256]{1,0:T(8,128)(2,1)S(1)} %get-tuple-element.29.r_1_), channel_id=1, source_target_pairs={{0,2},{1,3},{2,0},{3,1},{4,6},{5,7},{6,4},{7,5},{8,10},{9,11},{10,... | collective-permute-start | bytes 49160 | tf_op jit(solution)/shard_map/ppermute | solution.py:207
  7.2 5.6 %collective-permute-start.6 = (bf16[32,256]{1,0:T(8,128)(2,1)S(1)}, bf16[32,256]{1,0:T(8,128)(2,1)S(1)}, u32[]{:S(2)}, u32[]{:S(2)}) collective-permute-start(bf16[32,256]{1,0:T(8,128)(2,1)S(1)} %get-tuple-element.29.r_1_), channel_id=1, source_target_pairs={{0,3},{1,2},{2,1},{3,0},{4,7},{5,6},{6,5},{7,4},{8,11},{9,10},{10,... | collective-permute-start | bytes 49160 | tf_op jit(solution)/shard_map/ppermute | solution.py:207
  8.7 4.1 %collective-permute-start.7 = (bf16[32,256]{1,0:T(8,128)(2,1)S(1)}, bf16[32,256]{1,0:T(8,128)(2,1)S(1)}, u32[]{:S(2)}, u32[]{:S(2)}) collective-permute-start(bf16[32,256]{1,0:T(8,128)(2,1)S(1)} %get-tuple-element.29.r_1_), channel_id=1, source_target_pairs={{0,1},{1,0},{2,3},{3,2},{4,5},{5,4},{6,7},{7,6},{8,9},{9,8},{10,11... | collective-permute-start | bytes 49160 | tf_op jit(solution)/shard_map/ppermute | solution.py:207
  9.5 8.0 %collective-permute-start.1 = (bf16[256,256]{1,0:T(8,128)(2,1)S(1)}, bf16[256,256]{1,0:T(8,128)(2,1)S(1)}, u32[]{:S(2)}, u32[]{:S(2)}) collective-permute-start(bf16[256,256]{1,0:T(8,128)(2,1)S(1)} %get-tuple-element.30.refs_0_.r_0_), channel_id=1, source_target_pairs={{0,8},{4,12},{8,0},{12,4},{16,24},{20,28},{24,16},{28,20},{1,9},{5... | collective-permute-start | bytes 393224 | tf_op jit(solution)/shard_map/ppermute | solution.py:207
  12.1 5.5 %collective-permute-start.3 = (bf16[256,256]{1,0:T(8,128)(2,1)S(1)}, bf16[256,256]{1,0:T(8,128)(2,1)S(1)}, u32[]{:S(2)}, u32[]{:S(2)}) collective-permute-start(bf16[256,256]{1,0:T(8,128)(2,1)S(1)} %collective-permute-done.2.refs_1_.r_2_), channel_id=1, source_target_pairs={{0,8},{4,12},{8,0},{12,4},{16,24},{20,28},{24,16},{28,20},{1,9},{5... | collective-permute-start | bytes 393224 | tf_op jit(solution)/shard_map/ppermute | solution.py:207
  13.0 6.4 %collective-permute-start.8 = (f32[1,128]{1,0:T(1,128)S(1)}, f32[1,128]{1,0:T(1,128)S(1)}, u32[]{:S(2)}, u32[]{:S(2)}) collective-permute-start(f32[1,128]{1,0:T(1,128)S(1)} %get-tuple-element.45.r_0_), channel_id=1, source_target_pairs={{0,24},{4,28},{8,16},{12,20},{16,8},{20,12},{24,0},{28,4},{1,25},{... | collective-permute-start | bytes 1544 | tf_op jit(solution)/shard_map/ppermute | solution.py:207
  16.0 4.4 %collective-permute-start.9 = (f32[1,128]{1,0:T(1,128)S(1)}, f32[1,128]{1,0:T(1,128)S(1)}, u32[]{:S(2)}, u32[]{:S(2)}) collective-permute-start(f32[1,128]{1,0:T(1,128)S(1)} %get-tuple-element.45.r_0_), channel_id=1, source_target_pairs={{0,16},{4,20},{8,24},{12,28},{16,0},{20,4},{24,8},{28,12},{1,17},{... | collective-permute-start | bytes 1544 | tf_op jit(solution)/shard_map/ppermute | solution.py:207
  16.6 3.8 %collective-permute-start.10 = (f32[1,128]{1,0:T(1,128)S(1)}, f32[1,128]{1,0:T(1,128)S(1)}, u32[]{:S(2)}, u32[]{:S(2)}) collective-permute-start(f32[1,128]{1,0:T(1,128)S(1)} %get-tuple-element.45.r_0_), channel_id=1, source_target_pairs={{0,8},{4,12},{8,0},{12,4},{16,24},{20,28},{24,16},{28,20},{1,9},{5... | collective-permute-start | bytes 1544 | tf_op jit(solution)/shard_map/ppermute | solution.py:207
  17.5 2.9 %collective-permute-start.4 = (bf16[512,256]{1,0:T(8,128)(2,1)S(1)}, bf16[512,256]{1,0:T(8,128)(2,1)S(1)}, u32[]{:S(2)}, u32[]{:S(2)}) collective-permute-start(bf16[512,256]{1,0:T(8,128)(2,1)S(1)} %shard_map.113), channel_id=1, source_target_pairs={{0,4},{4,0},{8,12},{12,8},{16,20},{20,16},{24,28},{28,24},{1,5},{5... | collective-permute-start | bytes 786440 | tf_op jit(solution)/shard_map/ppermute | solution.py:207
  17.7 2.8 %collective-permute-start.5 = (bf16[512,256]{1,0:T(8,128)(2,1)S(1)}, bf16[512,256]{1,0:T(8,128)(2,1)S(1)}, u32[]{:S(2)}, u32[]{:S(2)}) collective-permute-start(bf16[512,256]{1,0:T(8,128)(2,1)S(1)} %shard_map.114), channel_id=1, source_target_pairs={{0,4},{4,0},{8,12},{12,8},{16,20},{20,16},{24,28},{28,24},{1,5},{5... | collective-permute-start | bytes 786440 | tf_op jit(solution)/shard_map/ppermute | solution.py:207
  20.4 1.5 %collective-permute-start.11 = (f32[4,128]{1,0:T(4,128)S(1)}, f32[4,128]{1,0:T(4,128)S(1)}, u32[]{:S(2)}, u32[]{:S(2)}) collective-permute-start(f32[4,128]{1,0:T(4,128)S(1)} %shard_map.118.r_7_), channel_id=1, source_target_pairs={{0,4},{4,0},{8,12},{12,8},{16,20},{20,16},{24,28},{28,24},{1,5},{5... | collective-permute-start | bytes 6152 | tf_op jit(solution)/shard_map/ppermute | solution.py:207

commit v8 on v7

--- a/solution.py
+++ b/solution.py
@@ -31,14 +31,6 @@
     return jnp.broadcast_to(row, (LANES, LANES)).T
 
 
-def fetch(pairs, sems):
-    copies = [pltpu.make_async_copy(src, dst, sems.at[k]) for k, (src, dst) in enumerate(pairs)]
-    for copy in copies:
-        copy.start()
-    for copy in copies:
-        copy.wait()
-
-
 def pack_kernel(count, *refs):
     ins, outs = refs[: count + 2], refs[count + 2 : 2 * count + 3]
     q_ref, sems = refs[-2:]
@@ -46,8 +38,13 @@
     rows = q_ref.shape[0]
     pairs = [(ins[count], q_ref), (ins[count + 1], pack_ref.at[pl.ds(rows, rows)])]
     pairs += [*zip(ins[:count], outs[:count])]
-    fetch(pairs, sems)
+    copies = [pltpu.make_async_copy(src, dst, sems.at[k]) for k, (src, dst) in enumerate(pairs)]
+    for copy in copies:
+        copy.start()
+    copies[0].wait()
     pack_ref[:rows, :] = q_ref[...] * jnp.bfloat16(inv_temp)
+    for copy in copies[1:]:
+        copy.wait()
 
 
 def prep_kernel(

time: 23.1 us -> 23.1 us (level)
  no operation moved by 1% of the time
where the time goes in v8:
time: 23.1 us; the launch traced here: 22.9 us
  starting transfers between devices  14.9 us (65%)
  Pallas kernels  4.93 us (21%)
  waiting for transfers between devices  2.44 us (11%)
  between operations  0.72 us (3%)
    ppermute x12, starting transfers between devices, swap(): return lax.ppermute(array, axis, [(s, s ^ mask) for s in range(size)])  14.9 us
    pallas_call x8, Pallas kernels, call(): pl.pallas_call(kernel, out_shape=outs, in_specs=[in_hbm if k in hbm else...  4.93 us
    ppermute x12, waiting for transfers between devices, swap(): return lax.ppermute(array, axis, [(s, s ^ mask) for s in range(size)])  2.44 us
  transfers between devices with their start and end apart: 12, of which 4 were waited for; matrix products, arithmetic and copies ran while one was open for 0% of the time, Pallas kernels for 13%

profile of v8, /device:TPU:0, one launch (start us, length us, event | category | flops | bytes accessed | tf_op | source)
XLA Modules:
  0.0 22.9 jit_solution(11231288800378114387)
XLA Ops:
  0.6 1.0 %shard_map.112 = (s32[32,128]{1,0:T(8,128)S(1)}, s32[32,128]{1,0:T(8,128)S(1)}, s32[4,128]{1,0:T(4,128)S(1)}, s32[8,128]{1,0:T(8,128)S(1)}, s32[8,128]{1,0:T(8,1...) custom-call(s32[32,128]{1,0:T(8,128)} %bitcast.7, s32[32,128]{1,0:T(8,128)} %bitcast.8, ...), custom_call_target="tpu_custom_call" | custom-call | flops 1000000000 | bytes 3000000 | tf_op jit(solution)/shard_map/pallas_call | solution.py:181
  1.6 4.1 %collective-permute-start.2 = (bf16[256,256]{1,0:T(8,128)(2,1)S(1)}, bf16[256,256]{1,0:T(8,128)(2,1)S(1)}, u32[]{:S(2)}, u32[]{:S(2)}) collective-permute-start(bf16[256,256]{1,0:T(8,128)(2,1)S(1)} %get-tuple-element.30.refs_0_.r_0_), channel_id=1, source_target_pairs={{0,16},{4,20},{8,24},{12,28},{16,0},{20,4},{24,8},{28,12},{1,17},{... | collective-permute-start | bytes 393224 | tf_op jit(solution)/shard_map/ppermute | solution.py:204
  5.7 1.5 %collective-permute-start = (bf16[32,256]{1,0:T(8,128)(2,1)S(1)}, bf16[32,256]{1,0:T(8,128)(2,1)S(1)}, u32[]{:S(2)}, u32[]{:S(2)}) collective-permute-start(bf16[32,256]{1,0:T(8,128)(2,1)S(1)} %get-tuple-element.29.r_1_), channel_id=1, source_target_pairs={{0,2},{1,3},{2,0},{3,1},{4,6},{5,7},{6,4},{7,5},{8,10},{9,11},{10,... | collective-permute-start | bytes 49160 | tf_op jit(solution)/shard_map/ppermute | solution.py:204
  7.2 1.4 %collective-permute-start.6 = (bf16[32,256]{1,0:T(8,128)(2,1)S(1)}, bf16[32,256]{1,0:T(8,128)(2,1)S(1)}, u32[]{:S(2)}, u32[]{:S(2)}) collective-permute-start(bf16[32,256]{1,0:T(8,128)(2,1)S(1)} %get-tuple-element.29.r_1_), channel_id=1, source_target_pairs={{0,3},{1,2},{2,1},{3,0},{4,7},{5,6},{6,5},{7,4},{8,11},{9,10},{10,... | collective-permute-start | bytes 49160 | tf_op jit(solution)/shard_map/ppermute | solution.py:204
  8.7 0.5 %collective-permute-start.7 = (bf16[32,256]{1,0:T(8,128)(2,1)S(1)}, bf16[32,256]{1,0:T(8,128)(2,1)S(1)}, u32[]{:S(2)}, u32[]{:S(2)}) collective-permute-start(bf16[32,256]{1,0:T(8,128)(2,1)S(1)} %get-tuple-element.29.r_1_), channel_id=1, source_target_pairs={{0,1},{1,0},{2,3},{3,2},{4,5},{5,4},{6,7},{7,6},{8,9},{9,8},{10,11... | collective-permute-start | bytes 49160 | tf_op jit(solution)/shard_map/ppermute | solution.py:204
  9.2 0.2 %collective-permute-done.r_4_ = bf16[32,256]{1,0:T(8,128)(2,1)S(1)} collective-permute-done((bf16[32,256]{1,0:T(8,128)(2,1)S(1)}, bf16[32,256]{1,0:T(8,128)(2,1)S(1)}, u32[]{:S(2)}, u32[]{:S(2)}) %collective-permute-start) | collective-permute-done | bytes 16416 | tf_op jit(solution)/shard_map/ppermute | solution.py:204
  9.5 1.6 %collective-permute-start.1 = (bf16[256,256]{1,0:T(8,128)(2,1)S(1)}, bf16[256,256]{1,0:T(8,128)(2,1)S(1)}, u32[]{:S(2)}, u32[]{:S(2)}) collective-permute-start(bf16[256,256]{1,0:T(8,128)(2,1)S(1)} %get-tuple-element.30.refs_0_.r_0_), channel_id=1, source_target_pairs={{0,8},{4,12},{8,0},{12,4},{16,24},{20,28},{24,16},{28,20},{1,9},{5... | collective-permute-start | bytes 393224 | tf_op jit(solution)/shard_map/ppermute | solution.py:204
  11.0 1.1 %collective-permute-done.2.refs_1_.r_2_ = bf16[256,256]{1,0:T(8,128)(2,1)S(1)} collective-permute-done((bf16[256,256]{1,0:T(8,128)(2,1)S(1)}, bf16[256,256]{1,0:T(8,128)(2,1)S(1)}, u32[]{:S(2)}, u32[]{:S(2)}) %collective-permute-start.2) | collective-permute-done | bytes 131104 | tf_op jit(solution)/shard_map/ppermute | solution.py:204
  12.1 0.7 %collective-permute-start.3 = (bf16[256,256]{1,0:T(8,128)(2,1)S(1)}, bf16[256,256]{1,0:T(8,128)(2,1)S(1)}, u32[]{:S(2)}, u32[]{:S(2)}) collective-permute-start(bf16[256,256]{1,0:T(8,128)(2,1)S(1)} %collective-permute-done.2.refs_1_.r_2_), channel_id=1, source_target_pairs={{0,8},{4,12},{8,0},{12,4},{16,24},{20,28},{24,16},{28,20},{1,9},{5... | collective-permute-start | bytes 393224 | tf_op jit(solution)/shard_map/ppermute | solution.py:204
  12.8 0.0 collective-permute-done.6.r_2_
  12.8 0.0 collective-permute-done.7.r_3_
  12.8 0.2 shard_map.117
  13.0 3.0 %collective-permute-start.8 = (f32[1,128]{1,0:T(1,128)S(1)}, f32[1,128]{1,0:T(1,128)S(1)}, u32[]{:S(2)}, u32[]{:S(2)}) collective-permute-start(f32[1,128]{1,0:T(1,128)S(1)} %get-tuple-element.45.r_0_), channel_id=1, source_target_pairs={{0,24},{4,28},{8,16},{12,20},{16,8},{20,12},{24,0},{28,4},{1,25},{... | collective-permute-start | bytes 1544 | tf_op jit(solution)/shard_map/ppermute | solution.py:204
  16.0 0.6 %collective-permute-start.9 = (f32[1,128]{1,0:T(1,128)S(1)}, f32[1,128]{1,0:T(1,128)S(1)}, u32[]{:S(2)}, u32[]{:S(2)}) collective-permute-start(f32[1,128]{1,0:T(1,128)S(1)} %get-tuple-element.45.r_0_), channel_id=1, source_target_pairs={{0,16},{4,20},{8,24},{12,28},{16,0},{20,4},{24,8},{28,12},{1,17},{... | collective-permute-start | bytes 1544 | tf_op jit(solution)/shard_map/ppermute | solution.py:204
  16.6 0.9 %collective-permute-start.10 = (f32[1,128]{1,0:T(1,128)S(1)}, f32[1,128]{1,0:T(1,128)S(1)}, u32[]{:S(2)}, u32[]{:S(2)}) collective-permute-start(f32[1,128]{1,0:T(1,128)S(1)} %get-tuple-element.45.r_0_), channel_id=1, source_target_pairs={{0,8},{4,12},{8,0},{12,4},{16,24},{20,28},{24,16},{28,20},{1,9},{5... | collective-permute-start | bytes 1544 | tf_op jit(solution)/shard_map/ppermute | solution.py:204
  17.5 0.0 collective-permute-done.1.refs_0_.r_1_
  17.5 0.1 collective-permute-start.4
  17.6 0.1 collective-permute-done.3.refs_1_.r_3_
  17.7 0.5 %collective-permute-start.5 = (bf16[512,256]{1,0:T(8,128)(2,1)S(1)}, bf16[512,256]{1,0:T(8,128)(2,1)S(1)}, u32[]{:S(2)}, u32[]{:S(2)}) collective-permute-start(bf16[512,256]{1,0:T(8,128)(2,1)S(1)} %shard_map.114), channel_id=1, source_target_pairs={{0,4},{4,0},{8,12},{12,8},{16,20},{20,16},{24,28},{28,24},{1,5},{5... | collective-permute-start | bytes 786440 | tf_op jit(solution)/shard_map/ppermute | solution.py:204
  18.2 1.2 %shard_map.115 = (f32[1024,1024]{1,0:T(8,128)S(1)}, f32[8,128]{1,0:T(8,128)S(1)}, f32[128,128]{1,0:T(8,128)S(1)}) custom-call(s32[32,128]{1,0:T(8,128)S(1)} %get-tuple-element.31.r_0_.r_5_, s32[32,128]{1,0:T(8,128)S(1)} %get-tuple-element.32.r_1_, s32[4,128]{1,0:T(4,128)S(1)} %get-tuple-element.33.r_2_), custom_call_target="tpu_custom_call" | custom-call | flops 3000000000 | bytes 9000000 | tf_op jit(solution)/shard_map/pallas_call | solution.py:181
  19.4 0.0 collective-permute-done.8.r_1_
  19.4 1.0 %collective-permute-done.9.r_2_ = f32[1,128]{1,0:T(1,128)S(1)} collective-permute-done((f32[1,128]{1,0:T(1,128)S(1)}, f32[1,128]{1,0:T(1,128)S(1)}, u32[]{:S(2)}, u32[]{:S(2)}) %collective-permute-start.9) | collective-permute-done | bytes 544 | tf_op jit(solution)/shard_map/ppermute | solution.py:204
  20.4 0.0 collective-permute-done.10.r_3_
  20.4 0.0 collective-permute-start.11
  20.4 0.0 collective-permute-done.4.r_4_
  20.4 0.0 collective-permute-done.5.r_5_
  20.4 1.5 %shard_map.116 = (bf16[1024,256]{1,0:T(8,128)(2,1)S(1)}, bf16[1024,256]{1,0:T(8,128)(2,1)S(1)}, f32[128,1024]{1,0:T(8,128)S(1)}, f32[128,256]{1,0:T(8,128)S(1)},...) custom-call(bf16[256,256]{1,0:T(8,128)(2,1)S(1)} %get-tuple-element.30.refs_0_.r_0_, ...), custom_call_target="tpu_custom_call" | custom-call | flops 3000000000 | bytes 9000000 | tf_op jit(solution)/shard_map/pallas_call | solution.py:181
  22.0 0.0 collective-permute-done.11.r_8_
  22.0 1.0 %shard_map.119 = (f32[1,128]{1,0:T(1,128)}, f32[128,256]{1,0:T(8,128)}, f32[128,256]{1,0:T(8,128)}) custom-call(bf16[1024,256]{1,0:T(8,128)(2,1)S(1)} %get-tuple-element.35.r_0_, bf16[1024,256]{1,0:T(8,128)(2,1)S(1)} %get-tuple-element.36.r_1_, f32[128,1024]{1,0:T(8,128)S(1)} %get-tuple-element.37.r_2_, f32[128,256]{1,0:T(8,128)S(1)} %get-tuple-element.38.r_3_, ...), custom_call_target="tpu_custom_call" | custom-call | flops 1000000000 | bytes 3000000 | tf_op jit(solution)/shard_map/pallas_call | solution.py:181
  (3 shorter events, 0.0 us)
Async XLA Ops:
  1.6 10.5 %collective-permute-start.2 = (bf16[256,256]{1,0:T(8,128)(2,1)S(1)}, bf16[256,256]{1,0:T(8,128)(2,1)S(1)}, u32[]{:S(2)}, u32[]{:S(2)}) collective-permute-start(bf16[256,256]{1,0:T(8,128)(2,1)S(1)} %get-tuple-element.30.refs_0_.r_0_), channel_id=1, source_target_pairs={{0,16},{4,20},{8,24},{12,28},{16,0},{20,4},{24,8},{28,12},{1,17},{... | collective-permute-start | bytes 393224 | tf_op jit(solution)/shard_map/ppermute | solution.py:204
  5.7 3.7 %collective-permute-start = (bf16[32,256]{1,0:T(8,128)(2,1)S(1)}, bf16[32,256]{1,0:T(8,128)(2,1)S(1)}, u32[]{:S(2)}, u32[]{:S(2)}) collective-permute-start(bf16[32,256]{1,0:T(8,128)(2,1)S(1)} %get-tuple-element.29.r_1_), channel_id=1, source_target_pairs={{0,2},{1,3},{2,0},{3,1},{4,6},{5,7},{6,4},{7,5},{8,10},{9,11},{10,... | collective-permute-start | bytes 49160 | tf_op jit(solution)/shard_map/ppermute | solution.py:204
  7.2 5.6 %collective-permute-start.6 = (bf16[32,256]{1,0:T(8,128)(2,1)S(1)}, bf16[32,256]{1,0:T(8,128)(2,1)S(1)}, u32[]{:S(2)}, u32[]{:S(2)}) collective-permute-start(bf16[32,256]{1,0:T(8,128)(2,1)S(1)} %get-tuple-element.29.r_1_), channel_id=1, source_target_pairs={{0,3},{1,2},{2,1},{3,0},{4,7},{5,6},{6,5},{7,4},{8,11},{9,10},{10,... | collective-permute-start | bytes 49160 | tf_op jit(solution)/shard_map/ppermute | solution.py:204
  8.7 4.1 %collective-permute-start.7 = (bf16[32,256]{1,0:T(8,128)(2,1)S(1)}, bf16[32,256]{1,0:T(8,128)(2,1)S(1)}, u32[]{:S(2)}, u32[]{:S(2)}) collective-permute-start(bf16[32,256]{1,0:T(8,128)(2,1)S(1)} %get-tuple-element.29.r_1_), channel_id=1, source_target_pairs={{0,1},{1,0},{2,3},{3,2},{4,5},{5,4},{6,7},{7,6},{8,9},{9,8},{10,11... | collective-permute-start | bytes 49160 | tf_op jit(solution)/shard_map/ppermute | solution.py:204
  9.5 8.0 %collective-permute-start.1 = (bf16[256,256]{1,0:T(8,128)(2,1)S(1)}, bf16[256,256]{1,0:T(8,128)(2,1)S(1)}, u32[]{:S(2)}, u32[]{:S(2)}) collective-permute-start(bf16[256,256]{1,0:T(8,128)(2,1)S(1)} %get-tuple-element.30.refs_0_.r_0_), channel_id=1, source_target_pairs={{0,8},{4,12},{8,0},{12,4},{16,24},{20,28},{24,16},{28,20},{1,9},{5... | collective-permute-start | bytes 393224 | tf_op jit(solution)/shard_map/ppermute | solution.py:204
  12.1 5.5 %collective-permute-start.3 = (bf16[256,256]{1,0:T(8,128)(2,1)S(1)}, bf16[256,256]{1,0:T(8,128)(2,1)S(1)}, u32[]{:S(2)}, u32[]{:S(2)}) collective-permute-start(bf16[256,256]{1,0:T(8,128)(2,1)S(1)} %collective-permute-done.2.refs_1_.r_2_), channel_id=1, source_target_pairs={{0,8},{4,12},{8,0},{12,4},{16,24},{20,28},{24,16},{28,20},{1,9},{5... | collective-permute-start | bytes 393224 | tf_op jit(solution)/shard_map/ppermute | solution.py:204
  13.0 6.4 %collective-permute-start.8 = (f32[1,128]{1,0:T(1,128)S(1)}, f32[1,128]{1,0:T(1,128)S(1)}, u32[]{:S(2)}, u32[]{:S(2)}) collective-permute-start(f32[1,128]{1,0:T(1,128)S(1)} %get-tuple-element.45.r_0_), channel_id=1, source_target_pairs={{0,24},{4,28},{8,16},{12,20},{16,8},{20,12},{24,0},{28,4},{1,25},{... | collective-permute-start | bytes 1544 | tf_op jit(solution)/shard_map/ppermute | solution.py:204
  16.0 4.4 %collective-permute-start.9 = (f32[1,128]{1,0:T(1,128)S(1)}, f32[1,128]{1,0:T(1,128)S(1)}, u32[]{:S(2)}, u32[]{:S(2)}) collective-permute-start(f32[1,128]{1,0:T(1,128)S(1)} %get-tuple-element.45.r_0_), channel_id=1, source_target_pairs={{0,16},{4,20},{8,24},{12,28},{16,0},{20,4},{24,8},{28,12},{1,17},{... | collective-permute-start | bytes 1544 | tf_op jit(solution)/shard_map/ppermute | solution.py:204
  16.6 3.8 %collective-permute-start.10 = (f32[1,128]{1,0:T(1,128)S(1)}, f32[1,128]{1,0:T(1,128)S(1)}, u32[]{:S(2)}, u32[]{:S(2)}) collective-permute-start(f32[1,128]{1,0:T(1,128)S(1)} %get-tuple-element.45.r_0_), channel_id=1, source_target_pairs={{0,8},{4,12},{8,0},{12,4},{16,24},{20,28},{24,16},{28,20},{1,9},{5... | collective-permute-start | bytes 1544 | tf_op jit(solution)/shard_map/ppermute | solution.py:204
  17.5 2.9 %collective-permute-start.4 = (bf16[512,256]{1,0:T(8,128)(2,1)S(1)}, bf16[512,256]{1,0:T(8,128)(2,1)S(1)}, u32[]{:S(2)}, u32[]{:S(2)}) collective-permute-start(bf16[512,256]{1,0:T(8,128)(2,1)S(1)} %shard_map.113), channel_id=1, source_target_pairs={{0,4},{4,0},{8,12},{12,8},{16,20},{20,16},{24,28},{28,24},{1,5},{5... | collective-permute-start | bytes 786440 | tf_op jit(solution)/shard_map/ppermute | solution.py:204
  17.7 2.8 %collective-permute-start.5 = (bf16[512,256]{1,0:T(8,128)(2,1)S(1)}, bf16[512,256]{1,0:T(8,128)(2,1)S(1)}, u32[]{:S(2)}, u32[]{:S(2)}) collective-permute-start(bf16[512,256]{1,0:T(8,128)(2,1)S(1)} %shard_map.114), channel_id=1, source_target_pairs={{0,4},{4,0},{8,12},{12,8},{16,20},{20,16},{24,28},{28,24},{1,5},{5... | collective-permute-start | bytes 786440 | tf_op jit(solution)/shard_map/ppermute | solution.py:204
  20.4 1.5 %collective-permute-start.11 = (f32[4,128]{1,0:T(4,128)S(1)}, f32[4,128]{1,0:T(4,128)S(1)}, u32[]{:S(2)}, u32[]{:S(2)}) collective-permute-start(f32[4,128]{1,0:T(4,128)S(1)} %shard_map.118.r_7_), channel_id=1, source_target_pairs={{0,4},{4,0},{8,12},{12,8},{16,20},{20,16},{24,28},{28,24},{1,5},{5... | collective-permute-start | bytes 6152 | tf_op jit(solution)/shard_map/ppermute | solution.py:204
